TPU v7x, 128 devices: a whole 4x4x4 slice. The times are simulated.
128 devices in a mesh: resp: 8 (over x, core), head: 16 (over y, z).
Axes of the slice: x: 4, y: 4, z: 4, core: 2. Of those that a mesh axis runs over, the one named last changes fastest.
Arguments:
- queries: bfloat16 [8192, 24576], P('resp', 'head'), may hold values from -72 to 72
- up_key: bfloat16 [128, 128, 512], P('head'), may hold values from -0.5 to 0.5
- up_value: bfloat16 [128, 512, 128], P('head'), may hold values from -0.25 to 0.25
- prompt_latent: bfloat16 [16, 256, 576], P('resp', 'head'), may hold values from -8 to 8
- resp_latent: bfloat16 [8192, 576], P('resp'), may hold values from -6 to 6
- grad_out: bfloat16 [8192, 16384], P('resp', 'head'), may hold values from -6 to 6
- response_prompt: int32 [64], replicated, may hold values from 0 to 15, as said below
- prompt_length: int32 [16], replicated, may hold values from 1 to 256, 3072 in all
Outputs:
- attn_out: bfloat16 [8192, 16384], P('resp', 'head')
- prompt_grad: float32 [16, 256, 576], P('resp', 'head')
Inputs may be any that keep to these rules, and one draw needn't show every extreme that they name: `response_prompt`: response n is held by index n // 8 of resp and prompt p is owned by index p // 2 of resp; the responses held by one index of resp never answer two different prompts of one owner.
All inputs are finite; a program needn't handle non-finite values.
Results may differ from a plain program's by a relative error of at most 0.013.
Values may be sent and summed in bfloat16 or wider, within the bound.
No kernel may reach another device: no remote copies, remote signals or barrier semaphores. Data moves between devices by JAX's collectives and lax.ppermute only.
A program may use at most 128 MiB of HBM per device.

v0:
```python
import math

import jax
import jax.numpy as jnp
from jax import lax
from jax.sharding import PartitionSpec as P


def attend(queries, up_key, up_value, latent, length, own_rows, grad_out):
    nope_width = up_key.shape[1]
    latent_width = up_value.shape[1]
    row_count = queries.shape[0]
    key_span = latent.shape[0]
    scaling = 1.0 / math.sqrt(queries.shape[2])
    absorbed = jnp.einsum(
        "lhn,hnc->lhc", queries[:, :, :nope_width], up_key, preferred_element_type=jnp.float32
    ).astype(jnp.bfloat16)
    full_query = jnp.concatenate([absorbed, queries[:, :, nope_width:]], axis=2)
    key_rows = jnp.concatenate([latent, own_rows], axis=0)
    scores = (
        jnp.einsum("lhc,kc->hlk", full_query, key_rows, preferred_element_type=jnp.float32)
        * scaling
    )
    key_index = jnp.arange(key_span + row_count)
    row_index = jnp.arange(row_count)
    allowed = jnp.where(
        key_index[None, :] < key_span,
        key_index[None, :] < length,
        key_index[None, :] - key_span <= row_index[:, None],
    )
    scores = jnp.where(allowed[None, :, :], scores, -jnp.inf)
    top_score = jnp.max(scores, axis=2, keepdims=True)
    weights = jnp.exp(scores - top_score)
    attention = weights / jnp.sum(weights, axis=2, keepdims=True)
    attention_low = attention.astype(jnp.bfloat16)
    values = key_rows[:, :latent_width]
    out_latent = jnp.einsum(
        "hlk,kc->lhc", attention_low, values, preferred_element_type=jnp.float32
    ).astype(jnp.bfloat16)
    result = jnp.einsum(
        "lhc,hcv->lhv", out_latent, up_value, preferred_element_type=jnp.float32
    ).astype(jnp.bfloat16)
    grad_latent = jnp.einsum(
        "lhv,hcv->lhc", grad_out, up_value, preferred_element_type=jnp.float32
    ).astype(jnp.bfloat16)
    grad_attention = jnp.einsum(
        "lhc,kc->hlk", grad_latent, values, preferred_element_type=jnp.float32
    )
    inner_sum = jnp.sum(attention * grad_attention, axis=2, keepdims=True)
    grad_scores = (attention * (grad_attention - inner_sum) * scaling).astype(jnp.bfloat16)
    key_term = jnp.einsum(
        "hlk,lhc->kc", grad_scores[:, :, :key_span], full_query, preferred_element_type=jnp.float32
    )
    value_term = jnp.einsum(
        "hlk,lhc->kc",
        attention_low[:, :, :key_span],
        grad_latent,
        preferred_element_type=jnp.float32,
    )
    combined = key_term + jnp.pad(value_term, ((0, 0), (0, key_term.shape[1] - latent_width)))
    return (result, combined)


def on_device(
    queries, up_key, up_value, prompt_latent, resp_latent, grad_out, response_prompt, prompt_length
):
    groups = lax.axis_size("resp")
    slab_count = lax.axis_size("head")
    my_group = lax.axis_index("resp")
    owned = prompt_latent.shape[0]
    slab_rows = prompt_latent.shape[1]
    channels = prompt_latent.shape[2]
    key_span = slab_rows * slab_count
    resp_count = response_prompt.shape[0] // groups
    local_heads = up_key.shape[0]
    row_count = resp_latent.shape[0] // resp_count
    owners = response_prompt // owned
    hit_table = owners[:, None] == jnp.arange(groups)[None, :]
    wanted = jnp.max(
        jnp.where(hit_table, (response_prompt % owned)[:, None], -1).reshape(
            groups, resp_count, groups
        ),
        axis=1,
    )
    wanted_mine = lax.dynamic_index_in_dim(wanted, my_group, 1, False)
    returned = wanted_mine[:, None] == jnp.arange(owned)[None, :]
    selector = returned.astype(jnp.bfloat16)
    outgoing = jnp.einsum(
        "rp,psc->rsc", selector, prompt_latent, preferred_element_type=jnp.float32
    ).astype(jnp.bfloat16)
    copies = jnp.repeat(outgoing, slab_count, axis=0)
    arrived = lax.all_to_all(copies, ("resp", "head"), split_axis=0, concat_axis=0, tiled=True)
    gathered = arrived.reshape(groups, key_span, channels)
    local_prompt = lax.dynamic_slice_in_dim(response_prompt, my_group * resp_count, resp_count)
    head_width = queries.shape[1] // local_heads
    shaped_query = queries.reshape(resp_count, row_count, local_heads, head_width)
    shaped_grad = grad_out.reshape(resp_count, row_count, local_heads, -1)
    shaped_own = resp_latent.reshape(resp_count, row_count, channels)
    prompt_slots = jnp.arange(prompt_length.shape[0])

    def one_response(buffer, inputs):
        response_query, own_rows, response_grad, prompt_id = inputs
        owner_slot = prompt_id // owned
        latent = lax.dynamic_index_in_dim(gathered, owner_slot, 0, False)
        length = jnp.sum(jnp.where(prompt_slots == prompt_id, prompt_length, 0))
        result, combined = attend(
            response_query, up_key, up_value, latent, length, own_rows, response_grad
        )
        current = lax.dynamic_index_in_dim(buffer, owner_slot, 0, False)
        buffer = lax.dynamic_update_index_in_dim(buffer, current + combined, owner_slot, 0)
        return (buffer, result)

    zero_buffer = jnp.zeros((groups, key_span, channels), jnp.float32)
    buffer, results = lax.scan(
        one_response, zero_buffer, (shaped_query, shaped_own, shaped_grad, local_prompt)
    )
    attn_out = results.reshape(resp_count * row_count, -1)
    grad_pieces = buffer.astype(jnp.bfloat16).reshape(groups * slab_count, slab_rows, channels)
    returned_grad = lax.all_to_all(
        grad_pieces, ("resp", "head"), split_axis=0, concat_axis=0, tiled=True
    )
    prompt_grad = jnp.einsum(
        "rp,rhsc->psc",
        selector,
        returned_grad.reshape(groups, slab_count, slab_rows, channels),
        preferred_element_type=jnp.float32,
    )
    return (attn_out, prompt_grad)


def solution(mesh):
    return jax.shard_map(
        on_device,
        mesh=mesh,
        in_specs=(
            P("resp", "head"),
            P("head", None, None),
            P("head", None, None),
            P("resp", "head", None),
            P("resp", None),
            P("resp", "head"),
            P(),
            P(),
        ),
        out_specs=(P("resp", "head"), P("resp", "head", None)),
        check_vma=False,
    )
```

profile of v0, /device:TPU:1, one launch (start us, length us, event | category | flops | bytes accessed | tf_op | source)
XLA Modules:
  0.0 352.1 jit_solution(5421292799933953926)
XLA Ops:
  2.9 1.8 broadcast_in_dim.97
  4.7 11.9 %all-to-all-start = ((bf16[128,16,576]{2,1,0:T(8,128)(2,1)}), bf16[128,16,576]{2,1,0:T(8,128)(2,1)}, u32[]{:S(2)}, u32[]{:S(2)}) async-start(bf16[128,16,576]{2,1,0:T(8,128)(2,1)} %bitcast.140), calls=%async_computation | async-start | bytes 5242880 | tf_op jit(solution)/shard_map/all_to_all | solution.py:92
  16.7 2.0 copy.104
  18.7 7.5 %reshape.128 = bf16[8,128,8,192]{3,2,1,0:T(8,128)(2,1)} reshape(bf16[1024,1536]{1,0:T(8,128)(2,1)} %param.10) | data formatting | bytes 6291456 | tf_op jit(solution)/shard_map/reshape | solution.py:96
  27.5 23.9 %all-to-all-done = bf16[128,16,576]{2,1,0:T(8,128)(2,1)} async-done(((bf16[128,16,576]{2,1,0:T(8,128)(2,1)}), bf16[128,16,576]{2,1,0:T(8,128)(2,1)}, u32[]{:S(2)}, u32[]{:S(2)}) %all-to-all-start) | async-done | bytes 2359328 | tf_op jit(solution)/shard_map/all_to_all | solution.py:92
  51.4 4.4 %copy.80 = bf16[8,256,576]{1,2,0:T(8,128)(2,1)} copy(bf16[8,256,576]{2,1,0:T(8,128)(2,1)} %bitcast.2) | data formatting | bytes 4718592
  55.8 2.5 broadcast_in_dim.92
  58.3 244.8 %while.15 = (s32[]{:T(128)}, f32[8,256,576]{1,2,0:T(8,128)}, bf16[8,128,8,128]{3,2,1,0:T(8,128)(2,1)}, s32[8]{0:T(128)S(1)}, s32[16]{0:T(128)S(1)}, /*index=5*/b...) while((s32[]{:T(128)}, f32[8,256,576]{1,2,0:T(8,128)}, ...), condition=%wide.region_6.7_spmd.clone, body=%wide.region_1.6_spmd.clone.sunk | while | flops 2244837888 | bytes 53974176 | solution.py:114
  61.5 1.4 fusion.93
  69.1 1.5 constant_dynamic-slice_fusion.7
  70.6 1.4 fusion.92
  72.0 3.0 fusion.95
  75.1 3.6 %multiply_reduce_fusion.2 = (f32[8,128]{1,0:T(8,128)S(1)}, f32[8,128,384]{1,2,0:T(8,128)S(1)}, f32[8,128,384]{1,2,0:T(8,128)}) fusion(f32[8,128,384]{1,2,0:T(8,128)} %get-tuple-element.342, f32[8,128]{1,0:T(8,128)S(1)} %get-tuple-element.343, bf16[128,8,512]{2,0,1:T(8,128)(2,1)} %fusion.92, bf16[256,576]{0,1:T(8,128)(2,1)} %copy-done.7, ...), kind=kOutput, calls=%fused_computation.4.clone.1 | convolution fusion | flops 404618240 | bytes 6217728 | tf_op jit(solution)/shard_map/while/body/eval_jaxpr/lhc,kc->hlk/dot_general | solution.py:46
  81.5 3.3 fusion.97
  84.8 3.2 fusion.96
  99.7 1.5 constant_dynamic-slice_fusion.7
  101.2 1.4 fusion.92
  102.6 3.0 fusion.95
  105.7 3.6 %multiply_reduce_fusion.2 = (f32[8,128]{1,0:T(8,128)S(1)}, f32[8,128,384]{1,2,0:T(8,128)S(1)}, f32[8,128,384]{1,2,0:T(8,128)}) fusion(f32[8,128,384]{1,2,0:T(8,128)} %get-tuple-element.342, f32[8,128]{1,0:T(8,128)S(1)} %get-tuple-element.343, bf16[128,8,512]{2,0,1:T(8,128)(2,1)} %fusion.92, bf16[256,576]{0,1:T(8,128)(2,1)} %copy-done.7, ...), kind=kOutput, calls=%fused_computation.4.clone.1 | convolution fusion | flops 404618240 | bytes 6217728 | tf_op jit(solution)/shard_map/while/body/eval_jaxpr/lhc,kc->hlk/dot_general | solution.py:46
  112.1 3.3 fusion.97
  115.4 3.2 fusion.96
  130.3 1.5 constant_dynamic-slice_fusion.7
  131.8 1.4 fusion.92
  133.2 3.0 fusion.95
  136.3 3.6 %multiply_reduce_fusion.2 = (f32[8,128]{1,0:T(8,128)S(1)}, f32[8,128,384]{1,2,0:T(8,128)S(1)}, f32[8,128,384]{1,2,0:T(8,128)}) fusion(f32[8,128,384]{1,2,0:T(8,128)} %get-tuple-element.342, f32[8,128]{1,0:T(8,128)S(1)} %get-tuple-element.343, bf16[128,8,512]{2,0,1:T(8,128)(2,1)} %fusion.92, bf16[256,576]{0,1:T(8,128)(2,1)} %copy-done.7, ...), kind=kOutput, calls=%fused_computation.4.clone.1 | convolution fusion | flops 404618240 | bytes 6217728 | tf_op jit(solution)/shard_map/while/body/eval_jaxpr/lhc,kc->hlk/dot_general | solution.py:46
  142.7 3.3 fusion.97
  146.0 3.3 fusion.96
  153.4 1.4 fusion.93
  160.9 1.5 constant_dynamic-slice_fusion.7
  162.4 1.4 fusion.92
  163.9 3.0 fusion.95
  166.9 3.6 %multiply_reduce_fusion.2 = (f32[8,128]{1,0:T(8,128)S(1)}, f32[8,128,384]{1,2,0:T(8,128)S(1)}, f32[8,128,384]{1,2,0:T(8,128)}) fusion(f32[8,128,384]{1,2,0:T(8,128)} %get-tuple-element.342, f32[8,128]{1,0:T(8,128)S(1)} %get-tuple-element.343, bf16[128,8,512]{2,0,1:T(8,128)(2,1)} %fusion.92, bf16[256,576]{0,1:T(8,128)(2,1)} %copy-done.7, ...), kind=kOutput, calls=%fused_computation.4.clone.1 | convolution fusion | flops 404618240 | bytes 6217728 | tf_op jit(solution)/shard_map/while/body/eval_jaxpr/lhc,kc->hlk/dot_general | solution.py:46
  173.4 3.3 fusion.97
  176.6 3.2 fusion.96
  191.5 1.5 constant_dynamic-slice_fusion.7
  193.0 1.4 fusion.92
  194.5 3.0 fusion.95
  197.5 3.6 %multiply_reduce_fusion.2 = (f32[8,128]{1,0:T(8,128)S(1)}, f32[8,128,384]{1,2,0:T(8,128)S(1)}, f32[8,128,384]{1,2,0:T(8,128)}) fusion(f32[8,128,384]{1,2,0:T(8,128)} %get-tuple-element.342, f32[8,128]{1,0:T(8,128)S(1)} %get-tuple-element.343, bf16[128,8,512]{2,0,1:T(8,128)(2,1)} %fusion.92, bf16[256,576]{0,1:T(8,128)(2,1)} %copy-done.7, ...), kind=kOutput, calls=%fused_computation.4.clone.1 | convolution fusion | flops 404618240 | bytes 6217728 | tf_op jit(solution)/shard_map/while/body/eval_jaxpr/lhc,kc->hlk/dot_general | solution.py:46
  204.0 3.3 fusion.97
  207.2 3.3 fusion.96
  222.2 1.5 constant_dynamic-slice_fusion.7
  223.7 1.4 fusion.92
  225.1 3.0 fusion.95
  228.1 3.6 %multiply_reduce_fusion.2 = (f32[8,128]{1,0:T(8,128)S(1)}, f32[8,128,384]{1,2,0:T(8,128)S(1)}, f32[8,128,384]{1,2,0:T(8,128)}) fusion(f32[8,128,384]{1,2,0:T(8,128)} %get-tuple-element.342, f32[8,128]{1,0:T(8,128)S(1)} %get-tuple-element.343, bf16[128,8,512]{2,0,1:T(8,128)(2,1)} %fusion.92, bf16[256,576]{0,1:T(8,128)(2,1)} %copy-done.7, ...), kind=kOutput, calls=%fused_computation.4.clone.1 | convolution fusion | flops 404618240 | bytes 6217728 | tf_op jit(solution)/shard_map/while/body/eval_jaxpr/lhc,kc->hlk/dot_general | solution.py:46
  234.6 3.3 fusion.97
  237.8 3.2 fusion.96
  252.8 1.5 constant_dynamic-slice_fusion.7
  254.3 1.4 fusion.92
  255.7 3.0 fusion.95
  258.7 3.6 %multiply_reduce_fusion.2 = (f32[8,128]{1,0:T(8,128)S(1)}, f32[8,128,384]{1,2,0:T(8,128)S(1)}, f32[8,128,384]{1,2,0:T(8,128)}) fusion(f32[8,128,384]{1,2,0:T(8,128)} %get-tuple-element.342, f32[8,128]{1,0:T(8,128)S(1)} %get-tuple-element.343, bf16[128,8,512]{2,0,1:T(8,128)(2,1)} %fusion.92, bf16[256,576]{0,1:T(8,128)(2,1)} %copy-done.7, ...), kind=kOutput, calls=%fused_computation.4.clone.1 | convolution fusion | flops 404618240 | bytes 6217728 | tf_op jit(solution)/shard_map/while/body/eval_jaxpr/lhc,kc->hlk/dot_general | solution.py:46
  265.2 3.3 fusion.97
  268.4 3.2 fusion.96
  283.3 1.5 constant_dynamic-slice_fusion.7
  284.8 1.4 fusion.92
  286.3 3.0 fusion.95
  289.3 3.6 %multiply_reduce_fusion.2 = (f32[8,128]{1,0:T(8,128)S(1)}, f32[8,128,384]{1,2,0:T(8,128)S(1)}, f32[8,128,384]{1,2,0:T(8,128)}) fusion(f32[8,128,384]{1,2,0:T(8,128)} %get-tuple-element.342, f32[8,128]{1,0:T(8,128)S(1)} %get-tuple-element.343, bf16[128,8,512]{2,0,1:T(8,128)(2,1)} %fusion.92, bf16[256,576]{0,1:T(8,128)(2,1)} %copy-done.7, ...), kind=kOutput, calls=%fused_computation.4.clone.1 | convolution fusion | flops 404618240 | bytes 6217728 | tf_op jit(solution)/shard_map/while/body/eval_jaxpr/lhc,kc->hlk/dot_general | solution.py:46
  295.8 3.3 fusion.97
  299.0 3.2 fusion.96
  303.1 2.6 convert_element_type.64
  305.8 2.6 copy.85
  308.3 5.8 %all-to-all-start.1 = ((bf16[128,16,576]{2,1,0:T(8,128)(2,1)}), bf16[128,16,576]{2,1,0:T(8,128)(2,1)}, u32[]{:S(2)}, u32[]{:S(2)}) async-start(bf16[128,16,576]{2,1,0:T(8,128)(2,1)} %bitcast.141), calls=%async_computation.1 | async-start | bytes 5242880 | tf_op jit(solution)/shard_map/all_to_all | solution.py:119
  314.2 1.9 copy.117
  316.1 33.0 %all-to-all-done.1 = bf16[128,16,576]{2,1,0:T(8,128)(2,1)} async-done(((bf16[128,16,576]{2,1,0:T(8,128)(2,1)}), bf16[128,16,576]{2,1,0:T(8,128)(2,1)}, u32[]{:S(2)}, u32[]{:S(2)}) %all-to-all-start.1) | async-done | bytes 2359328 | tf_op jit(solution)/shard_map/all_to_all | solution.py:119
  349.1 2.1 convert_reduce_fusion
  (268 shorter events, 96.3 us)
Async XLA Ops:
  0.6 25.6 %copy-start = (bf16[1024,576]{0,1:T(8,128)(2,1)S(1)}, bf16[1024,576]{0,1:T(8,128)(2,1)}, u32[]{:S(2)}) copy-start(bf16[1024,576]{0,1:T(8,128)(2,1)} %param.14) | copy-start | bytes 3538948
  4.7 11.9 %copy-start.11 = (s32[64]{0:T(128)S(1)}, s32[64]{0:T(128)}, u32[]{:S(2)}) copy-start(s32[64]{0:T(128)} %param.16) | copy-start | bytes 772
  4.7 12.0 %copy-start.9 = (bf16[1024,1024]{1,0:T(8,128)(2,1)S(1)}, bf16[1024,1024]{1,0:T(8,128)(2,1)}, u32[]{:S(2)}) copy-start(bf16[1024,1024]{1,0:T(8,128)(2,1)} %param.15) | copy-start | bytes 6291460
  4.7 46.7 %all-to-all-start = ((bf16[128,16,576]{2,1,0:T(8,128)(2,1)}), bf16[128,16,576]{2,1,0:T(8,128)(2,1)}, u32[]{:S(2)}, u32[]{:S(2)}) async-start(bf16[128,16,576]{2,1,0:T(8,128)(2,1)} %bitcast.140), calls=%async_computation | async-start | bytes 5242880 | tf_op jit(solution)/shard_map/all_to_all | solution.py:92
  55.8 2.5 copy-start.12
  61.5 7.1 %copy-start.5 = (bf16[8,128,512]{2,1,0:T(8,128)(2,1)S(1)}, bf16[8,128,512]{2,1,0:T(8,128)(2,1)}, u32[]{:S(2)}) copy-start(bf16[8,128,512]{2,1,0:T(8,128)(2,1)} %get-tuple-element.385) | copy-start | bytes 3145732 | tf_op jit(solution)/shard_map/while
  67.3 4.8 %copy-start.7 = (bf16[256,576]{0,1:T(8,128)(2,1)}, bf16[256,576]{0,1:T(8,128)(2,1)S(1)}, u32[]{:S(2)}) copy-start(bf16[256,576]{0,1:T(8,128)(2,1)S(1)} %dynamic-slice_bitcast_fusion.5) | copy-start | bytes 884740 | tf_op jit(solution)/shard_map/while
  68.6 2.0 copy-start.6
  68.7 3.4 copy-start.4
  69.1 6.0 %copy-start.2 = (bf16[128,8,512]{2,0,1:T(8,128)(2,1)}, bf16[128,8,512]{2,0,1:T(8,128)(2,1)S(1)}, u32[]{:S(2)}) copy-start(bf16[128,8,512]{2,0,1:T(8,128)(2,1)S(1)} %fusion.91) | copy-start | bytes 3145732 | tf_op jit(solution)/shard_map/while
  78.7 1.5 copy-start.1
  78.8 0.9 copy-start.3
  84.8 3.2 copy-start.8
  92.1 7.1 %copy-start.5 = (bf16[8,128,512]{2,1,0:T(8,128)(2,1)S(1)}, bf16[8,128,512]{2,1,0:T(8,128)(2,1)}, u32[]{:S(2)}) copy-start(bf16[8,128,512]{2,1,0:T(8,128)(2,1)} %get-tuple-element.385) | copy-start | bytes 3145732 | tf_op jit(solution)/shard_map/while
  97.9 4.7 %copy-start.7 = (bf16[256,576]{0,1:T(8,128)(2,1)}, bf16[256,576]{0,1:T(8,128)(2,1)S(1)}, u32[]{:S(2)}) copy-start(bf16[256,576]{0,1:T(8,128)(2,1)S(1)} %dynamic-slice_bitcast_fusion.5) | copy-start | bytes 884740 | tf_op jit(solution)/shard_map/while
  99.2 2.0 copy-start.6
  99.3 3.4 copy-start.4
  99.7 6.0 %copy-start.2 = (bf16[128,8,512]{2,0,1:T(8,128)(2,1)}, bf16[128,8,512]{2,0,1:T(8,128)(2,1)S(1)}, u32[]{:S(2)}) copy-start(bf16[128,8,512]{2,0,1:T(8,128)(2,1)S(1)} %fusion.91) | copy-start | bytes 3145732 | tf_op jit(solution)/shard_map/while
  109.3 1.5 copy-start.1
  115.4 3.2 copy-start.8
  122.7 7.1 %copy-start.5 = (bf16[8,128,512]{2,1,0:T(8,128)(2,1)S(1)}, bf16[8,128,512]{2,1,0:T(8,128)(2,1)}, u32[]{:S(2)}) copy-start(bf16[8,128,512]{2,1,0:T(8,128)(2,1)} %get-tuple-element.385) | copy-start | bytes 3145732 | tf_op jit(solution)/shard_map/while
  128.5 4.7 %copy-start.7 = (bf16[256,576]{0,1:T(8,128)(2,1)}, bf16[256,576]{0,1:T(8,128)(2,1)S(1)}, u32[]{:S(2)}) copy-start(bf16[256,576]{0,1:T(8,128)(2,1)S(1)} %dynamic-slice_bitcast_fusion.5) | copy-start | bytes 884740 | tf_op jit(solution)/shard_map/while
  129.8 2.0 copy-start.6
  129.9 3.4 copy-start.4
  130.3 6.0 %copy-start.2 = (bf16[128,8,512]{2,0,1:T(8,128)(2,1)}, bf16[128,8,512]{2,0,1:T(8,128)(2,1)S(1)}, u32[]{:S(2)}) copy-start(bf16[128,8,512]{2,0,1:T(8,128)(2,1)S(1)} %fusion.91) | copy-start | bytes 3145732 | tf_op jit(solution)/shard_map/while
  139.9 1.5 copy-start.1
  146.0 3.3 copy-start.8
  153.3 7.1 %copy-start.5 = (bf16[8,128,512]{2,1,0:T(8,128)(2,1)S(1)}, bf16[8,128,512]{2,1,0:T(8,128)(2,1)}, u32[]{:S(2)}) copy-start(bf16[8,128,512]{2,1,0:T(8,128)(2,1)} %get-tuple-element.385) | copy-start | bytes 3145732 | tf_op jit(solution)/shard_map/while
  159.1 4.7 %copy-start.7 = (bf16[256,576]{0,1:T(8,128)(2,1)}, bf16[256,576]{0,1:T(8,128)(2,1)S(1)}, u32[]{:S(2)}) copy-start(bf16[256,576]{0,1:T(8,128)(2,1)S(1)} %dynamic-slice_bitcast_fusion.5) | copy-start | bytes 884740 | tf_op jit(solution)/shard_map/while
  160.4 2.0 copy-start.6
  160.5 3.4 copy-start.4
  160.9 6.0 %copy-start.2 = (bf16[128,8,512]{2,0,1:T(8,128)(2,1)}, bf16[128,8,512]{2,0,1:T(8,128)(2,1)S(1)}, u32[]{:S(2)}) copy-start(bf16[128,8,512]{2,0,1:T(8,128)(2,1)S(1)} %fusion.91) | copy-start | bytes 3145732 | tf_op jit(solution)/shard_map/while
  170.5 1.5 copy-start.1
  176.6 3.2 copy-start.8
  183.9 7.1 %copy-start.5 = (bf16[8,128,512]{2,1,0:T(8,128)(2,1)S(1)}, bf16[8,128,512]{2,1,0:T(8,128)(2,1)}, u32[]{:S(2)}) copy-start(bf16[8,128,512]{2,1,0:T(8,128)(2,1)} %get-tuple-element.385) | copy-start | bytes 3145732 | tf_op jit(solution)/shard_map/while
  189.7 4.7 %copy-start.7 = (bf16[256,576]{0,1:T(8,128)(2,1)}, bf16[256,576]{0,1:T(8,128)(2,1)S(1)}, u32[]{:S(2)}) copy-start(bf16[256,576]{0,1:T(8,128)(2,1)S(1)} %dynamic-slice_bitcast_fusion.5) | copy-start | bytes 884740 | tf_op jit(solution)/shard_map/while
  191.0 2.0 copy-start.6
  191.1 3.4 copy-start.4
  191.5 6.0 %copy-start.2 = (bf16[128,8,512]{2,0,1:T(8,128)(2,1)}, bf16[128,8,512]{2,0,1:T(8,128)(2,1)S(1)}, u32[]{:S(2)}) copy-start(bf16[128,8,512]{2,0,1:T(8,128)(2,1)S(1)} %fusion.91) | copy-start | bytes 3145732 | tf_op jit(solution)/shard_map/while
  201.1 1.5 copy-start.1
  207.2 3.3 copy-start.8
  214.6 7.1 %copy-start.5 = (bf16[8,128,512]{2,1,0:T(8,128)(2,1)S(1)}, bf16[8,128,512]{2,1,0:T(8,128)(2,1)}, u32[]{:S(2)}) copy-start(bf16[8,128,512]{2,1,0:T(8,128)(2,1)} %get-tuple-element.385) | copy-start | bytes 3145732 | tf_op jit(solution)/shard_map/while
  220.3 4.8 %copy-start.7 = (bf16[256,576]{0,1:T(8,128)(2,1)}, bf16[256,576]{0,1:T(8,128)(2,1)S(1)}, u32[]{:S(2)}) copy-start(bf16[256,576]{0,1:T(8,128)(2,1)S(1)} %dynamic-slice_bitcast_fusion.5) | copy-start | bytes 884740 | tf_op jit(solution)/shard_map/while
  221.6 2.0 copy-start.6
  221.7 3.4 copy-start.4
  222.1 6.0 %copy-start.2 = (bf16[128,8,512]{2,0,1:T(8,128)(2,1)}, bf16[128,8,512]{2,0,1:T(8,128)(2,1)S(1)}, u32[]{:S(2)}) copy-start(bf16[128,8,512]{2,0,1:T(8,128)(2,1)S(1)} %fusion.91) | copy-start | bytes 3145732 | tf_op jit(solution)/shard_map/while
  231.7 1.5 copy-start.1
  237.8 3.2 copy-start.8
  245.2 7.1 %copy-start.5 = (bf16[8,128,512]{2,1,0:T(8,128)(2,1)S(1)}, bf16[8,128,512]{2,1,0:T(8,128)(2,1)}, u32[]{:S(2)}) copy-start(bf16[8,128,512]{2,1,0:T(8,128)(2,1)} %get-tuple-element.385) | copy-start | bytes 3145732 | tf_op jit(solution)/shard_map/while
  250.9 4.7 %copy-start.7 = (bf16[256,576]{0,1:T(8,128)(2,1)}, bf16[256,576]{0,1:T(8,128)(2,1)S(1)}, u32[]{:S(2)}) copy-start(bf16[256,576]{0,1:T(8,128)(2,1)S(1)} %dynamic-slice_bitcast_fusion.5) | copy-start | bytes 884740 | tf_op jit(solution)/shard_map/while
  252.2 2.0 copy-start.6
  252.3 3.4 copy-start.4
  252.7 6.0 %copy-start.2 = (bf16[128,8,512]{2,0,1:T(8,128)(2,1)}, bf16[128,8,512]{2,0,1:T(8,128)(2,1)S(1)}, u32[]{:S(2)}) copy-start(bf16[128,8,512]{2,0,1:T(8,128)(2,1)S(1)} %fusion.91) | copy-start | bytes 3145732 | tf_op jit(solution)/shard_map/while
  262.3 1.5 copy-start.1
  268.4 3.3 copy-start.8
  275.7 7.1 %copy-start.5 = (bf16[8,128,512]{2,1,0:T(8,128)(2,1)S(1)}, bf16[8,128,512]{2,1,0:T(8,128)(2,1)}, u32[]{:S(2)}) copy-start(bf16[8,128,512]{2,1,0:T(8,128)(2,1)} %get-tuple-element.385) | copy-start | bytes 3145732 | tf_op jit(solution)/shard_map/while
  281.5 4.8 %copy-start.7 = (bf16[256,576]{0,1:T(8,128)(2,1)}, bf16[256,576]{0,1:T(8,128)(2,1)S(1)}, u32[]{:S(2)}) copy-start(bf16[256,576]{0,1:T(8,128)(2,1)S(1)} %dynamic-slice_bitcast_fusion.5) | copy-start | bytes 884740 | tf_op jit(solution)/shard_map/while
  282.8 2.0 copy-start.6
  282.9 3.4 copy-start.4
  283.3 6.0 %copy-start.2 = (bf16[128,8,512]{2,0,1:T(8,128)(2,1)}, bf16[128,8,512]{2,0,1:T(8,128)(2,1)S(1)}, u32[]{:S(2)}) copy-start(bf16[128,8,512]{2,0,1:T(8,128)(2,1)S(1)} %fusion.91) | copy-start | bytes 3145732 | tf_op jit(solution)/shard_map/while
  292.9 1.5 copy-start.1
  299.0 3.2 copy-start.8
  308.3 5.9 %copy-start.10 = (bf16[8,128,8,128]{3,2,1,0:T(8,128)(2,1)S(1)}, bf16[8,128,8,128]{3,2,1,0:T(8,128)(2,1)}, u32[]{:S(2)}) copy-start(bf16[8,128,8,128]{3,2,1,0:T(8,128)(2,1)} %get-tuple-element.155) | copy-start | bytes 6291460
  308.3 40.8 %all-to-all-start.1 = ((bf16[128,16,576]{2,1,0:T(8,128)(2,1)}), bf16[128,16,576]{2,1,0:T(8,128)(2,1)}, u32[]{:S(2)}, u32[]{:S(2)}) async-start(bf16[128,16,576]{2,1,0:T(8,128)(2,1)} %bitcast.141), calls=%async_computation.1 | async-start | bytes 5242880 | tf_op jit(solution)/shard_map/all_to_all | solution.py:119
  (7 other events, 6.4 us)
where the time goes:
time: 356 us; the launch traced here: 352 us
  matrix products  132 us (37%)
  local copies, waits for them, and re-layouts  93.6 us (26%)
  waiting for transfers between devices  56.9 us (16%)
  other arithmetic  29.3 us (8%)
  loops' own time  21.9 us (6%)
  starting transfers between devices  17.7 us (5%)
    all_to_all x1, waiting for transfers between devices, on_device(): lax.all_to_all(grad_pieces, ('resp', 'head'), split_axis=0, concat_axis=0...  33 us
    dot_general x8, matrix products, attend(): jnp.einsum('lhc,kc->hlk', grad_latent, values, preferred_element_type=jnp...  28.8 us
    dot_general x8, matrix products, attend(): jnp.einsum('lhc,hcv->lhv', out_latent, up_value, preferred_element_type=j...  26.1 us
    dot_general x8, matrix products, attend(): jnp.einsum('hlk,lhc->kc', grad_scores[:, :, :key_span], full_query, prefe...  26 us
    sub x8, matrix products, attend(): weights = jnp.exp(scores - top_score)  24.2 us
    all_to_all x1, waiting for transfers between devices, on_device(): lax.all_to_all(copies, ('resp', 'head'), split_axis=0, concat_axis=0, til...  23.9 us
    dynamic_slice x32, local copies, waits for them, and re-layouts, on_device(): lax.scan(one_response, zero_buffer, (shaped_query, shaped_own, shaped_gra...  22.8 us
    another operation x1, loops' own time, on_device(): lax.scan(one_response, zero_buffer, (shaped_query, shaped_own, shaped_gra...  21.9 us
  transfers between devices with their start and end apart: 2, of which 2 were waited for; matrix products, arithmetic and copies ran while one was open for 4% of the time, Pallas kernels for 0%

commit v1 on v0

v1 whole, which is shorter than its diff:
```python
import functools
import math

import jax
import jax.numpy as jnp
from jax import lax
from jax.experimental import pallas as pl
from jax.experimental.pallas import tpu as pltpu
from jax.sharding import PartitionSpec as P

BF16 = jnp.bfloat16
F32 = jnp.float32
VMEM_LIMIT = 60 * 1024 * 1024
LOG2E = 1.4426950408889634


def dot_nn(a, b):
    return lax.dot_general(a, b, (((1,), (0,)), ((), ())), preferred_element_type=F32)


def dot_nt(a, b):
    return lax.dot_general(a, b, (((1,), (1,)), ((), ())), preferred_element_type=F32)


def up_kernel(q_ref, uk_ref, go_ref, uv_ref, fq_ref, gl_ref):
    resp_count, channels, _ = fq_ref.shape
    latent_width = gl_ref.shape[1]
    rope = channels - latent_width
    rows = q_ref.shape[0] // resp_count
    nope = uk_ref.shape[1]
    span = 2 * nope
    for e in range(2):
        lead = e * rope
        lift = uk_ref[e]
        parts = [lift, jnp.zeros((nope - lead, latent_width), BF16)]
        if lead:
            parts = [jnp.zeros((lead, latent_width), BF16)] + parts
        lifted = jnp.concatenate(parts, axis=0).T
        row = lax.broadcasted_iota(jnp.int32, (rope, span), 0)
        col = lax.broadcasted_iota(jnp.int32, (rope, span), 1)
        pick = jnp.where(col == row + (nope + lead), 1.0, 0.0).astype(BF16)
        up_value = uv_ref[e]
        for j in range(0, resp_count, 2):
            window = q_ref[pl.ds(j * rows, 2 * rows), pl.ds(e * nope, span)]
            grad = go_ref[pl.ds(j * rows, 2 * rows), pl.ds(e * rows, rows)]
            top = dot_nt(lifted, window).astype(BF16)
            low = dot_nt(pick, window).astype(BF16)
            lat = dot_nt(up_value, grad).astype(BF16)
            for i in range(2):
                src = slice(i * rows, (i + 1) * rows)
                dst = pl.ds(e * rows, rows)
                fq_ref[j + i, pl.ds(0, latent_width), dst] = top[:, src]
                fq_ref[j + i, pl.ds(latent_width, rope), dst] = low[:, src]
                gl_ref[j + i, :, dst] = lat[:, src]


def lift_tokens(queries, up_key, grad_out, up_value, resp_count):
    tokens = queries.shape[0]
    rows = tokens // resp_count
    heads, nope, latent_width = up_key.shape
    value_width = up_value.shape[2]
    head_width = queries.shape[1] // heads
    channels = latent_width + head_width - nope
    return pl.pallas_call(
        up_kernel,
        grid=(heads // 2,),
        in_specs=[
            pl.BlockSpec((tokens, 2 * head_width), lambda i: (0, i)),
            pl.BlockSpec((2, nope, latent_width), lambda i: (i, 0, 0)),
            pl.BlockSpec((tokens, 2 * value_width), lambda i: (0, i)),
            pl.BlockSpec((2, latent_width, value_width), lambda i: (i, 0, 0)),
        ],
        out_specs=[
            pl.BlockSpec((resp_count, channels, 2 * rows), lambda i: (0, 0, i)),
            pl.BlockSpec((resp_count, latent_width, 2 * rows), lambda i: (0, 0, i)),
        ],
        out_shape=[
            jax.ShapeDtypeStruct((resp_count, channels, heads * rows), BF16),
            jax.ShapeDtypeStruct((resp_count, latent_width, heads * rows), BF16),
        ],
        compiler_params=pltpu.CompilerParams(vmem_limit_bytes=VMEM_LIMIT),
        cost_estimate=pl.CostEstimate(
            flops=4 * tokens * heads * nope * latent_width,
            bytes_accessed=30 * 1024 * 1024,
            transcendentals=0,
        ),
        name="lift_tokens",
    )(queries, up_key, grad_out, up_value)


def attend_kernel(
    head_width, slot_ref, len_ref, latent_ref, own_ref, fq_ref, gl_ref, aT_ref, piece_ref, acc_ref, gs_ref
):
    j = pl.program_id(0)
    steps = pl.num_programs(0)
    key_span = latent_ref.shape[1]
    rows = own_ref.shape[0]
    channels = own_ref.shape[1]
    latent_width = gl_ref.shape[1]
    columns = fq_ref.shape[2]
    rope = channels - latent_width
    scaling = 1.0 / math.sqrt(head_width)
    chunk = 2 * rows

    @pl.when(j == 0)
    def _():
        acc_ref[...] = jnp.zeros_like(acc_ref)

    length = len_ref[j]
    keys = jnp.concatenate([latent_ref[0], own_ref[...]], axis=0)
    values = keys[:, :latent_width]
    row = lax.broadcasted_iota(jnp.int32, (key_span + rows, chunk), 0)
    col = lax.broadcasted_iota(jnp.int32, (key_span + rows, chunk), 1) % rows
    bound = jnp.where(row < key_span, length, col + (key_span + 1))
    allowed = row < bound
    for c in range(columns // chunk):
        at = pl.ds(c * chunk, chunk)
        scores = dot_nn(keys, fq_ref[0, :, at])
        grad_att = dot_nn(values, gl_ref[0, :, at])
        scores = jnp.where(allowed, scores * (scaling * LOG2E), -1e30)
        top = jnp.max(scores, axis=0, keepdims=True)
        weights = jnp.exp2(scores - top)
        total = jnp.sum(weights, axis=0, keepdims=True)
        attention = weights * (1.0 / total)
        inner = jnp.sum(attention * grad_att, axis=0, keepdims=True)
        aT_ref[0, :, at] = attention.astype(BF16)
        grad_scores = attention[:key_span] * ((grad_att[:key_span] - inner) * scaling)
        gs_ref[:, at] = grad_scores.astype(BF16)
    combined = dot_nt(gs_ref[...], fq_ref[0])
    value_term = dot_nt(aT_ref[0, pl.ds(0, key_span), :], gl_ref[0])
    slot = slot_ref[j]
    acc_ref[slot, :, pl.ds(0, latent_width)] += combined[:, :latent_width] + value_term
    acc_ref[slot, :, pl.ds(latent_width, rope)] += combined[:, latent_width:]

    @pl.when(j == steps - 1)
    def _():
        piece_ref[...] = acc_ref[...].astype(BF16)


def attend(slots, lengths, gathered, resp_latent, full_t, grad_t, head_width):
    groups, key_span, channels = gathered.shape
    resp_count, _, columns = full_t.shape
    latent_width = grad_t.shape[1]
    rows = resp_latent.shape[0] // resp_count
    grid_spec = pltpu.PrefetchScalarGridSpec(
        num_scalar_prefetch=2,
        grid=(resp_count,),
        in_specs=[
            pl.BlockSpec((1, key_span, channels), lambda j, s, n: (s[j], 0, 0)),
            pl.BlockSpec((rows, channels), lambda j, s, n: (j, 0)),
            pl.BlockSpec((1, channels, columns), lambda j, s, n: (j, 0, 0)),
            pl.BlockSpec((1, latent_width, columns), lambda j, s, n: (j, 0, 0)),
        ],
        out_specs=[
            pl.BlockSpec((1, key_span + rows, columns), lambda j, s, n: (j, 0, 0)),
            pl.BlockSpec((groups, key_span, channels), lambda j, s, n: (0, 0, 0)),
        ],
        scratch_shapes=[
            pltpu.VMEM((groups, key_span, channels), F32),
            pltpu.VMEM((key_span, columns), BF16),
        ],
    )
    return pl.pallas_call(
        functools.partial(attend_kernel, head_width),
        grid_spec=grid_spec,
        out_shape=[
            jax.ShapeDtypeStruct((resp_count, key_span + rows, columns), BF16),
            jax.ShapeDtypeStruct((groups, key_span, channels), BF16),
        ],
        compiler_params=pltpu.CompilerParams(vmem_limit_bytes=VMEM_LIMIT),
        cost_estimate=pl.CostEstimate(
            flops=2 * resp_count * columns * 384 * 2200,
            bytes_accessed=30 * 1024 * 1024,
            transcendentals=resp_count * columns * 384,
        ),
        name="attend",
    )(slots, lengths, gathered, resp_latent, full_t, grad_t)


def output_kernel(slot_ref, latent_ref, own_ref, aT_ref, uv_ref, out_ref):
    rows = own_ref.shape[0]
    heads, latent_width, value_width = uv_ref.shape
    values = jnp.concatenate(
        [latent_ref[0, :, pl.ds(0, latent_width)], own_ref[:, pl.ds(0, latent_width)]], axis=0
    )
    values_t = values.T
    for i in range(0, heads, 2):
        at = pl.ds(i * rows, 2 * rows)
        latent_t = dot_nn(values_t, aT_ref[0, :, at]).astype(BF16)
        for e in range(2):
            part = latent_t[:, e * rows : (e + 1) * rows].T
            done = dot_nn(part, uv_ref[i + e])
            out_ref[:, pl.ds((i + e) * value_width, value_width)] = done.astype(BF16)


def outputs(slots, gathered, resp_latent, attention_t, up_value):
    groups, key_span, channels = gathered.shape
    resp_count, keys, columns = attention_t.shape
    heads, latent_width, value_width = up_value.shape
    rows = resp_latent.shape[0] // resp_count
    grid_spec = pltpu.PrefetchScalarGridSpec(
        num_scalar_prefetch=1,
        grid=(resp_count,),
        in_specs=[
            pl.BlockSpec((1, key_span, channels), lambda j, s: (s[j], 0, 0)),
            pl.BlockSpec((rows, channels), lambda j, s: (j, 0)),
            pl.BlockSpec((1, keys, columns), lambda j, s: (j, 0, 0)),
            pl.BlockSpec((heads, latent_width, value_width), lambda j, s: (0, 0, 0)),
        ],
        out_specs=pl.BlockSpec((rows, heads * value_width), lambda j, s: (j, 0)),
    )
    return pl.pallas_call(
        output_kernel,
        grid_spec=grid_spec,
        out_shape=jax.ShapeDtypeStruct((resp_count * rows, heads * value_width), BF16),
        compiler_params=pltpu.CompilerParams(vmem_limit_bytes=VMEM_LIMIT),
        cost_estimate=pl.CostEstimate(
            flops=2 * resp_count * columns * (384 + 128) * 512,
            bytes_accessed=16 * 1024 * 1024,
            transcendentals=0,
        ),
        name="outputs",
    )(slots, gathered, resp_latent, attention_t, up_value)


def on_device(
    queries, up_key, up_value, prompt_latent, resp_latent, grad_out, response_prompt, prompt_length
):
    groups = lax.axis_size("resp")
    slab_count = lax.axis_size("head")
    my_group = lax.axis_index("resp")
    owned, slab_rows, channels = prompt_latent.shape
    key_span = slab_rows * slab_count
    resp_count = response_prompt.shape[0] // groups
    owners = response_prompt // owned
    hit_table = owners[:, None] == jnp.arange(groups)[None, :]
    wanted = jnp.max(
        jnp.where(hit_table, (response_prompt % owned)[:, None], -1).reshape(
            groups, resp_count, groups
        ),
        axis=1,
    )
    wanted_mine = lax.dynamic_index_in_dim(wanted, my_group, 1, False)
    outgoing = jnp.where(
        (wanted_mine == 1)[:, None, None], prompt_latent[1][None], prompt_latent[0][None]
    )
    copies = jnp.repeat(outgoing, slab_count, axis=0)
    arrived = lax.all_to_all(copies, ("resp", "head"), split_axis=0, concat_axis=0, tiled=True)
    gathered = arrived.reshape(groups, key_span, channels)
    local_prompt = lax.dynamic_slice_in_dim(response_prompt, my_group * resp_count, resp_count)
    slots = local_prompt // owned
    hits = local_prompt[:, None] == jnp.arange(prompt_length.shape[0])[None, :]
    lengths = jnp.sum(jnp.where(hits, prompt_length[None, :], 0), axis=1)
    full_t, grad_t = lift_tokens(queries, up_key, grad_out, up_value, resp_count)
    attention_t, pieces = attend(slots, lengths, gathered, resp_latent, full_t, grad_t, queries.shape[1] // up_key.shape[0])
    returned_grad = lax.all_to_all(
        pieces.reshape(groups * slab_count, slab_rows, channels),
        ("resp", "head"),
        split_axis=0,
        concat_axis=0,
        tiled=True,
    )
    attn_out = outputs(slots, gathered, resp_latent, attention_t, up_value)
    summed = jnp.sum(
        returned_grad.reshape(groups, slab_count, slab_rows, channels).astype(F32), axis=1
    )
    prompt_grad = jnp.stack(
        [
            jnp.sum(jnp.where((wanted_mine == p)[:, None, None], summed, 0.0), axis=0)
            for p in range(owned)
        ]
    )
    return (attn_out, prompt_grad)


def solution(mesh):
    return jax.shard_map(
        on_device,
        mesh=mesh,
        in_specs=(
            P("resp", "head"),
            P("head", None, None),
            P("head", None, None),
            P("resp", "head", None),
            P("resp", None),
            P("resp", "head"),
            P(),
            P(),
        ),
        out_specs=(P("resp", "head"), P("resp", "head", None)),
        check_vma=False,
    )
```

time: 356 us -> 118 us (0.33)
  matrix products: 132 us -> 0 us
  local copies, waits for them, and re-layouts: 93.6 us -> 6.6 us
  Pallas kernels: 0 us -> 55 us
  other arithmetic: 29.3 us -> 3.46 us
  loops' own time: 21.9 us -> 0 us
  waiting for transfers between devices: 56.9 us -> 35.2 us
    dot_general x50 -> x0, matrix products: 108 us -> none  [the longest x8 28.8 us: attend(): jnp.einsum('lhc,kc->hlk', grad_latent, values, preferred_element_type=jnp...]
    pallas_call x0 -> x3, Pallas kernels: none -> 55 us  [the longest x1 23.6 us: attend(): pl.pallas_call(functools.partial(attend_kernel, head_width), grid_spec=gr...]
    dynamic_slice x42 -> x0, local copies, waits for them, and re-layouts: 35 us -> none  [the longest x32 22.8 us: on_device(): lax.scan(one_response, zero_buffer, (shaped_query, shaped_own, shaped_gra...]
    sub x8 -> x0, matrix products: 24.2 us -> none  [attend(): weights = jnp.exp(scores - top_score)]
    another operation x1 -> x0, loops' own time: 21.9 us -> none  [on_device(): lax.scan(one_response, zero_buffer, (shaped_query, shaped_own, shaped_gra...]
    all_to_all x1, waiting for transfers between devices: 33 us -> 15.5 us  [on_device(): lax.all_to_all(pieces.reshape(groups * slab_count, slab_rows, channels),...]
    squeeze x16 -> x0, local copies, waits for them, and re-layouts: 15.3 us -> none  [the longest x8 7.9 us: one_response(): latent = lax.dynamic_index_in_dim(gathered, owner_slot, 0, False)]
    reduce_sum x9 -> x3, other arithmetic: 13.1 us -> 1.18 us  [the longest x1 0.69 us: on_device(): lengths = jnp.sum(jnp.where(hits, prompt_length[None, :], 0), axis=1)]
  transfers between devices with their start and end apart: 2 -> 2, of which waited for: 2 -> 2; matrix products, arithmetic and copies ran while one was open for 4% -> 3% of each run, Pallas kernels for 0% -> 27%
where the time goes in v1:
time: 118 us; the launch traced here: 117 us
  Pallas kernels  55 us (47%)
  waiting for transfers between devices  35.2 us (30%)
  starting transfers between devices  16.3 us (14%)
  local copies, waits for them, and re-layouts  6.6 us (6%)
  other arithmetic  3.46 us (3%)
    pallas_call x1, Pallas kernels, attend(): pl.pallas_call(functools.partial(attend_kernel, head_width), grid_spec=gr...  23.6 us
    all_to_all x1, waiting for transfers between devices, on_device(): lax.all_to_all(copies, ('resp', 'head'), split_axis=0, concat_axis=0, til...  19.7 us
    pallas_call x1, Pallas kernels, outputs(): pl.pallas_call(output_kernel, grid_spec=grid_spec, out_shape=jax.ShapeDty...  19.6 us
    all_to_all x1, waiting for transfers between devices, on_device(): lax.all_to_all(pieces.reshape(groups * slab_count, slab_rows, channels),...  15.5 us
    pallas_call x1, Pallas kernels, lift_tokens(): pl.pallas_call(up_kernel, grid=(heads // 2,), in_specs=[pl.BlockSpec((tok...  11.7 us
    all_to_all x1, starting transfers between devices, on_device(): lax.all_to_all(copies, ('resp', 'head'), split_axis=0, concat_axis=0, til...  11.5 us
    all_to_all x1, starting transfers between devices, on_device(): lax.all_to_all(pieces.reshape(groups * slab_count, slab_rows, channels),...  4.85 us
    unnamed x7, local copies, waits for them, and re-layouts  4.01 us
  transfers between devices with their start and end apart: 2, of which 2 were waited for; matrix products, arithmetic and copies ran while one was open for 3% of the time, Pallas kernels for 27%

profile of v1, /device:TPU:1, one launch (start us, length us, event | category | flops | bytes accessed | tf_op | source)
XLA Modules:
  0.0 117.3 jit_solution(16187720546053317518)
XLA Ops:
  0.6 0.7 and_select_fusion.1
  1.3 0.1 eq.52
  1.4 0.1 broadcast_in_dim.82
  1.5 0.8 slice_bitcast_fusion.1
  2.2 0.1 select_reduce_fusion.2
  2.3 0.2 compare_reduce_fusion
  2.5 0.1 broadcast_select_fusion
  2.6 1.7 %broadcast_in_dim.90 = bf16[8,16,16,576]{3,2,1,0:T(8,128)(2,1)} broadcast(bf16[8,16,576]{2,1,0:T(8,128)(2,1)S(1)} %broadcast_select_fusion), dimensions={0,2,3} | broadcast | bytes 2506752 | tf_op jit(solution)/shard_map/broadcast_in_dim | solution.py:247
  4.3 0.0 copy-start.1
  4.3 0.0 copy-start.2
  4.3 11.5 %all-to-all-start = ((bf16[128,16,576]{2,1,0:T(8,128)(2,1)}), bf16[128,16,576]{2,1,0:T(8,128)(2,1)S(1)}, u32[]{:S(2)}, u32[]{:S(2)}) async-start(bf16[128,16,576]{2,1,0:T(8,128)(2,1)} %bitcast.2), calls=%async_computation | async-start | bytes 5242880 | tf_op jit(solution)/shard_map/all_to_all | solution.py:248
  15.8 2.5 %copy.15.own_ref = bf16[1024,576]{1,0:T(8,128)(2,1)} copy(bf16[1024,576]{0,1:T(8,128)(2,1)} %param.12) | data formatting | bytes 2359296 | tf_op args[4]
  18.3 0.0 copy-done.1
  18.3 0.6 and_select_fusion.2
  18.8 0.0 copy-done.2
  18.8 0.7 select_reduce_fusion.3.len_ref
  19.5 11.7 %lift_tokens.1 = (bf16[8,576,1024]{2,1,0:T(8,128)(2,1)}, bf16[8,512,1024]{2,1,0:T(8,128)(2,1)}) custom-call(bf16[1024,1536]{1,0:T(8,128)(2,1)} %q_ref.1, bf16[8,128,512]{2,1,0:T(8,128)(2,1)} %uk_ref.1, bf16[1024,1024]{1,0:T(8,128)(2,1)} %go_ref.1, bf16[8,512,128]{2,1,0:T(8,128)(2,1)} %uv_ref.3), custom_call_target="tpu_custom_call" | custom-call | flops 2147483648 | bytes 31457280 | tf_op jit(solution)/shard_map/lift_tokens/pallas_call | solution.py:64
  31.2 19.7 %all-to-all-done = bf16[128,16,576]{2,1,0:T(8,128)(2,1)S(1)} async-done(((bf16[128,16,576]{2,1,0:T(8,128)(2,1)}), bf16[128,16,576]{2,1,0:T(8,128)(2,1)S(1)}, u32[]{:S(2)}, u32[]{:S(2)}) %all-to-all-start) | async-done | bytes 2359328 | tf_op jit(solution)/shard_map/all_to_all | solution.py:248
  50.9 0.0 copy-start
  50.9 1.5 %copy-done = bf16[128,16,576]{2,1,0:T(8,128)(2,1)} copy-done((bf16[128,16,576]{2,1,0:T(8,128)(2,1)}, bf16[128,16,576]{2,1,0:T(8,128)(2,1)S(1)}, u32[]{:S(2)}) %copy-start) | copy-done | bytes 2359320
  52.5 23.6 %attend.1 = (bf16[8,384,1024]{2,1,0:T(8,128)(2,1)}, bf16[8,256,576]{2,1,0:T(8,128)(2,1)}) custom-call(s32[8]{0:T(128)} %get-tuple-element.14.slot_ref, s32[8]{0:T(128)} %select_reduce_fusion.3.len_ref, bf16[8,256,576]{2,1,0:T(8,128)(2,1)} %bitcast.12, bf16[1024,576]{1,0:T(8,128)(2,1)} %copy.15.own_ref, bf16[8,576,1024]{2,1,0:T(8,128)(2,1)} %get-tuple-element.6.fq_ref, ...), custom_call_target="tpu_custom_call" | custom-call | flops 13841203200 | bytes 31457280 | tf_op jit(solution)/shard_map/attend/pallas_call | solution.py:163
  76.1 4.9 %all-to-all-start.1 = ((bf16[128,16,576]{2,1,0:T(8,128)(2,1)}), bf16[128,16,576]{2,1,0:T(8,128)(2,1)S(1)}, u32[]{:S(2)}, u32[]{:S(2)}) async-start(bf16[128,16,576]{2,1,0:T(8,128)(2,1)} %bitcast.14), calls=%async_computation.1 | async-start | bytes 5242880 | tf_op jit(solution)/shard_map/all_to_all | solution.py:256
  81.0 19.6 %outputs.1 = bf16[1024,1024]{1,0:T(8,128)(2,1)} custom-call(s32[8]{0:T(128)} %get-tuple-element.14.slot_ref, bf16[8,256,576]{2,1,0:T(8,128)(2,1)} %bitcast.13, bf16[1024,576]{1,0:T(8,128)(2,1)} %copy.15.own_ref, bf16[8,384,1024]{2,1,0:T(8,128)(2,1)} %get-tuple-element.8.aT_ref, bf16[8,512,128]{2,1,0:T(8,128)(2,1)} %uv_ref.3), custom_call_target="tpu_custom_call" | custom-call | flops 4294967296 | bytes 16777216 | tf_op jit(solution)/shard_map/outputs/pallas_call | solution.py:212
  100.6 15.5 %all-to-all-done.1 = bf16[128,16,576]{2,1,0:T(8,128)(2,1)S(1)} async-done(((bf16[128,16,576]{2,1,0:T(8,128)(2,1)}), bf16[128,16,576]{2,1,0:T(8,128)(2,1)S(1)}, u32[]{:S(2)}, u32[]{:S(2)}) %all-to-all-start.1) | async-done | bytes 2359328 | tf_op jit(solution)/shard_map/all_to_all | solution.py:256
  116.1 0.4 convert_reduce_fusion
  116.5 0.1 select_reduce_fusion.1
  116.6 0.6 pad_maximum_fusion
Async XLA Ops:
  4.3 14.0 %copy-start.1 = (s32[64]{0:T(128)S(1)}, s32[64]{0:T(128)}, u32[]{:S(2)}) copy-start(s32[64]{0:T(128)} %param.14) | copy-start | bytes 772
  4.3 14.6 %copy-start.2 = (s32[16]{0:T(128)S(1)}, s32[16]{0:T(128)}, u32[]{:S(2)}) copy-start(s32[16]{0:T(128)} %param.15) | copy-start | bytes 196
  4.3 46.6 %all-to-all-start = ((bf16[128,16,576]{2,1,0:T(8,128)(2,1)}), bf16[128,16,576]{2,1,0:T(8,128)(2,1)S(1)}, u32[]{:S(2)}, u32[]{:S(2)}) async-start(bf16[128,16,576]{2,1,0:T(8,128)(2,1)} %bitcast.2), calls=%async_computation | async-start | bytes 5242880 | tf_op jit(solution)/shard_map/all_to_all | solution.py:248
  50.9 1.6 %copy-start = (bf16[128,16,576]{2,1,0:T(8,128)(2,1)}, bf16[128,16,576]{2,1,0:T(8,128)(2,1)S(1)}, u32[]{:S(2)}) copy-start(bf16[128,16,576]{2,1,0:T(8,128)(2,1)S(1)} %all-to-all-done) | copy-start | bytes 7077892
  76.1 40.0 %all-to-all-start.1 = ((bf16[128,16,576]{2,1,0:T(8,128)(2,1)}), bf16[128,16,576]{2,1,0:T(8,128)(2,1)S(1)}, u32[]{:S(2)}, u32[]{:S(2)}) async-start(bf16[128,16,576]{2,1,0:T(8,128)(2,1)} %bitcast.14), calls=%async_computation.1 | async-start | bytes 5242880 | tf_op jit(solution)/shard_map/all_to_all | solution.py:256

commit v2 on v1

v2 whole, which is shorter than its diff:
```python
import functools
import math

import jax
import jax.numpy as jnp
from jax import lax
from jax.experimental import pallas as pl
from jax.experimental.pallas import tpu as pltpu
from jax.sharding import PartitionSpec as P

BF16 = jnp.bfloat16
F32 = jnp.float32
LOG2E = 1.4426950408889634


def dot_nn(a, b):
    return lax.dot_general(a, b, (((1,), (0,)), ((), ())), preferred_element_type=F32)


def dot_nt(a, b):
    return lax.dot_general(a, b, (((1,), (1,)), ((), ())), preferred_element_type=F32)


def up_kernel(q_ref, uk_ref, go_ref, uv_ref, fq_ref, gl_ref):
    resp_count, channels, _ = fq_ref.shape
    latent_width = gl_ref.shape[1]
    rope = channels - latent_width
    rows = q_ref.shape[0] // resp_count
    nope = uk_ref.shape[1]
    span = 2 * nope
    for e in range(2):
        lead = e * rope
        lift = uk_ref[e]
        parts = [lift, jnp.zeros((nope - lead, latent_width), BF16)]
        if lead:
            parts = [jnp.zeros((lead, latent_width), BF16)] + parts
        lifted = jnp.concatenate(parts, axis=0).T
        row = lax.broadcasted_iota(jnp.int32, (rope, span), 0)
        col = lax.broadcasted_iota(jnp.int32, (rope, span), 1)
        pick = jnp.where(col == row + (nope + lead), 1.0, 0.0).astype(BF16)
        up_value = uv_ref[e]
        for j in range(0, resp_count, 2):
            window = q_ref[pl.ds(j * rows, 2 * rows), pl.ds(e * nope, span)]
            grad = go_ref[pl.ds(j * rows, 2 * rows), pl.ds(e * rows, rows)]
            top = dot_nt(lifted, window).astype(BF16)
            low = dot_nt(pick, window).astype(BF16)
            lat = dot_nt(up_value, grad).astype(BF16)
            for i in range(2):
                src = slice(i * rows, (i + 1) * rows)
                dst = pl.ds(e * rows, rows)
                fq_ref[j + i, pl.ds(0, latent_width), dst] = top[:, src]
                fq_ref[j + i, pl.ds(latent_width, rope), dst] = low[:, src]
                gl_ref[j + i, :, dst] = lat[:, src]


def lift_tokens(queries, up_key, grad_out, up_value, resp_count):
    tokens = queries.shape[0]
    rows = tokens // resp_count
    heads, nope, latent_width = up_key.shape
    value_width = up_value.shape[2]
    head_width = queries.shape[1] // heads
    channels = latent_width + head_width - nope
    return pl.pallas_call(
        up_kernel,
        grid=(heads // 2,),
        in_specs=[
            pl.BlockSpec((tokens, 2 * head_width), lambda i: (0, i)),
            pl.BlockSpec((2, nope, latent_width), lambda i: (i, 0, 0)),
            pl.BlockSpec((tokens, 2 * value_width), lambda i: (0, i)),
            pl.BlockSpec((2, latent_width, value_width), lambda i: (i, 0, 0)),
        ],
        out_specs=[
            pl.BlockSpec((resp_count, channels, 2 * rows), lambda i: (0, 0, i)),
            pl.BlockSpec((resp_count, latent_width, 2 * rows), lambda i: (0, 0, i)),
        ],
        out_shape=[
            jax.ShapeDtypeStruct((resp_count, channels, heads * rows), BF16),
            jax.ShapeDtypeStruct((resp_count, latent_width, heads * rows), BF16),
        ],
        compiler_params=pltpu.CompilerParams(vmem_limit_bytes=14*1024*1024),
        cost_estimate=pl.CostEstimate(
            flops=4 * tokens * heads * nope * latent_width,
            bytes_accessed=30 * 1024 * 1024,
            transcendentals=0,
        ),
        name="lift_tokens",
    )(queries, up_key, grad_out, up_value)


def pack_rows(rows):
    slab, channels = rows.shape
    blocks = channels // 128
    half = slab // 2
    tail = jnp.concatenate([rows[:half, 128 * blocks :], rows[half:, 128 * blocks :]], axis=1)
    return jnp.concatenate([rows[:, 128 * c : 128 * (c + 1)] for c in range(blocks)] + [tail], axis=0)


def pack_kernel(prompt_ref, group_ref, latent_ref, out_ref):
    groups, slab_count, packed_rows, lanes = out_ref.shape
    owned = latent_ref.shape[0]
    resp_count = prompt_ref.shape[0] // groups
    packed = [pack_rows(latent_ref[p].astype(F32)) for p in range(owned)]
    for r in range(groups):
        wanted = jnp.int32(-1)
        for i in range(resp_count):
            prompt = prompt_ref[r * resp_count + i]
            wanted = jnp.where(prompt // owned == group_ref[0], prompt % owned, wanted)
        chosen = packed[0]
        for p in range(1, owned):
            chosen = jnp.where(wanted == p, packed[p], chosen)
        chosen = chosen.astype(BF16)
        out_ref[r] = jnp.broadcast_to(chosen[None], (slab_count, packed_rows, lanes))


def pack(response_prompt, my_group, prompt_latent, groups, slab_count):
    owned, slab_rows, channels = prompt_latent.shape
    packed_rows = slab_rows * channels // 128
    return pl.pallas_call(
        pack_kernel,
        grid_spec=pltpu.PrefetchScalarGridSpec(
            num_scalar_prefetch=2,
            grid=(1,),
            in_specs=[pl.BlockSpec((owned, slab_rows, channels), lambda i, p, g: (0, 0, 0))],
            out_specs=pl.BlockSpec(
                (groups, slab_count, packed_rows, 128), lambda i, p, g: (0, 0, 0, 0)
            ),
        ),
        out_shape=jax.ShapeDtypeStruct((groups, slab_count, packed_rows, 128), BF16),
        compiler_params=pltpu.CompilerParams(vmem_limit_bytes=10 * 1024 * 1024),
        name="pack",
    )(response_prompt, my_group, prompt_latent)


def own_kernel(head_width, own_ref, fq_ref, gl_ref, e_ref, stat_ref):
    rows = own_ref.shape[0]
    latent_width = gl_ref.shape[1]
    columns = fq_ref.shape[2]
    scaling = LOG2E / math.sqrt(head_width)
    chunk = 2 * rows
    keys = own_ref[...]
    values = keys[:, :latent_width]
    row = lax.broadcasted_iota(jnp.int32, (rows, chunk), 0)
    col = lax.broadcasted_iota(jnp.int32, (rows, chunk), 1) % rows
    allowed = row <= col
    for c in range(columns // chunk):
        at = pl.ds(c * chunk, chunk)
        scores = dot_nn(keys, fq_ref[0, :, at])
        grad_att = dot_nn(values, gl_ref[0, :, at])
        scores = jnp.where(allowed, scores * scaling, -1e30)
        top = jnp.max(scores, axis=0, keepdims=True)
        weights = jnp.exp2(scores - top)
        e_ref[0, :, at] = weights.astype(BF16)
        stat_ref[0, pl.ds(0, 1), at] = top
        stat_ref[0, pl.ds(1, 1), at] = jnp.sum(weights, axis=0, keepdims=True)
        stat_ref[0, pl.ds(2, 1), at] = jnp.sum(weights * grad_att, axis=0, keepdims=True)


def own_scores(resp_latent, full_t, grad_t, head_width):
    resp_count, channels, columns = full_t.shape
    latent_width = grad_t.shape[1]
    rows = resp_latent.shape[0] // resp_count
    return pl.pallas_call(
        functools.partial(own_kernel, head_width),
        grid=(resp_count,),
        in_specs=[
            pl.BlockSpec((rows, channels), lambda j: (j, 0)),
            pl.BlockSpec((1, channels, columns), lambda j: (j, 0, 0)),
            pl.BlockSpec((1, latent_width, columns), lambda j: (j, 0, 0)),
        ],
        out_specs=[
            pl.BlockSpec((1, rows, columns), lambda j: (j, 0, 0)),
            pl.BlockSpec((1, 8, columns), lambda j: (j, 0, 0)),
        ],
        out_shape=[
            jax.ShapeDtypeStruct((resp_count, rows, columns), BF16),
            jax.ShapeDtypeStruct((resp_count, 8, columns), F32),
        ],
        compiler_params=pltpu.CompilerParams(vmem_limit_bytes=10*1024*1024),
        cost_estimate=pl.CostEstimate(
            flops=2 * resp_count * columns * rows * (channels + latent_width),
            bytes_accessed=22 * 1024 * 1024,
            transcendentals=resp_count * columns * rows,
        ),
        name="own_scores",
    )(resp_latent, full_t, grad_t)


def unpack_latent(packed_ref, slab):
    slabs, packed_rows, lanes = packed_ref.shape[1:]
    return jnp.concatenate(
        [
            jnp.concatenate(
                [packed_ref[0, h, pl.ds(slab * c, slab), :] for h in range(slabs)], axis=0
            )
            for c in range(packed_rows // slab)
        ],
        axis=1,
    )


def unpack_rope(packed_ref, slab):
    slabs, packed_rows, lanes = packed_ref.shape[1:]
    rows = []
    for h in range(slabs):
        tail = packed_ref[0, h].astype(F32)[packed_rows - slab // 2 :]
        rows += [tail[:, : lanes // 2], tail[:, lanes // 2 :]]
    return jnp.concatenate(rows, axis=0).astype(BF16)


def attend_kernel(
    head_width,
    slot_ref,
    len_ref,
    latent_ref,
    stat_ref,
    fq_ref,
    gl_ref,
    aT_ref,
    ratio_ref,
    piece_ref,
    acc_ref,
    gs_ref,
):
    j = pl.program_id(0)
    steps = pl.num_programs(0)
    channels = fq_ref.shape[1]
    latent_width = gl_ref.shape[1]
    columns = fq_ref.shape[2]
    rope = channels - latent_width
    groups, key_span, _ = acc_ref.shape
    slabs = latent_ref.shape[1]
    slab = key_span // slabs
    scaling = 1.0 / math.sqrt(head_width)
    chunk = 256

    @pl.when(j == 0)
    def _():
        acc_ref[...] = jnp.zeros_like(acc_ref)

    length = len_ref[j]
    values = unpack_latent(latent_ref, slab)
    keys = jnp.concatenate([values, unpack_rope(latent_ref, slab)], axis=1)
    row = lax.broadcasted_iota(jnp.int32, (key_span, chunk), 0)
    allowed = row < length
    for c in range(columns // chunk):
        at = pl.ds(c * chunk, chunk)
        scores = dot_nn(keys, fq_ref[0, :, at])
        grad_att = dot_nn(values, gl_ref[0, :, at])
        own_top = stat_ref[0, pl.ds(0, 1), at]
        scores = jnp.where(allowed, scores * (scaling * LOG2E), -1e30)
        top = jnp.maximum(jnp.max(scores, axis=0, keepdims=True), own_top)
        weights = jnp.exp2(scores - top)
        shift = jnp.exp2(own_top - top)
        total = jnp.sum(weights, axis=0, keepdims=True) + shift * stat_ref[0, pl.ds(1, 1), at]
        inverse = 1.0 / total
        inner = jnp.sum(weights * grad_att, axis=0, keepdims=True)
        inner = (inner + shift * stat_ref[0, pl.ds(2, 1), at]) * inverse
        attention = weights * inverse
        aT_ref[0, :, at] = attention.astype(BF16)
        gs_ref[:, at] = (attention * ((grad_att - inner) * scaling)).astype(BF16)
        ratio_ref[0, pl.ds(0, 1), at] = shift * inverse
    combined = dot_nt(gs_ref[...], fq_ref[0])
    value_term = dot_nt(aT_ref[0], gl_ref[0])
    slot = slot_ref[j]
    acc_ref[slot, :, pl.ds(0, latent_width)] += combined[:, :latent_width] + value_term
    acc_ref[slot, :, pl.ds(latent_width, rope)] += combined[:, latent_width:]

    @pl.when(j == steps - 1)
    def _():
        for g in range(groups):
            for h in range(slabs):
                rows = acc_ref[g, pl.ds(h * slab, slab), :]
                piece_ref[g, h] = pack_rows(rows).astype(BF16)


def attend(slots, lengths, gathered, stats, full_t, grad_t, head_width):
    groups, slabs, packed_rows, lanes = gathered.shape
    resp_count, channels, columns = full_t.shape
    key_span = slabs * packed_rows * lanes // channels
    latent_width = grad_t.shape[1]
    grid_spec = pltpu.PrefetchScalarGridSpec(
        num_scalar_prefetch=2,
        grid=(resp_count,),
        in_specs=[
            pl.BlockSpec((1, slabs, packed_rows, lanes), lambda j, s, n: (s[j], 0, 0, 0)),
            pl.BlockSpec((1, 8, columns), lambda j, s, n: (j, 0, 0)),
            pl.BlockSpec((1, channels, columns), lambda j, s, n: (j, 0, 0)),
            pl.BlockSpec((1, latent_width, columns), lambda j, s, n: (j, 0, 0)),
        ],
        out_specs=[
            pl.BlockSpec((1, key_span, columns), lambda j, s, n: (j, 0, 0)),
            pl.BlockSpec((1, 8, columns), lambda j, s, n: (j, 0, 0)),
            pl.BlockSpec((groups, slabs, packed_rows, lanes), lambda j, s, n: (0, 0, 0, 0)),
        ],
        scratch_shapes=[
            pltpu.VMEM((groups, key_span, channels), F32),
            pltpu.VMEM((key_span, columns), BF16),
        ],
    )
    return pl.pallas_call(
        functools.partial(attend_kernel, head_width),
        grid_spec=grid_spec,
        out_shape=[
            jax.ShapeDtypeStruct((resp_count, key_span, columns), BF16),
            jax.ShapeDtypeStruct((resp_count, 8, columns), F32),
            jax.ShapeDtypeStruct((groups, slabs, packed_rows, lanes), BF16),
        ],
        compiler_params=pltpu.CompilerParams(vmem_limit_bytes=20*1024*1024),
        cost_estimate=pl.CostEstimate(
            flops=2 * resp_count * columns * key_span * 2176,
            bytes_accessed=30 * 1024 * 1024,
            transcendentals=resp_count * columns * key_span,
        ),
        name="attend",
    )(slots, lengths, gathered, stats, full_t, grad_t)


def output_kernel(slot_ref, latent_ref, own_ref, aT_ref, e_ref, ratio_ref, uv_ref, out_ref):
    rows = own_ref.shape[0]
    heads, latent_width, value_width = uv_ref.shape
    slab = aT_ref.shape[1] // latent_ref.shape[1]
    values = jnp.concatenate(
        [unpack_latent(latent_ref, slab), own_ref[:, pl.ds(0, latent_width)]], axis=0
    )
    values_t = values.T
    for i in range(0, heads, 2):
        at = pl.ds(i * rows, 2 * rows)
        own = (e_ref[0, :, at].astype(F32) * ratio_ref[0, pl.ds(0, 1), at]).astype(BF16)
        weights = jnp.concatenate([aT_ref[0, :, at], own], axis=0)
        latent_t = dot_nn(values_t, weights).astype(BF16)
        for e in range(2):
            part = latent_t[:, e * rows : (e + 1) * rows].T
            done = dot_nn(part, uv_ref[i + e])
            out_ref[:, pl.ds((i + e) * value_width, value_width)] = done.astype(BF16)


def outputs(slots, gathered, resp_latent, attention_t, own_weights, ratio, up_value):
    groups, slabs, packed_rows, lanes = gathered.shape
    resp_count, key_span, columns = attention_t.shape
    channels = resp_latent.shape[1]
    heads, latent_width, value_width = up_value.shape
    rows = resp_latent.shape[0] // resp_count
    grid_spec = pltpu.PrefetchScalarGridSpec(
        num_scalar_prefetch=1,
        grid=(resp_count,),
        in_specs=[
            pl.BlockSpec((1, slabs, packed_rows, lanes), lambda j, s: (s[j], 0, 0, 0)),
            pl.BlockSpec((rows, channels), lambda j, s: (j, 0)),
            pl.BlockSpec((1, key_span, columns), lambda j, s: (j, 0, 0)),
            pl.BlockSpec((1, rows, columns), lambda j, s: (j, 0, 0)),
            pl.BlockSpec((1, 8, columns), lambda j, s: (j, 0, 0)),
            pl.BlockSpec((heads, latent_width, value_width), lambda j, s: (0, 0, 0)),
        ],
        out_specs=pl.BlockSpec((rows, heads * value_width), lambda j, s: (j, 0)),
    )
    return pl.pallas_call(
        output_kernel,
        grid_spec=grid_spec,
        out_shape=jax.ShapeDtypeStruct((resp_count * rows, heads * value_width), BF16),
        compiler_params=pltpu.CompilerParams(vmem_limit_bytes=12*1024*1024),
        cost_estimate=pl.CostEstimate(
            flops=2 * resp_count * columns * (384 + 128) * 512,
            bytes_accessed=16 * 1024 * 1024,
            transcendentals=0,
        ),
        name="outputs",
    )(slots, gathered, resp_latent, attention_t, own_weights, ratio, up_value)


def on_device(
    queries, up_key, up_value, prompt_latent, resp_latent, grad_out, response_prompt, prompt_length
):
    groups = lax.axis_size("resp")
    slab_count = lax.axis_size("head")
    my_group = lax.axis_index("resp")
    owned, slab_rows, channels = prompt_latent.shape
    resp_count = response_prompt.shape[0] // groups
    owners = response_prompt // owned
    hit_table = owners[:, None] == jnp.arange(groups)[None, :]
    wanted = jnp.max(
        jnp.where(hit_table, (response_prompt % owned)[:, None], -1).reshape(
            groups, resp_count, groups
        ),
        axis=1,
    )
    wanted_mine = lax.dynamic_index_in_dim(wanted, my_group, 1, False)
    copies = pack(
        response_prompt, jnp.reshape(my_group, (1,)), prompt_latent, groups, slab_count
    ).reshape(groups * slab_count, -1, 128)
    arrived = lax.all_to_all(copies, ("resp", "head"), split_axis=0, concat_axis=0, tiled=True)
    gathered = arrived.reshape(groups, slab_count, -1, 128)
    local_prompt = lax.dynamic_slice_in_dim(response_prompt, my_group * resp_count, resp_count)
    slots = local_prompt // owned
    hits = local_prompt[:, None] == jnp.arange(prompt_length.shape[0])[None, :]
    lengths = jnp.sum(jnp.where(hits, prompt_length[None, :], 0), axis=1)
    head_width = queries.shape[1] // up_key.shape[0]
    full_t, grad_t = lift_tokens(queries, up_key, grad_out, up_value, resp_count)
    own_weights, stats = own_scores(resp_latent, full_t, grad_t, head_width)
    attention_t, ratio, pieces = attend(
        slots, lengths, gathered, stats, full_t, grad_t, head_width
    )
    returned_grad = lax.all_to_all(
        pieces.reshape(groups * slab_count, -1, 128),
        ("resp", "head"),
        split_axis=0,
        concat_axis=0,
        tiled=True,
    )
    attn_out = outputs(slots, gathered, resp_latent, attention_t, own_weights, ratio, up_value)
    summed = jnp.sum(returned_grad.reshape(groups, slab_count, -1, 128).astype(F32), axis=1)
    packed = jnp.stack(
        [
            jnp.sum(jnp.where((wanted_mine == p)[:, None, None], summed, 0.0), axis=0)
            for p in range(owned)
        ]
    )
    blocks = channels // 128
    latent = packed[:, : slab_rows * blocks].reshape(owned, blocks, slab_rows, 128)
    tail = packed[:, slab_rows * blocks :].reshape(owned, slab_rows // 2, 2, 64)
    prompt_grad = jnp.concatenate(
        [
            jnp.transpose(latent, (0, 2, 1, 3)).reshape(owned, slab_rows, blocks * 128),
            jnp.transpose(tail, (0, 2, 1, 3)).reshape(owned, slab_rows, 64),
        ],
        axis=2,
    )
    return (attn_out, prompt_grad)


def solution(mesh):
    return jax.shard_map(
        on_device,
        mesh=mesh,
        in_specs=(
            P("resp", "head"),
            P("head", None, None),
            P("head", None, None),
            P("resp", "head", None),
            P("resp", None),
            P("resp", "head"),
            P(),
            P(),
        ),
        out_specs=(P("resp", "head"), P("resp", "head", None)),
        check_vma=False,
    )
```

time: 118 us -> 119 us (level)
  local copies, waits for them, and re-layouts: 6.6 us -> 31.9 us
  waiting for transfers between devices: 35.2 us -> 12.1 us
  Pallas kernels: 55 us -> 51.3 us
  starting transfers between devices: 16.3 us -> 18.4 us
    unnamed x7 -> x41, local copies, waits for them, and re-layouts: 4.01 us -> 31.7 us
    all_to_all x1, waiting for transfers between devices: 19.7 us -> 3.79 us  [on_device(): lax.all_to_all(copies, ('resp', 'head'), split_axis=0, concat_axis=0, til...]
    pallas_call x1, Pallas kernels: 23.6 us -> 16.4 us  [attend(): pl.pallas_call(functools.partial(attend_kernel, head_width), grid_spec=gr...]
    all_to_all x1, waiting for transfers between devices: 15.5 us -> 8.35 us  [on_device(): lax.all_to_all(pieces.reshape(groups * slab_count, -1, 128), ('resp', 'he...]
    pallas_call x0 -> x2, Pallas kernels: none -> 7.12 us  [the longest x1 4.75 us: own_scores(): pl.pallas_call(functools.partial(own_kernel, head_width), grid=(resp_coun...]
    pallas_call x1, Pallas kernels: 11.7 us -> 9.14 us  [lift_tokens(): pl.pallas_call(up_kernel, grid=(heads // 2,), in_specs=[pl.BlockSpec((tok...]
    broadcast_in_dim x2 -> x0, local copies, waits for them, and re-layouts: 2.44 us -> none  [the longest x1 1.68 us: on_device(): copies = jnp.repeat(outgoing, slab_count, axis=0)]
    all_to_all x1, starting transfers between devices: 4.85 us -> 6.51 us  [on_device(): lax.all_to_all(pieces.reshape(groups * slab_count, -1, 128), ('resp', 'he...]
  transfers between devices with their start and end apart: 2 -> 2, of which waited for: 2 -> 2; matrix products, arithmetic and copies ran while one was open for 3% -> 2% of each run, Pallas kernels for 27% -> 28%
where the time goes in v2:
time: 119 us; the launch traced here: 118 us
  Pallas kernels  51.3 us (43%)
  local copies, waits for them, and re-layouts  31.9 us (27%)
  starting transfers between devices  18.4 us (15%)
  waiting for transfers between devices  12.1 us (10%)
  other arithmetic  3.35 us (3%)
    unnamed x41, local copies, waits for them, and re-layouts  31.7 us
    pallas_call x1, Pallas kernels, outputs(): pl.pallas_call(output_kernel, grid_spec=grid_spec, out_shape=jax.ShapeDty...  18.7 us
    pallas_call x1, Pallas kernels, attend(): pl.pallas_call(functools.partial(attend_kernel, head_width), grid_spec=gr...  16.4 us
    all_to_all x1, starting transfers between devices, on_device(): lax.all_to_all(copies, ('resp', 'head'), split_axis=0, concat_axis=0, til...  11.9 us
    pallas_call x1, Pallas kernels, lift_tokens(): pl.pallas_call(up_kernel, grid=(heads // 2,), in_specs=[pl.BlockSpec((tok...  9.14 us
    all_to_all x1, waiting for transfers between devices, on_device(): lax.all_to_all(pieces.reshape(groups * slab_count, -1, 128), ('resp', 'he...  8.35 us
    all_to_all x1, starting transfers between devices, on_device(): lax.all_to_all(pieces.reshape(groups * slab_count, -1, 128), ('resp', 'he...  6.51 us
    pallas_call x1, Pallas kernels, own_scores(): pl.pallas_call(functools.partial(own_kernel, head_width), grid=(resp_coun...  4.75 us
  transfers between devices with their start and end apart: 2, of which 2 were waited for; matrix products, arithmetic and copies ran while one was open for 2% of the time, Pallas kernels for 28%

profile of v2, /device:TPU:1, one launch (start us, length us, event | category | flops | bytes accessed | tf_op | source)
XLA Modules:
  0.0 117.9 jit_solution(11074136571407785178)
XLA Ops:
  0.6 0.0 copy-start.5
  0.6 0.8 copy-done.5
  1.4 0.0 copy-start.6
  1.4 0.7 copy-done.6
  2.1 2.4 %pack.1 = bf16[8,16,72,128]{3,2,1,0:T(8,128)(2,1)} custom-call(s32[64]{0:T(128)S(1)} %copy-done.6, s32[1]{0:T(128)} %bitcast.group_ref, bf16[2,16,576]{2,1,0:T(8,128)(2,1)S(1)} %copy-done.5), custom_call_target="tpu_custom_call" | custom-call | tf_op jit(solution)/shard_map/pack/pallas_call | solution.py:118
  4.4 11.9 %all-to-all-start = ((bf16[128,72,128]{2,1,0:T(8,128)(2,1)}), bf16[128,72,128]{2,1,0:T(8,128)(2,1)}, u32[]{:S(2)}, u32[]{:S(2)}) async-start(bf16[128,72,128]{2,1,0:T(8,128)(2,1)} %bitcast.1), calls=%async_computation | async-start | bytes 4718592 | tf_op jit(solution)/shard_map/all_to_all | solution.py:390
  16.3 0.0 copy-start.7
  16.4 0.0 copy-start.19
  16.4 0.0 copy-start.9
  16.4 1.8 %copy.23.own_ref = bf16[1024,576]{1,0:T(8,128)(2,1)S(1)} copy(bf16[1024,576]{0,1:T(8,128)(2,1)} %param.12) | data formatting | bytes 2359296 | tf_op args[4]
  18.2 0.0 copy-done.7
  18.2 0.1 and_select_fusion.2
  18.3 0.0 copy-done.19
  18.3 0.2 select_reduce_fusion.3.len_ref
  18.5 0.0 copy-done.9
  18.5 0.0 copy-start.8
  18.5 1.9 %copy-done.8 = bf16[1024,1536]{1,0:T(8,128)(2,1)S(1)} copy-done((bf16[1024,1536]{1,0:T(8,128)(2,1)S(1)}, bf16[1024,1536]{1,0:T(8,128)(2,1)}, u32[]{:S(2)}) %copy-start.8) | copy-done | bytes 3145752
  20.4 0.0 copy-start.10
  20.4 1.2 %copy-done.10 = bf16[8,128,512]{2,1,0:T(8,128)(2,1)S(1)} copy-done((bf16[8,128,512]{2,1,0:T(8,128)(2,1)S(1)}, bf16[8,128,512]{2,1,0:T(8,128)(2,1)}, u32[]{:S(2)}) %copy-start.10) | copy-done | bytes 1048600
  21.6 0.0 copy-start.11
  21.6 1.2 %copy-done.11 = bf16[8,512,128]{2,1,0:T(8,128)(2,1)S(1)} copy-done((bf16[8,512,128]{2,1,0:T(8,128)(2,1)S(1)}, bf16[8,512,128]{2,1,0:T(8,128)(2,1)}, u32[]{:S(2)}) %copy-start.11) | copy-done | bytes 1048600
  22.8 9.1 %lift_tokens.1 = (bf16[8,576,1024]{2,1,0:T(8,128)(2,1)S(1)}, bf16[8,512,1024]{2,1,0:T(8,128)(2,1)S(1)}) custom-call(bf16[1024,1536]{1,0:T(8,128)(2,1)S(1)} %copy-done.8, bf16[8,128,512]{2,1,0:T(8,128)(2,1)S(1)} %copy-done.10, bf16[1024,1024]{1,0:T(8,128)(2,1)S(1)} %copy-done.9, bf16[8,512,128]{2,1,0:T(8,128)(2,1)S(1)} %copy-done.11), custom_call_target="tpu_custom_call" | custom-call | flops 2147483648 | bytes 31457280 | tf_op jit(solution)/shard_map/lift_tokens/pallas_call | solution.py:63
  32.0 4.8 %own_scores.1 = (bf16[8,128,1024]{2,1,0:T(8,128)(2,1)S(1)}, f32[8,8,1024]{2,1,0:T(8,128)S(1)}) custom-call(bf16[1024,576]{1,0:T(8,128)(2,1)S(1)} %copy.23.own_ref, bf16[8,576,1024]{2,1,0:T(8,128)(2,1)S(1)} %get-tuple-element.9.fq_ref, bf16[8,512,1024]{2,1,0:T(8,128)(2,1)S(1)} %get-tuple-element.10.gl_ref), custom_call_target="tpu_custom_call" | custom-call | flops 2281701376 | bytes 23068672 | tf_op jit(solution)/shard_map/own_scores/pallas_call | solution.py:162
  36.8 0.0 copy-start
  36.8 3.6 %copy-done = bf16[8,576,1024]{2,1,0:T(8,128)(2,1)} copy-done((bf16[8,576,1024]{2,1,0:T(8,128)(2,1)}, bf16[8,576,1024]{2,1,0:T(8,128)(2,1)S(1)}, u32[]{:S(2)}) %copy-start) | copy-done | bytes 9437208
  40.4 0.0 copy-start.2
  40.4 3.3 %copy-done.2 = bf16[8,512,1024]{2,1,0:T(8,128)(2,1)} copy-done((bf16[8,512,1024]{2,1,0:T(8,128)(2,1)}, bf16[8,512,1024]{2,1,0:T(8,128)(2,1)S(1)}, u32[]{:S(2)}) %copy-start.2) | copy-done | bytes 8388632
  43.7 0.0 copy-start.13
  43.7 0.7 copy-done.13
  44.4 3.8 %all-to-all-done = bf16[128,72,128]{2,1,0:T(8,128)(2,1)} async-done(((bf16[128,72,128]{2,1,0:T(8,128)(2,1)}), bf16[128,72,128]{2,1,0:T(8,128)(2,1)}, u32[]{:S(2)}, u32[]{:S(2)}) %all-to-all-start) | async-done | bytes 2359328 | tf_op jit(solution)/shard_map/all_to_all | solution.py:390
  48.2 0.0 copy-start.1
  48.2 3.7 %copy-done.1 = bf16[8,576,1024]{2,1,0:T(8,128)(2,1)S(1)} copy-done((bf16[8,576,1024]{2,1,0:T(8,128)(2,1)S(1)}, bf16[8,576,1024]{2,1,0:T(8,128)(2,1)}, u32[]{:S(2)}) %copy-start.1) | copy-done | bytes 9437208
  51.9 0.0 copy-start.3
  51.9 3.4 %copy-done.3 = bf16[8,512,1024]{2,1,0:T(8,128)(2,1)S(1)} copy-done((bf16[8,512,1024]{2,1,0:T(8,128)(2,1)S(1)}, bf16[8,512,1024]{2,1,0:T(8,128)(2,1)}, u32[]{:S(2)}) %copy-start.3) | copy-done | bytes 8388632
  55.2 0.0 copy-start.14
  55.2 0.9 copy-done.14
  56.2 16.4 %attend.1 = (bf16[8,256,1024]{2,1,0:T(8,128)(2,1)S(1)}, f32[8,8,1024]{2,1,0:T(8,128)S(1)}, bf16[8,16,72,128]{3,2,1,0:T(8,128)(2,1)S(1)}) custom-call(s32[8]{0:T(128)S(1)} %get-tuple-element.20.slot_ref, s32[8]{0:T(128)S(1)} %select_reduce_fusion.3.len_ref, bf16[8,16,72,128]{3,2,1,0:T(8,128)(2,1)} %bitcast.2.latent_ref, f32[8,8,1024]{2,1,0:T(8,128)S(1)} %copy-done.14, ...), custom_call_target="tpu_custom_call" | custom-call | flops 9126805504 | bytes 31457280 | tf_op jit(solution)/shard_map/attend/pallas_call | solution.py:300
  72.6 0.0 copy-start.4
  72.6 1.4 %copy-done.4 = bf16[8,16,72,128]{3,2,1,0:T(8,128)(2,1)} copy-done((bf16[8,16,72,128]{3,2,1,0:T(8,128)(2,1)}, bf16[8,16,72,128]{3,2,1,0:T(8,128)(2,1)S(1)}, u32[]{:S(2)}) %copy-start.4) | copy-done | bytes 2359320
  74.0 0.0 copy-start.15
  74.0 1.9 %copy-done.15 = bf16[8,256,1024]{2,1,0:T(8,128)(2,1)} copy-done((bf16[8,256,1024]{2,1,0:T(8,128)(2,1)}, bf16[8,256,1024]{2,1,0:T(8,128)(2,1)S(1)}, u32[]{:S(2)}) %copy-start.15) | copy-done | bytes 4194328
  76.0 0.0 copy-start.17
  76.0 0.7 copy-done.17
  76.7 6.5 %all-to-all-start.1 = ((bf16[128,72,128]{2,1,0:T(8,128)(2,1)}), bf16[128,72,128]{2,1,0:T(8,128)(2,1)}, u32[]{:S(2)}, u32[]{:S(2)}) async-start(bf16[128,72,128]{2,1,0:T(8,128)(2,1)} %bitcast.20), calls=%async_computation.1 | async-start | bytes 4718592 | tf_op jit(solution)/shard_map/all_to_all | solution.py:402
  83.2 0.1 broadcast_in_dim.54
  83.3 0.1 eq.54
  83.4 0.1 select_reduce_fusion.2
  83.5 0.2 compare_reduce_fusion.1
  83.7 0.0 copy-start.12
  83.7 1.2 %copy-done.12 = bf16[8,512,128]{2,1,0:T(8,128)(2,1)S(1)} copy-done((bf16[8,512,128]{2,1,0:T(8,128)(2,1)S(1)}, bf16[8,512,128]{2,1,0:T(8,128)(2,1)}, u32[]{:S(2)}) %copy-start.12) | copy-done | bytes 1048600
  84.9 0.0 copy-start.16
  84.9 2.2 %copy-done.16 = bf16[8,256,1024]{2,1,0:T(8,128)(2,1)S(1)} copy-done((bf16[8,256,1024]{2,1,0:T(8,128)(2,1)S(1)}, bf16[8,256,1024]{2,1,0:T(8,128)(2,1)}, u32[]{:S(2)}) %copy-start.16) | copy-done | bytes 4194328
  87.1 0.0 copy-start.18
  87.1 0.9 copy-done.18
  88.0 18.7 %outputs.1 = bf16[1024,1024]{1,0:T(8,128)(2,1)} custom-call(s32[8]{0:T(128)S(1)} %get-tuple-element.20.slot_ref, bf16[8,16,72,128]{3,2,1,0:T(8,128)(2,1)} %bitcast.2.latent_ref, bf16[1024,576]{1,0:T(8,128)(2,1)S(1)} %copy.23.own_ref, bf16[8,256,1024]{2,1,0:T(8,128)(2,1)S(1)} %copy-done.16, bf16[8,128,1024]{2,1,0:T(8,128)(2,1)S(1)} %get-tuple-element.13.e_ref, ...), custom_call_target="tpu_custom_call" | custom-call | flops 4294967296 | bytes 16777216 | tf_op jit(solution)/shard_map/outputs/pallas_call | solution.py:356
  106.7 8.3 %all-to-all-done.1 = bf16[128,72,128]{2,1,0:T(8,128)(2,1)} async-done(((bf16[128,72,128]{2,1,0:T(8,128)(2,1)}), bf16[128,72,128]{2,1,0:T(8,128)(2,1)}, u32[]{:S(2)}, u32[]{:S(2)}) %all-to-all-start.1) | async-done | bytes 2359328 | tf_op jit(solution)/shard_map/all_to_all | solution.py:402
  115.0 2.0 %convert_reduce_fusion = f32[8,72,128]{2,1,0:T(8,128)S(1)} fusion(bf16[128,72,128]{2,1,0:T(8,128)(2,1)} %all-to-all-done.1), kind=kLoop, calls=%fused_computation | loop fusion | flops 2285568 | bytes 2654208 | tf_op jit(solution)/shard_map/reduce_sum | solution.py:410
  117.0 0.1 select_reduce_fusion.1
  117.2 0.1 reshape.69
  117.3 0.6 pad_maximum_fusion
  (5 shorter events, 0.0 us)
Async XLA Ops:
  0.6 0.8 copy-start.5
  1.4 0.7 copy-start.6
  4.4 43.7 %all-to-all-start = ((bf16[128,72,128]{2,1,0:T(8,128)(2,1)}), bf16[128,72,128]{2,1,0:T(8,128)(2,1)}, u32[]{:S(2)}, u32[]{:S(2)}) async-start(bf16[128,72,128]{2,1,0:T(8,128)(2,1)} %bitcast.1), calls=%async_computation | async-start | bytes 4718592 | tf_op jit(solution)/shard_map/all_to_all | solution.py:390
  16.3 1.9 %copy-start.7 = (s32[64]{0:T(128)S(1)}, s32[64]{0:T(128)}, u32[]{:S(2)}) copy-start(s32[64]{0:T(128)} %prompt_ref.1) | copy-start | bytes 772
  16.4 2.0 %copy-start.19 = (s32[16]{0:T(128)S(1)}, s32[16]{0:T(128)}, u32[]{:S(2)}) copy-start(s32[16]{0:T(128)} %param.15) | copy-start | bytes 196
  16.4 2.1 %copy-start.9 = (bf16[1024,1024]{1,0:T(8,128)(2,1)S(1)}, bf16[1024,1024]{1,0:T(8,128)(2,1)}, u32[]{:S(2)}) copy-start(bf16[1024,1024]{1,0:T(8,128)(2,1)} %go_ref.1) | copy-start | bytes 6291460
  18.5 1.9 %copy-start.8 = (bf16[1024,1536]{1,0:T(8,128)(2,1)S(1)}, bf16[1024,1536]{1,0:T(8,128)(2,1)}, u32[]{:S(2)}) copy-start(bf16[1024,1536]{1,0:T(8,128)(2,1)} %q_ref.1) | copy-start | bytes 9437188
  20.4 1.2 %copy-start.10 = (bf16[8,128,512]{2,1,0:T(8,128)(2,1)S(1)}, bf16[8,128,512]{2,1,0:T(8,128)(2,1)}, u32[]{:S(2)}) copy-start(bf16[8,128,512]{2,1,0:T(8,128)(2,1)} %uk_ref.1) | copy-start | bytes 3145732
  21.6 1.2 %copy-start.11 = (bf16[8,512,128]{2,1,0:T(8,128)(2,1)S(1)}, bf16[8,512,128]{2,1,0:T(8,128)(2,1)}, u32[]{:S(2)}) copy-start(bf16[8,512,128]{2,1,0:T(8,128)(2,1)} %uv_ref.3) | copy-start | bytes 3145732
  36.8 3.6 %copy-start = (bf16[8,576,1024]{2,1,0:T(8,128)(2,1)}, bf16[8,576,1024]{2,1,0:T(8,128)(2,1)S(1)}, u32[]{:S(2)}) copy-start(bf16[8,576,1024]{2,1,0:T(8,128)(2,1)S(1)} %get-tuple-element.9.fq_ref) | copy-start | bytes 28311556
  40.4 3.3 %copy-start.2 = (bf16[8,512,1024]{2,1,0:T(8,128)(2,1)}, bf16[8,512,1024]{2,1,0:T(8,128)(2,1)S(1)}, u32[]{:S(2)}) copy-start(bf16[8,512,1024]{2,1,0:T(8,128)(2,1)S(1)} %get-tuple-element.10.gl_ref) | copy-start | bytes 25165828
  43.7 0.7 copy-start.13
  48.2 3.7 %copy-start.1 = (bf16[8,576,1024]{2,1,0:T(8,128)(2,1)S(1)}, bf16[8,576,1024]{2,1,0:T(8,128)(2,1)}, u32[]{:S(2)}) copy-start(bf16[8,576,1024]{2,1,0:T(8,128)(2,1)} %copy-done) | copy-start | bytes 28311556
  51.9 3.4 %copy-start.3 = (bf16[8,512,1024]{2,1,0:T(8,128)(2,1)S(1)}, bf16[8,512,1024]{2,1,0:T(8,128)(2,1)}, u32[]{:S(2)}) copy-start(bf16[8,512,1024]{2,1,0:T(8,128)(2,1)} %copy-done.2) | copy-start | bytes 25165828
  55.2 0.9 copy-start.14
  72.6 1.4 %copy-start.4 = (bf16[8,16,72,128]{3,2,1,0:T(8,128)(2,1)}, bf16[8,16,72,128]{3,2,1,0:T(8,128)(2,1)S(1)}, u32[]{:S(2)}) copy-start(bf16[8,16,72,128]{3,2,1,0:T(8,128)(2,1)S(1)} %get-tuple-element.15) | copy-start | bytes 7077892
  74.0 1.9 %copy-start.15 = (bf16[8,256,1024]{2,1,0:T(8,128)(2,1)}, bf16[8,256,1024]{2,1,0:T(8,128)(2,1)S(1)}, u32[]{:S(2)}) copy-start(bf16[8,256,1024]{2,1,0:T(8,128)(2,1)S(1)} %get-tuple-element.12.aT_ref) | copy-start | bytes 12582916
  76.0 0.7 copy-start.17
  76.7 38.4 %all-to-all-start.1 = ((bf16[128,72,128]{2,1,0:T(8,128)(2,1)}), bf16[128,72,128]{2,1,0:T(8,128)(2,1)}, u32[]{:S(2)}, u32[]{:S(2)}) async-start(bf16[128,72,128]{2,1,0:T(8,128)(2,1)} %bitcast.20), calls=%async_computation.1 | async-start | bytes 4718592 | tf_op jit(solution)/shard_map/all_to_all | solution.py:402
  83.7 1.2 %copy-start.12 = (bf16[8,512,128]{2,1,0:T(8,128)(2,1)S(1)}, bf16[8,512,128]{2,1,0:T(8,128)(2,1)}, u32[]{:S(2)}) copy-start(bf16[8,512,128]{2,1,0:T(8,128)(2,1)} %uv_ref.3) | copy-start | bytes 3145732
  84.9 2.2 %copy-start.16 = (bf16[8,256,1024]{2,1,0:T(8,128)(2,1)S(1)}, bf16[8,256,1024]{2,1,0:T(8,128)(2,1)}, u32[]{:S(2)}) copy-start(bf16[8,256,1024]{2,1,0:T(8,128)(2,1)} %copy-done.15) | copy-start | bytes 12582916
  87.1 0.9 copy-start.18

commit v3 on v2

--- a/solution.py
+++ b/solution.py
@@ -11,6 +11,10 @@
 BF16 = jnp.bfloat16
 F32 = jnp.float32
 LOG2E = 1.4426950408889634
+
+
+def in_hbm(*arrays):
+    return [pltpu.with_memory_space_constraint(a, pltpu.HBM) for a in arrays]
 
 
 def dot_nn(a, b):
@@ -74,8 +78,8 @@
             pl.BlockSpec((resp_count, latent_width, 2 * rows), lambda i: (0, 0, i)),
         ],
         out_shape=[
-            jax.ShapeDtypeStruct((resp_count, channels, heads * rows), BF16),
-            jax.ShapeDtypeStruct((resp_count, latent_width, heads * rows), BF16),
+            pltpu.HBM((resp_count, channels, heads * rows), BF16),
+            pltpu.HBM((resp_count, latent_width, heads * rows), BF16),
         ],
         compiler_params=pltpu.CompilerParams(vmem_limit_bytes=14*1024*1024),
         cost_estimate=pl.CostEstimate(
@@ -84,7 +88,7 @@
             transcendentals=0,
         ),
         name="lift_tokens",
-    )(queries, up_key, grad_out, up_value)
+    )(*in_hbm(queries, up_key, grad_out, up_value))
 
 
 def pack_rows(rows):
@@ -128,7 +132,7 @@
         out_shape=jax.ShapeDtypeStruct((groups, slab_count, packed_rows, 128), BF16),
         compiler_params=pltpu.CompilerParams(vmem_limit_bytes=10 * 1024 * 1024),
         name="pack",
-    )(response_prompt, my_group, prompt_latent)
+    )(response_prompt, my_group, *in_hbm(prompt_latent))
 
 
 def own_kernel(head_width, own_ref, fq_ref, gl_ref, e_ref, stat_ref):
@@ -172,8 +176,8 @@
             pl.BlockSpec((1, 8, columns), lambda j: (j, 0, 0)),
         ],
         out_shape=[
-            jax.ShapeDtypeStruct((resp_count, rows, columns), BF16),
-            jax.ShapeDtypeStruct((resp_count, 8, columns), F32),
+            pltpu.HBM((resp_count, rows, columns), BF16),
+            pltpu.HBM((resp_count, 8, columns), F32),
         ],
         compiler_params=pltpu.CompilerParams(vmem_limit_bytes=10*1024*1024),
         cost_estimate=pl.CostEstimate(
@@ -182,7 +186,7 @@
             transcendentals=resp_count * columns * rows,
         ),
         name="own_scores",
-    )(resp_latent, full_t, grad_t)
+    )(*in_hbm(resp_latent, full_t, grad_t))
 
 
 def unpack_latent(packed_ref, slab):
@@ -301,9 +305,9 @@
         functools.partial(attend_kernel, head_width),
         grid_spec=grid_spec,
         out_shape=[
-            jax.ShapeDtypeStruct((resp_count, key_span, columns), BF16),
-            jax.ShapeDtypeStruct((resp_count, 8, columns), F32),
-            jax.ShapeDtypeStruct((groups, slabs, packed_rows, lanes), BF16),
+            pltpu.HBM((resp_count, key_span, columns), BF16),
+            pltpu.HBM((resp_count, 8, columns), F32),
+            pltpu.HBM((groups, slabs, packed_rows, lanes), BF16),
         ],
         compiler_params=pltpu.CompilerParams(vmem_limit_bytes=20*1024*1024),
         cost_estimate=pl.CostEstimate(
@@ -312,7 +316,7 @@
             transcendentals=resp_count * columns * key_span,
         ),
         name="attend",
-    )(slots, lengths, gathered, stats, full_t, grad_t)
+    )(slots, lengths, *in_hbm(gathered, stats, full_t, grad_t))
 
 
 def output_kernel(slot_ref, latent_ref, own_ref, aT_ref, e_ref, ratio_ref, uv_ref, out_ref):
@@ -364,7 +368,10 @@
             transcendentals=0,
         ),
         name="outputs",
-    )(slots, gathered, resp_latent, attention_t, own_weights, ratio, up_value)
+    )(
+        slots,
+        *in_hbm(gathered, resp_latent, attention_t, own_weights, ratio, up_value),
+    )
 
 
 def on_device(

time: 119 us -> 108 us (0.908)
  local copies, waits for them, and re-layouts: 31.9 us -> 3.83 us
  Pallas kernels: 51.3 us -> 64.8 us
  waiting for transfers between devices: 12.1 us -> 19.4 us
  starting transfers between devices: 18.4 us -> 16.6 us
  other arithmetic: 3.35 us -> 1.65 us
    unnamed x41 -> x11, local copies, waits for them, and re-layouts: 31.7 us -> 3.58 us
    pallas_call x1, Pallas kernels: 4.75 us -> 11.2 us  [own_scores(): pl.pallas_call(functools.partial(own_kernel, head_width), grid=(resp_coun...]
    all_to_all x1, waiting for transfers between devices: 3.79 us -> 7.45 us  [on_device(): lax.all_to_all(copies, ('resp', 'head'), split_axis=0, concat_axis=0, til...]
    all_to_all x1, waiting for transfers between devices: 8.35 us -> 12 us  [on_device(): lax.all_to_all(pieces.reshape(groups * slab_count, -1, 128), ('resp', 'he...]
    pallas_call x1, Pallas kernels: 16.4 us -> 19.2 us  [attend(): pl.pallas_call(functools.partial(attend_kernel, head_width), grid_spec=gr...]
    pallas_call x1, Pallas kernels: 9.14 us -> 11.7 us  [lift_tokens(): pl.pallas_call(up_kernel, grid=(heads // 2,), in_specs=[pl.BlockSpec((tok...]
    reduce_sum x1, other arithmetic: 2 us -> 0.31 us  [on_device(): jnp.sum(returned_grad.reshape(groups, slab_count, -1, 128).astype(F32), a...]
    all_to_all x1, starting transfers between devices: 6.51 us -> 5.08 us  [on_device(): lax.all_to_all(pieces.reshape(groups * slab_count, -1, 128), ('resp', 'he...]
  transfers between devices with their start and end apart: 2 -> 2, of which waited for: 2 -> 2; matrix products, arithmetic and copies ran while one was open for 2% -> 2% of each run, Pallas kernels for 28% -> 40%
where the time goes in v3:
time: 108 us; the launch traced here: 107 us
  Pallas kernels  64.8 us (60%)
  waiting for transfers between devices  19.4 us (18%)
  starting transfers between devices  16.6 us (15%)
  local copies, waits for them, and re-layouts  3.83 us (4%)
  other arithmetic  1.65 us (2%)
    pallas_call x1, Pallas kernels, outputs(): pl.pallas_call(output_kernel, grid_spec=grid_spec, out_shape=jax.ShapeDty...  19.7 us
    pallas_call x1, Pallas kernels, attend(): pl.pallas_call(functools.partial(attend_kernel, head_width), grid_spec=gr...  19.2 us
    all_to_all x1, waiting for transfers between devices, on_device(): lax.all_to_all(pieces.reshape(groups * slab_count, -1, 128), ('resp', 'he...  12 us
    pallas_call x1, Pallas kernels, lift_tokens(): pl.pallas_call(up_kernel, grid=(heads // 2,), in_specs=[pl.BlockSpec((tok...  11.7 us
    all_to_all x1, starting transfers between devices, on_device(): lax.all_to_all(copies, ('resp', 'head'), split_axis=0, concat_axis=0, til...  11.5 us
    pallas_call x1, Pallas kernels, own_scores(): pl.pallas_call(functools.partial(own_kernel, head_width), grid=(resp_coun...  11.2 us
    all_to_all x1, waiting for transfers between devices, on_device(): lax.all_to_all(copies, ('resp', 'head'), split_axis=0, concat_axis=0, til...  7.45 us
    all_to_all x1, starting transfers between devices, on_device(): lax.all_to_all(pieces.reshape(groups * slab_count, -1, 128), ('resp', 'he...  5.08 us
  transfers between devices with their start and end apart: 2, of which 2 were waited for; matrix products, arithmetic and copies ran while one was open for 2% of the time, Pallas kernels for 40%

profile of v3, /device:TPU:1, one launch (start us, length us, event | category | flops | bytes accessed | tf_op | source)
XLA Modules:
  0.0 107.1 jit_solution(4899944596724481114)
XLA Ops:
  0.6 0.0 copy-start
  0.6 0.6 copy-done
  1.3 3.1 %pack.1 = bf16[8,16,72,128]{3,2,1,0:T(8,128)(2,1)} custom-call(s32[64]{0:T(128)S(1)} %copy-done, s32[1]{0:T(128)} %bitcast.group_ref, bf16[2,16,576]{2,1,0:T(8,128)(2,1)} %latent_ref.1), custom_call_target="tpu_custom_call" | custom-call | tf_op jit(solution)/shard_map/pack/pallas_call | solution.py:122
  4.4 0.0 copy-start.3
  4.4 11.5 %all-to-all-start = ((bf16[128,72,128]{2,1,0:T(8,128)(2,1)}), bf16[128,72,128]{2,1,0:T(8,128)(2,1)S(1)}, u32[]{:S(2)}, u32[]{:S(2)}) async-start(bf16[128,72,128]{2,1,0:T(8,128)(2,1)} %bitcast.1), calls=%async_computation | async-start | bytes 4718592 | tf_op jit(solution)/shard_map/all_to_all | solution.py:397
  15.9 0.0 copy-start.1
  15.9 0.0 copy-start.4
  15.9 0.0 copy-done.3
  15.9 1.5 %copy.23.own_ref = bf16[1024,576]{1,0:T(8,128)(2,1)} copy(bf16[1024,576]{0,1:T(8,128)(2,1)S(1)} %copy-done.3) | data formatting | bytes 2359296 | tf_op args[4]
  17.4 0.0 copy-done.1
  17.4 0.1 and_select_fusion.2
  17.5 0.0 copy-done.4
  17.5 0.2 select_reduce_fusion.3.len_ref
  17.7 11.7 %lift_tokens.1 = (bf16[8,576,1024]{2,1,0:T(8,128)(2,1)}, bf16[8,512,1024]{2,1,0:T(8,128)(2,1)}) custom-call(bf16[1024,1536]{1,0:T(8,128)(2,1)} %q_ref.1, bf16[8,128,512]{2,1,0:T(8,128)(2,1)} %uk_ref.1, bf16[1024,1024]{1,0:T(8,128)(2,1)} %go_ref.1, bf16[8,512,128]{2,1,0:T(8,128)(2,1)} %uv_ref.3), custom_call_target="tpu_custom_call" | custom-call | flops 2147483648 | bytes 31457280 | tf_op jit(solution)/shard_map/lift_tokens/pallas_call | solution.py:67
  29.4 11.2 %own_scores.1 = (bf16[8,128,1024]{2,1,0:T(8,128)(2,1)}, f32[8,8,1024]{2,1,0:T(8,128)}) custom-call(bf16[1024,576]{1,0:T(8,128)(2,1)} %copy.23.own_ref, bf16[8,576,1024]{2,1,0:T(8,128)(2,1)} %get-tuple-element.9.fq_ref, bf16[8,512,1024]{2,1,0:T(8,128)(2,1)} %get-tuple-element.10.gl_ref), custom_call_target="tpu_custom_call" | custom-call | flops 2281701376 | bytes 23068672 | tf_op jit(solution)/shard_map/own_scores/pallas_call | solution.py:166
  40.6 7.4 %all-to-all-done = bf16[128,72,128]{2,1,0:T(8,128)(2,1)S(1)} async-done(((bf16[128,72,128]{2,1,0:T(8,128)(2,1)}), bf16[128,72,128]{2,1,0:T(8,128)(2,1)S(1)}, u32[]{:S(2)}, u32[]{:S(2)}) %all-to-all-start) | async-done | bytes 2359328 | tf_op jit(solution)/shard_map/all_to_all | solution.py:397
  48.0 0.0 copy-start.2
  48.0 1.4 %copy-done.2 = bf16[128,72,128]{2,1,0:T(8,128)(2,1)} copy-done((bf16[128,72,128]{2,1,0:T(8,128)(2,1)}, bf16[128,72,128]{2,1,0:T(8,128)(2,1)S(1)}, u32[]{:S(2)}) %copy-start.2) | copy-done | bytes 2359320
  49.5 19.2 %attend.1 = (bf16[8,256,1024]{2,1,0:T(8,128)(2,1)}, f32[8,8,1024]{2,1,0:T(8,128)}, bf16[8,16,72,128]{3,2,1,0:T(8,128)(2,1)}) custom-call(s32[8]{0:T(128)S(1)} %get-tuple-element.20.slot_ref, s32[8]{0:T(128)S(1)} %select_reduce_fusion.3.len_ref, bf16[8,16,72,128]{3,2,1,0:T(8,128)(2,1)} %bitcast.20, f32[8,8,1024]{2,1,0:T(8,128)} %get-tuple-element.11.stat_ref, ...), custom_call_target="tpu_custom_call" | custom-call | flops 9126805504 | bytes 31457280 | tf_op jit(solution)/shard_map/attend/pallas_call | solution.py:304
  68.6 5.1 %all-to-all-start.1 = ((bf16[128,72,128]{2,1,0:T(8,128)(2,1)}), bf16[128,72,128]{2,1,0:T(8,128)(2,1)S(1)}, u32[]{:S(2)}, u32[]{:S(2)}) async-start(bf16[128,72,128]{2,1,0:T(8,128)(2,1)} %bitcast.22), calls=%async_computation.1 | async-start | bytes 4718592 | tf_op jit(solution)/shard_map/all_to_all | solution.py:409
  73.7 0.1 broadcast_in_dim.54
  73.8 0.1 eq.54
  73.9 0.1 select_reduce_fusion.2
  74.0 0.2 compare_reduce_fusion.1
  74.2 19.7 %outputs.1 = bf16[1024,1024]{1,0:T(8,128)(2,1)} custom-call(s32[8]{0:T(128)S(1)} %get-tuple-element.20.slot_ref, bf16[8,16,72,128]{3,2,1,0:T(8,128)(2,1)} %bitcast.21, bf16[1024,576]{1,0:T(8,128)(2,1)} %copy.23.own_ref, bf16[8,256,1024]{2,1,0:T(8,128)(2,1)} %get-tuple-element.12.aT_ref, bf16[8,128,1024]{2,1,0:T(8,128)(2,1)} %get-tuple-element.13.e_ref, ...), custom_call_target="tpu_custom_call" | custom-call | flops 4294967296 | bytes 16777216 | tf_op jit(solution)/shard_map/outputs/pallas_call | solution.py:360
  93.9 12.0 %all-to-all-done.1 = bf16[128,72,128]{2,1,0:T(8,128)(2,1)S(1)} async-done(((bf16[128,72,128]{2,1,0:T(8,128)(2,1)}), bf16[128,72,128]{2,1,0:T(8,128)(2,1)S(1)}, u32[]{:S(2)}, u32[]{:S(2)}) %all-to-all-start.1) | async-done | bytes 2359328 | tf_op jit(solution)/shard_map/all_to_all | solution.py:409
  105.9 0.3 convert_reduce_fusion
  106.2 0.1 select_reduce_fusion.1
  106.3 0.1 reshape.69
  106.4 0.6 pad_maximum_fusion
  (5 shorter events, 0.0 us)
Async XLA Ops:
  0.6 0.7 copy-start
  4.4 11.5 %copy-start.3 = (bf16[1024,576]{0,1:T(8,128)(2,1)S(1)}, bf16[1024,576]{0,1:T(8,128)(2,1)}, u32[]{:S(2)}) copy-start(bf16[1024,576]{0,1:T(8,128)(2,1)} %param.12) | copy-start | bytes 3538948
  4.4 43.6 %all-to-all-start = ((bf16[128,72,128]{2,1,0:T(8,128)(2,1)}), bf16[128,72,128]{2,1,0:T(8,128)(2,1)S(1)}, u32[]{:S(2)}, u32[]{:S(2)}) async-start(bf16[128,72,128]{2,1,0:T(8,128)(2,1)} %bitcast.1), calls=%async_computation | async-start | bytes 4718592 | tf_op jit(solution)/shard_map/all_to_all | solution.py:397
  15.9 1.5 %copy-start.1 = (s32[64]{0:T(128)S(1)}, s32[64]{0:T(128)}, u32[]{:S(2)}) copy-start(s32[64]{0:T(128)} %prompt_ref.1) | copy-start | bytes 772
  15.9 1.6 %copy-start.4 = (s32[16]{0:T(128)S(1)}, s32[16]{0:T(128)}, u32[]{:S(2)}) copy-start(s32[16]{0:T(128)} %param.15) | copy-start | bytes 196
  48.0 1.4 %copy-start.2 = (bf16[128,72,128]{2,1,0:T(8,128)(2,1)}, bf16[128,72,128]{2,1,0:T(8,128)(2,1)S(1)}, u32[]{:S(2)}) copy-start(bf16[128,72,128]{2,1,0:T(8,128)(2,1)S(1)} %all-to-all-done) | copy-start | bytes 7077892
  68.6 37.2 %all-to-all-start.1 = ((bf16[128,72,128]{2,1,0:T(8,128)(2,1)}), bf16[128,72,128]{2,1,0:T(8,128)(2,1)S(1)}, u32[]{:S(2)}, u32[]{:S(2)}) async-start(bf16[128,72,128]{2,1,0:T(8,128)(2,1)} %bitcast.22), calls=%async_computation.1 | async-start | bytes 4718592 | tf_op jit(solution)/shard_map/all_to_all | solution.py:409

commit v4 on v3

--- a/solution.py
+++ b/solution.py
@@ -99,40 +99,44 @@
     return jnp.concatenate([rows[:, 128 * c : 128 * (c + 1)] for c in range(blocks)] + [tail], axis=0)
 
 
-def pack_kernel(prompt_ref, group_ref, latent_ref, out_ref):
+def pack_kernel(axis, prompt_any, latent_any, out_ref, prompt_ref, latent_ref, sem):
+    copies = [
+        pltpu.make_async_copy(prompt_any, prompt_ref, sem.at[0]),
+        pltpu.make_async_copy(latent_any, latent_ref, sem.at[1]),
+    ]
+    for copy in copies:
+        copy.start()
+    for copy in copies:
+        copy.wait()
     groups, slab_count, packed_rows, lanes = out_ref.shape
     owned = latent_ref.shape[0]
     resp_count = prompt_ref.shape[0] // groups
-    packed = [pack_rows(latent_ref[p].astype(F32)) for p in range(owned)]
+    first = lax.axis_index(axis) * owned
+    packed = [pack_rows(latent_ref[p].astype(F32)).astype(BF16) for p in range(owned)]
     for r in range(groups):
-        wanted = jnp.int32(-1)
-        for i in range(resp_count):
-            prompt = prompt_ref[r * resp_count + i]
-            wanted = jnp.where(prompt // owned == group_ref[0], prompt % owned, wanted)
         chosen = packed[0]
         for p in range(1, owned):
-            chosen = jnp.where(wanted == p, packed[p], chosen)
-        chosen = chosen.astype(BF16)
+            hits = [prompt_ref[r * resp_count + i] == first + p for i in range(resp_count)]
+            chosen = jnp.where(functools.reduce(jnp.logical_or, hits), packed[p], chosen)
         out_ref[r] = jnp.broadcast_to(chosen[None], (slab_count, packed_rows, lanes))
 
 
-def pack(response_prompt, my_group, prompt_latent, groups, slab_count):
+def pack(response_prompt, prompt_latent, groups, slab_count):
     owned, slab_rows, channels = prompt_latent.shape
     packed_rows = slab_rows * channels // 128
     return pl.pallas_call(
-        pack_kernel,
-        grid_spec=pltpu.PrefetchScalarGridSpec(
-            num_scalar_prefetch=2,
-            grid=(1,),
-            in_specs=[pl.BlockSpec((owned, slab_rows, channels), lambda i, p, g: (0, 0, 0))],
-            out_specs=pl.BlockSpec(
-                (groups, slab_count, packed_rows, 128), lambda i, p, g: (0, 0, 0, 0)
-            ),
-        ),
-        out_shape=jax.ShapeDtypeStruct((groups, slab_count, packed_rows, 128), BF16),
+        functools.partial(pack_kernel, "resp"),
+        in_specs=[pl.BlockSpec(memory_space=pl.ANY)] * 2,
+        out_specs=pl.BlockSpec(memory_space=pltpu.VMEM),
+        scratch_shapes=[
+            pltpu.SMEM(response_prompt.shape, response_prompt.dtype),
+            pltpu.VMEM(prompt_latent.shape, BF16),
+            pltpu.SemaphoreType.DMA((2,)),
+        ],
+        out_shape=pltpu.VMEM((groups, slab_count, packed_rows, 128), BF16),
         compiler_params=pltpu.CompilerParams(vmem_limit_bytes=10 * 1024 * 1024),
         name="pack",
-    )(response_prompt, my_group, *in_hbm(prompt_latent))
+    )(*in_hbm(response_prompt, prompt_latent))
 
 
 def own_kernel(head_width, own_ref, fq_ref, gl_ref, e_ref, stat_ref):
@@ -221,12 +225,12 @@
     gl_ref,
     aT_ref,
     ratio_ref,
+    value_ref,
     piece_ref,
     acc_ref,
     gs_ref,
 ):
     j = pl.program_id(0)
-    steps = pl.num_programs(0)
     channels = fq_ref.shape[1]
     latent_width = gl_ref.shape[1]
     columns = fq_ref.shape[2]
@@ -237,12 +241,13 @@
     scaling = 1.0 / math.sqrt(head_width)
     chunk = 256
 
-    @pl.when(j == 0)
-    def _():
-        acc_ref[...] = jnp.zeros_like(acc_ref)
-
+    slot = slot_ref[j]
     length = len_ref[j]
+    seen = jnp.int32(0)
+    for k in range(slot_ref.shape[0]):
+        seen = jnp.where((k < j) & (slot_ref[k] == slot), 1, seen)
     values = unpack_latent(latent_ref, slab)
+    value_ref[0] = values
     keys = jnp.concatenate([values, unpack_rope(latent_ref, slab)], axis=1)
     row = lax.broadcasted_iota(jnp.int32, (key_span, chunk), 0)
     allowed = row < length
@@ -265,16 +270,15 @@
         ratio_ref[0, pl.ds(0, 1), at] = shift * inverse
     combined = dot_nt(gs_ref[...], fq_ref[0])
     value_term = dot_nt(aT_ref[0], gl_ref[0])
-    slot = slot_ref[j]
-    acc_ref[slot, :, pl.ds(0, latent_width)] += combined[:, :latent_width] + value_term
-    acc_ref[slot, :, pl.ds(latent_width, rope)] += combined[:, latent_width:]
-
-    @pl.when(j == steps - 1)
-    def _():
-        for g in range(groups):
-            for h in range(slabs):
-                rows = acc_ref[g, pl.ds(h * slab, slab), :]
-                piece_ref[g, h] = pack_rows(rows).astype(BF16)
+    latent_part = combined[:, :latent_width] + value_term
+    rope_part = combined[:, latent_width:]
+    earlier = acc_ref[slot]
+    latent_part += jnp.where(seen == 1, earlier[:, :latent_width], 0.0)
+    rope_part += jnp.where(seen == 1, earlier[:, latent_width:], 0.0)
+    acc_ref[slot, :, pl.ds(0, latent_width)] = latent_part
+    acc_ref[slot, :, pl.ds(latent_width, rope)] = rope_part
+    for h in range(slabs):
+        piece_ref[0, h] = pack_rows(acc_ref[slot, pl.ds(h * slab, slab), :]).astype(BF16)
 
 
 def attend(slots, lengths, gathered, stats, full_t, grad_t, head_width):
@@ -294,7 +298,8 @@
         out_specs=[
             pl.BlockSpec((1, key_span, columns), lambda j, s, n: (j, 0, 0)),
             pl.BlockSpec((1, 8, columns), lambda j, s, n: (j, 0, 0)),
-            pl.BlockSpec((groups, slabs, packed_rows, lanes), lambda j, s, n: (0, 0, 0, 0)),
+            pl.BlockSpec((1, key_span, latent_width), lambda j, s, n: (j, 0, 0)),
+            pl.BlockSpec((1, slabs, packed_rows, lanes), lambda j, s, n: (s[j], 0, 0, 0)),
         ],
         scratch_shapes=[
             pltpu.VMEM((groups, key_span, channels), F32),
@@ -307,6 +312,7 @@
         out_shape=[
             pltpu.HBM((resp_count, key_span, columns), BF16),
             pltpu.HBM((resp_count, 8, columns), F32),
+            pltpu.HBM((resp_count, key_span, latent_width), BF16),
             pltpu.HBM((groups, slabs, packed_rows, lanes), BF16),
         ],
         compiler_params=pltpu.CompilerParams(vmem_limit_bytes=20*1024*1024),
@@ -316,15 +322,14 @@
             transcendentals=resp_count * columns * key_span,
         ),
         name="attend",
-    )(slots, lengths, *in_hbm(gathered, stats, full_t, grad_t))
-
-
-def output_kernel(slot_ref, latent_ref, own_ref, aT_ref, e_ref, ratio_ref, uv_ref, out_ref):
+    )(slots, lengths, gathered, *in_hbm(stats, full_t, grad_t))
+
+
+def output_kernel(latent_ref, own_ref, aT_ref, e_ref, ratio_ref, uv_ref, out_ref):
     rows = own_ref.shape[0]
     heads, latent_width, value_width = uv_ref.shape
-    slab = aT_ref.shape[1] // latent_ref.shape[1]
     values = jnp.concatenate(
-        [unpack_latent(latent_ref, slab), own_ref[:, pl.ds(0, latent_width)]], axis=0
+        [latent_ref[0], own_ref[:, pl.ds(0, latent_width)]], axis=0
     )
     values_t = values.T
     for i in range(0, heads, 2):
@@ -338,28 +343,23 @@
             out_ref[:, pl.ds((i + e) * value_width, value_width)] = done.astype(BF16)
 
 
-def outputs(slots, gathered, resp_latent, attention_t, own_weights, ratio, up_value):
-    groups, slabs, packed_rows, lanes = gathered.shape
+def outputs(prompt_values, resp_latent, attention_t, own_weights, ratio, up_value):
     resp_count, key_span, columns = attention_t.shape
     channels = resp_latent.shape[1]
     heads, latent_width, value_width = up_value.shape
     rows = resp_latent.shape[0] // resp_count
-    grid_spec = pltpu.PrefetchScalarGridSpec(
-        num_scalar_prefetch=1,
+    return pl.pallas_call(
+        output_kernel,
         grid=(resp_count,),
         in_specs=[
-            pl.BlockSpec((1, slabs, packed_rows, lanes), lambda j, s: (s[j], 0, 0, 0)),
-            pl.BlockSpec((rows, channels), lambda j, s: (j, 0)),
-            pl.BlockSpec((1, key_span, columns), lambda j, s: (j, 0, 0)),
-            pl.BlockSpec((1, rows, columns), lambda j, s: (j, 0, 0)),
-            pl.BlockSpec((1, 8, columns), lambda j, s: (j, 0, 0)),
-            pl.BlockSpec((heads, latent_width, value_width), lambda j, s: (0, 0, 0)),
-        ],
-        out_specs=pl.BlockSpec((rows, heads * value_width), lambda j, s: (j, 0)),
-    )
-    return pl.pallas_call(
-        output_kernel,
-        grid_spec=grid_spec,
+            pl.BlockSpec((1, key_span, latent_width), lambda j: (j, 0, 0)),
+            pl.BlockSpec((rows, channels), lambda j: (j, 0)),
+            pl.BlockSpec((1, key_span, columns), lambda j: (j, 0, 0)),
+            pl.BlockSpec((1, rows, columns), lambda j: (j, 0, 0)),
+            pl.BlockSpec((1, 8, columns), lambda j: (j, 0, 0)),
+            pl.BlockSpec((heads, latent_width, value_width), lambda j: (0, 0, 0)),
+        ],
+        out_specs=pl.BlockSpec((rows, heads * value_width), lambda j: (j, 0)),
         out_shape=jax.ShapeDtypeStruct((resp_count * rows, heads * value_width), BF16),
         compiler_params=pltpu.CompilerParams(vmem_limit_bytes=12*1024*1024),
         cost_estimate=pl.CostEstimate(
@@ -368,10 +368,7 @@
             transcendentals=0,
         ),
         name="outputs",
-    )(
-        slots,
-        *in_hbm(gathered, resp_latent, attention_t, own_weights, ratio, up_value),
-    )
+    )(*in_hbm(prompt_values, resp_latent, attention_t, own_weights, ratio, up_value))
 
 
 def on_device(
@@ -391,9 +388,8 @@
         axis=1,
     )
     wanted_mine = lax.dynamic_index_in_dim(wanted, my_group, 1, False)
-    copies = pack(
-        response_prompt, jnp.reshape(my_group, (1,)), prompt_latent, groups, slab_count
-    ).reshape(groups * slab_count, -1, 128)
+    copies = pack(response_prompt, prompt_latent, groups, slab_count)
+    copies = copies.reshape(groups * slab_count, -1, 128)
     arrived = lax.all_to_all(copies, ("resp", "head"), split_axis=0, concat_axis=0, tiled=True)
     gathered = arrived.reshape(groups, slab_count, -1, 128)
     local_prompt = lax.dynamic_slice_in_dim(response_prompt, my_group * resp_count, resp_count)
@@ -403,7 +399,7 @@
     head_width = queries.shape[1] // up_key.shape[0]
     full_t, grad_t = lift_tokens(queries, up_key, grad_out, up_value, resp_count)
     own_weights, stats = own_scores(resp_latent, full_t, grad_t, head_width)
-    attention_t, ratio, pieces = attend(
+    attention_t, ratio, prompt_values, pieces = attend(
         slots, lengths, gathered, stats, full_t, grad_t, head_width
     )
     returned_grad = lax.all_to_all(
@@ -413,7 +409,7 @@
         concat_axis=0,
         tiled=True,
     )
-    attn_out = outputs(slots, gathered, resp_latent, attention_t, own_weights, ratio, up_value)
+    attn_out = outputs(prompt_values, resp_latent, attention_t, own_weights, ratio, up_value)
     summed = jnp.sum(returned_grad.reshape(groups, slab_count, -1, 128).astype(F32), axis=1)
     packed = jnp.stack(
         [

time: 108 us -> 103 us (0.954)
  Pallas kernels: 64.8 us -> 61.9 us
  local copies, waits for them, and re-layouts: 3.83 us -> 1.73 us
    unnamed x11 -> x7, local copies, waits for them, and re-layouts: 3.58 us -> 1.48 us
    pallas_call x1, Pallas kernels: 19.2 us -> 17.4 us  [attend(): pl.pallas_call(functools.partial(attend_kernel, head_width), grid_spec=gr...]
    pallas_call x2, Pallas kernels: 22.8 us -> 21.6 us  [the longest x1 19.1 us: outputs(): pl.pallas_call(output_kernel, grid=(resp_count,), in_specs=[pl.BlockSpec(...]
  transfers between devices with their start and end apart: 2 -> 2, of which waited for: 2 -> 2; matrix products, arithmetic and copies ran while one was open for 2% -> 2% of each run, Pallas kernels for 40% -> 41%
where the time goes in v4:
time: 103 us
  Pallas kernels  61.9 us (60%)
  waiting for transfers between devices  20 us (19%)
  starting transfers between devices  16.6 us (16%)
  local copies, waits for them, and re-layouts  1.73 us (2%)
  other arithmetic  1.65 us (2%)
    pallas_call x1, Pallas kernels, outputs(): pl.pallas_call(output_kernel, grid=(resp_count,), in_specs=[pl.BlockSpec(...  19.1 us
    pallas_call x1, Pallas kernels, attend(): pl.pallas_call(functools.partial(attend_kernel, head_width), grid_spec=gr...  17.4 us
    all_to_all x1, waiting for transfers between devices, on_device(): lax.all_to_all(pieces.reshape(groups * slab_count, -1, 128), ('resp', 'he...  12.6 us
    pallas_call x1, Pallas kernels, lift_tokens(): pl.pallas_call(up_kernel, grid=(heads // 2,), in_specs=[pl.BlockSpec((tok...  11.7 us
    all_to_all x1, starting transfers between devices, on_device(): lax.all_to_all(copies, ('resp', 'head'), split_axis=0, concat_axis=0, til...  11.5 us
    pallas_call x1, Pallas kernels, own_scores(): pl.pallas_call(functools.partial(own_kernel, head_width), grid=(resp_coun...  11.2 us
    all_to_all x1, waiting for transfers between devices, on_device(): lax.all_to_all(copies, ('resp', 'head'), split_axis=0, concat_axis=0, til...  7.44 us
    all_to_all x1, starting transfers between devices, on_device(): lax.all_to_all(pieces.reshape(groups * slab_count, -1, 128), ('resp', 'he...  5.1 us
  transfers between devices with their start and end apart: 2, of which 2 were waited for; matrix products, arithmetic and copies ran while one was open for 2% of the time, Pallas kernels for 41%

profile of v4, /device:TPU:1, one launch (start us, length us, event | category | flops | bytes accessed | tf_op | source)
XLA Modules:
  0.0 102.6 jit_solution(6751186790939381822)
XLA Ops:
  0.6 2.5 %pack.1 = bf16[8,16,72,128]{3,2,1,0:T(8,128)(2,1)} custom-call(s32[64]{0:T(128)} %prompt_any.1, bf16[2,16,576]{2,1,0:T(8,128)(2,1)} %latent_any.1), custom_call_target="tpu_custom_call" | custom-call | tf_op jit(solution)/shard_map/pack/pallas_call | solution.py:127
  3.1 0.0 copy-start
  3.2 11.5 %all-to-all-start = ((bf16[128,72,128]{2,1,0:T(8,128)(2,1)}), bf16[128,72,128]{2,1,0:T(8,128)(2,1)S(1)}, u32[]{:S(2)}, u32[]{:S(2)}) async-start(bf16[128,72,128]{2,1,0:T(8,128)(2,1)} %bitcast), calls=%async_computation | async-start | bytes 4718592 | tf_op jit(solution)/shard_map/all_to_all | solution.py:393
  14.7 0.0 copy-start.1
  14.7 0.0 copy-start.2
  14.7 0.0 copy-done
  14.7 1.5 %copy.22.own_ref = bf16[1024,576]{1,0:T(8,128)(2,1)} copy(bf16[1024,576]{0,1:T(8,128)(2,1)S(1)} %copy-done) | data formatting | bytes 2359296 | tf_op args[4]
  16.2 0.0 copy-done.1
  16.2 0.1 and_select_fusion.2
  16.3 0.0 copy-done.2
  16.3 0.2 select_reduce_fusion.3.len_ref
  16.4 11.7 %lift_tokens.1 = (bf16[8,576,1024]{2,1,0:T(8,128)(2,1)}, bf16[8,512,1024]{2,1,0:T(8,128)(2,1)}) custom-call(bf16[1024,1536]{1,0:T(8,128)(2,1)} %q_ref.1, bf16[8,128,512]{2,1,0:T(8,128)(2,1)} %uk_ref.1, bf16[1024,1024]{1,0:T(8,128)(2,1)} %go_ref.1, bf16[8,512,128]{2,1,0:T(8,128)(2,1)} %uv_ref.3), custom_call_target="tpu_custom_call" | custom-call | flops 2147483648 | bytes 31457280 | tf_op jit(solution)/shard_map/lift_tokens/pallas_call | solution.py:67
  28.2 11.2 %own_scores.1 = (bf16[8,128,1024]{2,1,0:T(8,128)(2,1)}, f32[8,8,1024]{2,1,0:T(8,128)}) custom-call(bf16[1024,576]{1,0:T(8,128)(2,1)} %copy.22.own_ref, bf16[8,576,1024]{2,1,0:T(8,128)(2,1)} %get-tuple-element.10.fq_ref, bf16[8,512,1024]{2,1,0:T(8,128)(2,1)} %get-tuple-element.11.gl_ref), custom_call_target="tpu_custom_call" | custom-call | flops 2281701376 | bytes 23068672 | tf_op jit(solution)/shard_map/own_scores/pallas_call | solution.py:170
  39.4 7.4 %all-to-all-done = bf16[128,72,128]{2,1,0:T(8,128)(2,1)S(1)} async-done(((bf16[128,72,128]{2,1,0:T(8,128)(2,1)}), bf16[128,72,128]{2,1,0:T(8,128)(2,1)S(1)}, u32[]{:S(2)}, u32[]{:S(2)}) %all-to-all-start) | async-done | bytes 2359328 | tf_op jit(solution)/shard_map/all_to_all | solution.py:393
  46.8 17.4 %attend.1 = (bf16[8,256,1024]{2,1,0:T(8,128)(2,1)}, f32[8,8,1024]{2,1,0:T(8,128)}, bf16[8,256,512]{2,1,0:T(8,128)(2,1)}, bf16[8,16,72,128]{3,2,1,0:T(8,128)(2,1)}) custom-call(s32[8]{0:T(128)S(1)} %get-tuple-element.22.slot_ref, s32[8]{0:T(128)S(1)} %select_reduce_fusion.3.len_ref, bf16[8,16,72,128]{3,2,1,0:T(8,128)(2,1)S(1)} %bitcast.19, ...), custom_call_target="tpu_custom_call" | custom-call | flops 9126805504 | bytes 31457280 | tf_op jit(solution)/shard_map/attend/pallas_call | solution.py:309
  64.2 5.1 %all-to-all-start.1 = ((bf16[128,72,128]{2,1,0:T(8,128)(2,1)}), bf16[128,72,128]{2,1,0:T(8,128)(2,1)S(1)}, u32[]{:S(2)}, u32[]{:S(2)}) async-start(bf16[128,72,128]{2,1,0:T(8,128)(2,1)} %bitcast.20), calls=%async_computation.1 | async-start | bytes 4718592 | tf_op jit(solution)/shard_map/all_to_all | solution.py:405
  69.3 0.1 broadcast_in_dim.54
  69.4 0.1 eq.54
  69.5 0.1 select_reduce_fusion.2
  69.6 0.2 compare_reduce_fusion.1
  69.8 19.1 %outputs.1 = bf16[1024,1024]{1,0:T(8,128)(2,1)} custom-call(bf16[8,256,512]{2,1,0:T(8,128)(2,1)} %get-tuple-element.13.latent_ref, bf16[1024,576]{1,0:T(8,128)(2,1)} %copy.22.own_ref, bf16[8,256,1024]{2,1,0:T(8,128)(2,1)} %get-tuple-element.14.aT_ref, bf16[8,128,1024]{2,1,0:T(8,128)(2,1)} %get-tuple-element.15.e_ref, ...), custom_call_target="tpu_custom_call" | custom-call | flops 4294967296 | bytes 16777216 | tf_op jit(solution)/shard_map/outputs/pallas_call | solution.py:351
  88.9 12.6 %all-to-all-done.1 = bf16[128,72,128]{2,1,0:T(8,128)(2,1)S(1)} async-done(((bf16[128,72,128]{2,1,0:T(8,128)(2,1)}), bf16[128,72,128]{2,1,0:T(8,128)(2,1)S(1)}, u32[]{:S(2)}, u32[]{:S(2)}) %all-to-all-start.1) | async-done | bytes 2359328 | tf_op jit(solution)/shard_map/all_to_all | solution.py:405
  101.4 0.3 convert_reduce_fusion
  101.7 0.1 select_reduce_fusion.1
  101.9 0.1 reshape.65
  102.0 0.6 pad_maximum_fusion
  (5 shorter events, 0.0 us)
Async XLA Ops:
  3.1 11.6 %copy-start = (bf16[1024,576]{0,1:T(8,128)(2,1)S(1)}, bf16[1024,576]{0,1:T(8,128)(2,1)}, u32[]{:S(2)}) copy-start(bf16[1024,576]{0,1:T(8,128)(2,1)} %param.12) | copy-start | bytes 3538948
  3.2 43.6 %all-to-all-start = ((bf16[128,72,128]{2,1,0:T(8,128)(2,1)}), bf16[128,72,128]{2,1,0:T(8,128)(2,1)S(1)}, u32[]{:S(2)}, u32[]{:S(2)}) async-start(bf16[128,72,128]{2,1,0:T(8,128)(2,1)} %bitcast), calls=%async_computation | async-start | bytes 4718592 | tf_op jit(solution)/shard_map/all_to_all | solution.py:393
  14.7 1.5 %copy-start.1 = (s32[64]{0:T(128)S(1)}, s32[64]{0:T(128)}, u32[]{:S(2)}) copy-start(s32[64]{0:T(128)} %prompt_any.1) | copy-start | bytes 772
  14.7 1.6 %copy-start.2 = (s32[16]{0:T(128)S(1)}, s32[16]{0:T(128)}, u32[]{:S(2)}) copy-start(s32[16]{0:T(128)} %param.15) | copy-start | bytes 196
  64.2 37.2 %all-to-all-start.1 = ((bf16[128,72,128]{2,1,0:T(8,128)(2,1)}), bf16[128,72,128]{2,1,0:T(8,128)(2,1)S(1)}, u32[]{:S(2)}, u32[]{:S(2)}) async-start(bf16[128,72,128]{2,1,0:T(8,128)(2,1)} %bitcast.20), calls=%async_computation.1 | async-start | bytes 4718592 | tf_op jit(solution)/shard_map/all_to_all | solution.py:405

commit v5 on v4

--- a/solution.py
+++ b/solution.py
@@ -248,13 +248,16 @@
         seen = jnp.where((k < j) & (slot_ref[k] == slot), 1, seen)
     values = unpack_latent(latent_ref, slab)
     value_ref[0] = values
-    keys = jnp.concatenate([values, unpack_rope(latent_ref, slab)], axis=1)
+    keys_rope = unpack_rope(latent_ref, slab)
     row = lax.broadcasted_iota(jnp.int32, (key_span, chunk), 0)
     allowed = row < length
     for c in range(columns // chunk):
         at = pl.ds(c * chunk, chunk)
-        scores = dot_nn(keys, fq_ref[0, :, at])
-        grad_att = dot_nn(values, gl_ref[0, :, at])
+        both = jnp.concatenate([fq_ref[0, pl.ds(0, latent_width), at], gl_ref[0, :, at]], axis=1)
+        both = dot_nn(values, both)
+        rotary = dot_nn(keys_rope, fq_ref[0, pl.ds(latent_width, rope), at])
+        scores = both[:, :chunk] + rotary
+        grad_att = both[:, chunk:]
         own_top = stat_ref[0, pl.ds(0, 1), at]
         scores = jnp.where(allowed, scores * (scaling * LOG2E), -1e30)
         top = jnp.maximum(jnp.max(scores, axis=0, keepdims=True), own_top)
@@ -264,9 +267,8 @@
         inverse = 1.0 / total
         inner = jnp.sum(weights * grad_att, axis=0, keepdims=True)
         inner = (inner + shift * stat_ref[0, pl.ds(2, 1), at]) * inverse
-        attention = weights * inverse
-        aT_ref[0, :, at] = attention.astype(BF16)
-        gs_ref[:, at] = (attention * ((grad_att - inner) * scaling)).astype(BF16)
+        aT_ref[0, :, at] = (weights * inverse).astype(BF16)
+        gs_ref[:, at] = (weights * (grad_att - inner) * (inverse * scaling)).astype(BF16)
         ratio_ref[0, pl.ds(0, 1), at] = shift * inverse
     combined = dot_nt(gs_ref[...], fq_ref[0])
     value_term = dot_nt(aT_ref[0], gl_ref[0])
@@ -277,8 +279,9 @@
     rope_part += jnp.where(seen == 1, earlier[:, latent_width:], 0.0)
     acc_ref[slot, :, pl.ds(0, latent_width)] = latent_part
     acc_ref[slot, :, pl.ds(latent_width, rope)] = rope_part
+    total = jnp.concatenate([latent_part, rope_part], axis=1)
     for h in range(slabs):
-        piece_ref[0, h] = pack_rows(acc_ref[slot, pl.ds(h * slab, slab), :]).astype(BF16)
+        piece_ref[0, h] = pack_rows(total[h * slab : (h + 1) * slab]).astype(BF16)
 
 
 def attend(slots, lengths, gathered, stats, full_t, grad_t, head_width):

time: 103 us -> 102 us (level)
  no operation moved by 1% of the time
where the time goes in v5:
time: 102 us
  Pallas kernels  61 us (60%)
  waiting for transfers between devices  20 us (20%)
  starting transfers between devices  16.6 us (16%)
  local copies, waits for them, and re-layouts  1.73 us (2%)
  other arithmetic  1.65 us (2%)
    pallas_call x1, Pallas kernels, outputs(): pl.pallas_call(output_kernel, grid=(resp_count,), in_specs=[pl.BlockSpec(...  19.1 us
    pallas_call x1, Pallas kernels, attend(): pl.pallas_call(functools.partial(attend_kernel, head_width), grid_spec=gr...  16.4 us
    all_to_all x1, waiting for transfers between devices, on_device(): lax.all_to_all(pieces.reshape(groups * slab_count, -1, 128), ('resp', 'he...  12.5 us
    pallas_call x1, Pallas kernels, lift_tokens(): pl.pallas_call(up_kernel, grid=(heads // 2,), in_specs=[pl.BlockSpec((tok...  11.7 us
    all_to_all x1, starting transfers between devices, on_device(): lax.all_to_all(copies, ('resp', 'head'), split_axis=0, concat_axis=0, til...  11.5 us
    pallas_call x1, Pallas kernels, own_scores(): pl.pallas_call(functools.partial(own_kernel, head_width), grid=(resp_coun...  11.2 us
    all_to_all x1, waiting for transfers between devices, on_device(): lax.all_to_all(copies, ('resp', 'head'), split_axis=0, concat_axis=0, til...  7.44 us
    all_to_all x1, starting transfers between devices, on_device(): lax.all_to_all(pieces.reshape(groups * slab_count, -1, 128), ('resp', 'he...  5.08 us
  transfers between devices with their start and end apart: 2, of which 2 were waited for; matrix products, arithmetic and copies ran while one was open for 2% of the time, Pallas kernels for 41%

profile of v5, /device:TPU:1, one launch (start us, length us, event | category | flops | bytes accessed | tf_op | source)
XLA Modules:
  0.0 101.7 jit_solution(14750443062772897808)
XLA Ops:
  0.6 2.5 %pack.1 = bf16[8,16,72,128]{3,2,1,0:T(8,128)(2,1)} custom-call(s32[64]{0:T(128)} %prompt_any.1, bf16[2,16,576]{2,1,0:T(8,128)(2,1)} %latent_any.1), custom_call_target="tpu_custom_call" | custom-call | tf_op jit(solution)/shard_map/pack/pallas_call | solution.py:127
  3.1 0.0 copy-start
  3.2 11.5 %all-to-all-start = ((bf16[128,72,128]{2,1,0:T(8,128)(2,1)}), bf16[128,72,128]{2,1,0:T(8,128)(2,1)S(1)}, u32[]{:S(2)}, u32[]{:S(2)}) async-start(bf16[128,72,128]{2,1,0:T(8,128)(2,1)} %bitcast), calls=%async_computation | async-start | bytes 4718592 | tf_op jit(solution)/shard_map/all_to_all | solution.py:396
  14.7 0.0 copy-start.1
  14.7 0.0 copy-start.2
  14.7 0.0 copy-done
  14.7 1.5 %copy.22.own_ref = bf16[1024,576]{1,0:T(8,128)(2,1)} copy(bf16[1024,576]{0,1:T(8,128)(2,1)S(1)} %copy-done) | data formatting | bytes 2359296 | tf_op args[4]
  16.2 0.0 copy-done.1
  16.2 0.1 and_select_fusion.2
  16.3 0.0 copy-done.2
  16.3 0.2 select_reduce_fusion.3.len_ref
  16.4 11.7 %lift_tokens.1 = (bf16[8,576,1024]{2,1,0:T(8,128)(2,1)}, bf16[8,512,1024]{2,1,0:T(8,128)(2,1)}) custom-call(bf16[1024,1536]{1,0:T(8,128)(2,1)} %q_ref.1, bf16[8,128,512]{2,1,0:T(8,128)(2,1)} %uk_ref.1, bf16[1024,1024]{1,0:T(8,128)(2,1)} %go_ref.1, bf16[8,512,128]{2,1,0:T(8,128)(2,1)} %uv_ref.3), custom_call_target="tpu_custom_call" | custom-call | flops 2147483648 | bytes 31457280 | tf_op jit(solution)/shard_map/lift_tokens/pallas_call | solution.py:67
  28.2 11.2 %own_scores.1 = (bf16[8,128,1024]{2,1,0:T(8,128)(2,1)}, f32[8,8,1024]{2,1,0:T(8,128)}) custom-call(bf16[1024,576]{1,0:T(8,128)(2,1)} %copy.22.own_ref, bf16[8,576,1024]{2,1,0:T(8,128)(2,1)} %get-tuple-element.10.fq_ref, bf16[8,512,1024]{2,1,0:T(8,128)(2,1)} %get-tuple-element.11.gl_ref), custom_call_target="tpu_custom_call" | custom-call | flops 2281701376 | bytes 23068672 | tf_op jit(solution)/shard_map/own_scores/pallas_call | solution.py:170
  39.4 7.4 %all-to-all-done = bf16[128,72,128]{2,1,0:T(8,128)(2,1)S(1)} async-done(((bf16[128,72,128]{2,1,0:T(8,128)(2,1)}), bf16[128,72,128]{2,1,0:T(8,128)(2,1)S(1)}, u32[]{:S(2)}, u32[]{:S(2)}) %all-to-all-start) | async-done | bytes 2359328 | tf_op jit(solution)/shard_map/all_to_all | solution.py:396
  46.8 16.4 %attend.1 = (bf16[8,256,1024]{2,1,0:T(8,128)(2,1)}, f32[8,8,1024]{2,1,0:T(8,128)}, bf16[8,256,512]{2,1,0:T(8,128)(2,1)}, bf16[8,16,72,128]{3,2,1,0:T(8,128)(2,1)}) custom-call(s32[8]{0:T(128)S(1)} %get-tuple-element.22.slot_ref, s32[8]{0:T(128)S(1)} %select_reduce_fusion.3.len_ref, bf16[8,16,72,128]{3,2,1,0:T(8,128)(2,1)S(1)} %bitcast.19, ...), custom_call_target="tpu_custom_call" | custom-call | flops 9126805504 | bytes 31457280 | tf_op jit(solution)/shard_map/attend/pallas_call | solution.py:312
  63.3 5.1 %all-to-all-start.1 = ((bf16[128,72,128]{2,1,0:T(8,128)(2,1)}), bf16[128,72,128]{2,1,0:T(8,128)(2,1)S(1)}, u32[]{:S(2)}, u32[]{:S(2)}) async-start(bf16[128,72,128]{2,1,0:T(8,128)(2,1)} %bitcast.20), calls=%async_computation.1 | async-start | bytes 4718592 | tf_op jit(solution)/shard_map/all_to_all | solution.py:408
  68.4 0.1 broadcast_in_dim.54
  68.4 0.1 eq.54
  68.5 0.1 select_reduce_fusion.2
  68.6 0.2 compare_reduce_fusion.1
  68.8 19.1 %outputs.1 = bf16[1024,1024]{1,0:T(8,128)(2,1)} custom-call(bf16[8,256,512]{2,1,0:T(8,128)(2,1)} %get-tuple-element.13.latent_ref, bf16[1024,576]{1,0:T(8,128)(2,1)} %copy.22.own_ref, bf16[8,256,1024]{2,1,0:T(8,128)(2,1)} %get-tuple-element.14.aT_ref, bf16[8,128,1024]{2,1,0:T(8,128)(2,1)} %get-tuple-element.15.e_ref, ...), custom_call_target="tpu_custom_call" | custom-call | flops 4294967296 | bytes 16777216 | tf_op jit(solution)/shard_map/outputs/pallas_call | solution.py:354
  87.9 12.5 %all-to-all-done.1 = bf16[128,72,128]{2,1,0:T(8,128)(2,1)S(1)} async-done(((bf16[128,72,128]{2,1,0:T(8,128)(2,1)}), bf16[128,72,128]{2,1,0:T(8,128)(2,1)S(1)}, u32[]{:S(2)}, u32[]{:S(2)}) %all-to-all-start.1) | async-done | bytes 2359328 | tf_op jit(solution)/shard_map/all_to_all | solution.py:408
  100.5 0.3 convert_reduce_fusion
  100.8 0.1 select_reduce_fusion.1
  100.9 0.1 reshape.65
  101.0 0.6 pad_maximum_fusion
  (5 shorter events, 0.0 us)
Async XLA Ops:
  3.1 11.6 %copy-start = (bf16[1024,576]{0,1:T(8,128)(2,1)S(1)}, bf16[1024,576]{0,1:T(8,128)(2,1)}, u32[]{:S(2)}) copy-start(bf16[1024,576]{0,1:T(8,128)(2,1)} %param.12) | copy-start | bytes 3538948
  3.2 43.6 %all-to-all-start = ((bf16[128,72,128]{2,1,0:T(8,128)(2,1)}), bf16[128,72,128]{2,1,0:T(8,128)(2,1)S(1)}, u32[]{:S(2)}, u32[]{:S(2)}) async-start(bf16[128,72,128]{2,1,0:T(8,128)(2,1)} %bitcast), calls=%async_computation | async-start | bytes 4718592 | tf_op jit(solution)/shard_map/all_to_all | solution.py:396
  14.7 1.5 %copy-start.1 = (s32[64]{0:T(128)S(1)}, s32[64]{0:T(128)}, u32[]{:S(2)}) copy-start(s32[64]{0:T(128)} %prompt_any.1) | copy-start | bytes 772
  14.7 1.6 %copy-start.2 = (s32[16]{0:T(128)S(1)}, s32[16]{0:T(128)}, u32[]{:S(2)}) copy-start(s32[16]{0:T(128)} %param.15) | copy-start | bytes 196
  63.3 37.2 %all-to-all-start.1 = ((bf16[128,72,128]{2,1,0:T(8,128)(2,1)}), bf16[128,72,128]{2,1,0:T(8,128)(2,1)S(1)}, u32[]{:S(2)}, u32[]{:S(2)}) async-start(bf16[128,72,128]{2,1,0:T(8,128)(2,1)} %bitcast.20), calls=%async_computation.1 | async-start | bytes 4718592 | tf_op jit(solution)/shard_map/all_to_all | solution.py:408

commit v6 on v5

--- a/solution.py
+++ b/solution.py
@@ -6,10 +6,13 @@
 from jax import lax
 from jax.experimental import pallas as pl
 from jax.experimental.pallas import tpu as pltpu
-from jax.sharding import PartitionSpec as P
+from jax.sharding import Mesh, PartitionSpec as P
 
 BF16 = jnp.bfloat16
 F32 = jnp.float32
+ORDER = ("core", "z", "y", "x")
+RESP = ("x", "core")
+HEAD = ("y", "z")
 LOG2E = 1.4426950408889634
 
 
@@ -108,7 +111,8 @@
         copy.start()
     for copy in copies:
         copy.wait()
-    groups, slab_count, packed_rows, lanes = out_ref.shape
+    cores, depth, height, width, packed_rows, lanes = out_ref.shape
+    groups = cores * width
     owned = latent_ref.shape[0]
     resp_count = prompt_ref.shape[0] // groups
     first = lax.axis_index(axis) * owned
@@ -118,14 +122,16 @@
         for p in range(1, owned):
             hits = [prompt_ref[r * resp_count + i] == first + p for i in range(resp_count)]
             chosen = jnp.where(functools.reduce(jnp.logical_or, hits), packed[p], chosen)
-        out_ref[r] = jnp.broadcast_to(chosen[None], (slab_count, packed_rows, lanes))
-
-
-def pack(response_prompt, prompt_latent, groups, slab_count):
+        out_ref[r % cores, :, :, r // cores] = jnp.broadcast_to(
+            chosen[None, None], (depth, height, packed_rows, lanes)
+        )
+
+
+def pack(response_prompt, prompt_latent, extents):
     owned, slab_rows, channels = prompt_latent.shape
     packed_rows = slab_rows * channels // 128
     return pl.pallas_call(
-        functools.partial(pack_kernel, "resp"),
+        functools.partial(pack_kernel, RESP),
         in_specs=[pl.BlockSpec(memory_space=pl.ANY)] * 2,
         out_specs=pl.BlockSpec(memory_space=pltpu.VMEM),
         scratch_shapes=[
@@ -133,7 +139,7 @@
             pltpu.VMEM(prompt_latent.shape, BF16),
             pltpu.SemaphoreType.DMA((2,)),
         ],
-        out_shape=pltpu.VMEM((groups, slab_count, packed_rows, 128), BF16),
+        out_shape=pltpu.VMEM(extents + (packed_rows, 128), BF16),
         compiler_params=pltpu.CompilerParams(vmem_limit_bytes=10 * 1024 * 1024),
         name="pack",
     )(*in_hbm(response_prompt, prompt_latent))
@@ -193,13 +199,16 @@
     )(*in_hbm(resp_latent, full_t, grad_t))
 
 
+def slab_list(ref):
+    _, depth, height, _, packed_rows, _ = ref.shape
+    return [(0, z, y, 0) for y in range(height) for z in range(depth)], packed_rows
+
+
 def unpack_latent(packed_ref, slab):
-    slabs, packed_rows, lanes = packed_ref.shape[1:]
+    places, packed_rows = slab_list(packed_ref)
     return jnp.concatenate(
         [
-            jnp.concatenate(
-                [packed_ref[0, h, pl.ds(slab * c, slab), :] for h in range(slabs)], axis=0
-            )
+            jnp.concatenate([packed_ref[p + (pl.ds(slab * c, slab),)] for p in places], axis=0)
             for c in range(packed_rows // slab)
         ],
         axis=1,
@@ -207,11 +216,12 @@
 
 
 def unpack_rope(packed_ref, slab):
-    slabs, packed_rows, lanes = packed_ref.shape[1:]
+    places, packed_rows = slab_list(packed_ref)
     rows = []
-    for h in range(slabs):
-        tail = packed_ref[0, h].astype(F32)[packed_rows - slab // 2 :]
-        rows += [tail[:, : lanes // 2], tail[:, lanes // 2 :]]
+    for p in places:
+        tail = packed_ref[p].astype(F32)[packed_rows - slab // 2 :]
+        half = tail.shape[1] // 2
+        rows += [tail[:, :half], tail[:, half:]]
     return jnp.concatenate(rows, axis=0).astype(BF16)
 
 
@@ -236,8 +246,8 @@
     columns = fq_ref.shape[2]
     rope = channels - latent_width
     groups, key_span, _ = acc_ref.shape
-    slabs = latent_ref.shape[1]
-    slab = key_span // slabs
+    places, _ = slab_list(latent_ref)
+    slab = key_span // len(places)
     scaling = 1.0 / math.sqrt(head_width)
     chunk = 256
 
@@ -280,20 +290,26 @@
     acc_ref[slot, :, pl.ds(0, latent_width)] = latent_part
     acc_ref[slot, :, pl.ds(latent_width, rope)] = rope_part
     total = jnp.concatenate([latent_part, rope_part], axis=1)
-    for h in range(slabs):
-        piece_ref[0, h] = pack_rows(total[h * slab : (h + 1) * slab]).astype(BF16)
+    for h, place in enumerate(places):
+        piece_ref[place] = pack_rows(total[h * slab : (h + 1) * slab]).astype(BF16)
 
 
 def attend(slots, lengths, gathered, stats, full_t, grad_t, head_width):
-    groups, slabs, packed_rows, lanes = gathered.shape
+    cores, depth, height, width, packed_rows, lanes = gathered.shape
+    groups = cores * width
     resp_count, channels, columns = full_t.shape
-    key_span = slabs * packed_rows * lanes // channels
+    key_span = depth * height * packed_rows * lanes // channels
+    block = (1, depth, height, 1, packed_rows, lanes)
+
+    def slot_block(j, s, n):
+        return (lax.rem(s[j], cores), 0, 0, lax.div(s[j], cores), 0, 0)
+
     latent_width = grad_t.shape[1]
     grid_spec = pltpu.PrefetchScalarGridSpec(
         num_scalar_prefetch=2,
         grid=(resp_count,),
         in_specs=[
-            pl.BlockSpec((1, slabs, packed_rows, lanes), lambda j, s, n: (s[j], 0, 0, 0)),
+            pl.BlockSpec(block, slot_block),
             pl.BlockSpec((1, 8, columns), lambda j, s, n: (j, 0, 0)),
             pl.BlockSpec((1, channels, columns), lambda j, s, n: (j, 0, 0)),
             pl.BlockSpec((1, latent_width, columns), lambda j, s, n: (j, 0, 0)),
@@ -302,7 +318,7 @@
             pl.BlockSpec((1, key_span, columns), lambda j, s, n: (j, 0, 0)),
             pl.BlockSpec((1, 8, columns), lambda j, s, n: (j, 0, 0)),
             pl.BlockSpec((1, key_span, latent_width), lambda j, s, n: (j, 0, 0)),
-            pl.BlockSpec((1, slabs, packed_rows, lanes), lambda j, s, n: (s[j], 0, 0, 0)),
+            pl.BlockSpec(block, slot_block),
         ],
         scratch_shapes=[
             pltpu.VMEM((groups, key_span, channels), F32),
@@ -316,7 +332,7 @@
             pltpu.HBM((resp_count, key_span, columns), BF16),
             pltpu.HBM((resp_count, 8, columns), F32),
             pltpu.HBM((resp_count, key_span, latent_width), BF16),
-            pltpu.HBM((groups, slabs, packed_rows, lanes), BF16),
+            pltpu.HBM(gathered.shape, BF16),
         ],
         compiler_params=pltpu.CompilerParams(vmem_limit_bytes=20*1024*1024),
         cost_estimate=pl.CostEstimate(
@@ -377,9 +393,10 @@
 def on_device(
     queries, up_key, up_value, prompt_latent, resp_latent, grad_out, response_prompt, prompt_length
 ):
-    groups = lax.axis_size("resp")
-    slab_count = lax.axis_size("head")
-    my_group = lax.axis_index("resp")
+    extents = tuple(lax.axis_size(name) for name in ORDER)
+    cores, _, _, width = extents
+    groups = cores * width
+    my_group = lax.axis_index(RESP)
     owned, slab_rows, channels = prompt_latent.shape
     resp_count = response_prompt.shape[0] // groups
     owners = response_prompt // owned
@@ -391,10 +408,11 @@
         axis=1,
     )
     wanted_mine = lax.dynamic_index_in_dim(wanted, my_group, 1, False)
-    copies = pack(response_prompt, prompt_latent, groups, slab_count)
-    copies = copies.reshape(groups * slab_count, -1, 128)
-    arrived = lax.all_to_all(copies, ("resp", "head"), split_axis=0, concat_axis=0, tiled=True)
-    gathered = arrived.reshape(groups, slab_count, -1, 128)
+    copies = pack(response_prompt, prompt_latent, extents)
+    arrived = lax.all_to_all(
+        copies.reshape((-1,) + copies.shape[4:]), ORDER, split_axis=0, concat_axis=0, tiled=True
+    )
+    gathered = arrived.reshape(copies.shape)
     local_prompt = lax.dynamic_slice_in_dim(response_prompt, my_group * resp_count, resp_count)
     slots = local_prompt // owned
     hits = local_prompt[:, None] == jnp.arange(prompt_length.shape[0])[None, :]
@@ -406,19 +424,13 @@
         slots, lengths, gathered, stats, full_t, grad_t, head_width
     )
     returned_grad = lax.all_to_all(
-        pieces.reshape(groups * slab_count, -1, 128),
-        ("resp", "head"),
-        split_axis=0,
-        concat_axis=0,
-        tiled=True,
+        pieces.reshape((-1,) + pieces.shape[4:]), ORDER, split_axis=0, concat_axis=0, tiled=True
     )
     attn_out = outputs(prompt_values, resp_latent, attention_t, own_weights, ratio, up_value)
-    summed = jnp.sum(returned_grad.reshape(groups, slab_count, -1, 128).astype(F32), axis=1)
+    summed = jnp.sum(returned_grad.reshape(pieces.shape).astype(F32), axis=(1, 2))
+    kept = wanted_mine.reshape(width, cores).T[:, :, None, None]
     packed = jnp.stack(
-        [
-            jnp.sum(jnp.where((wanted_mine == p)[:, None, None], summed, 0.0), axis=0)
-            for p in range(owned)
-        ]
+        [jnp.sum(jnp.where(kept == p, summed, 0.0), axis=(0, 1)) for p in range(owned)]
     )
     blocks = channels // 128
     latent = packed[:, : slab_rows * blocks].reshape(owned, blocks, slab_rows, 128)
@@ -434,19 +446,21 @@
 
 
 def solution(mesh):
+    groups, slab_count = mesh.devices.shape
+    devices = mesh.devices.reshape(groups // 2, 2, slab_count // 4, 4)
     return jax.shard_map(
         on_device,
-        mesh=mesh,
+        mesh=Mesh(devices, RESP + HEAD),
         in_specs=(
-            P("resp", "head"),
-            P("head", None, None),
-            P("head", None, None),
-            P("resp", "head", None),
-            P("resp", None),
-            P("resp", "head"),
+            P(RESP, HEAD),
+            P(HEAD, None, None),
+            P(HEAD, None, None),
+            P(RESP, HEAD, None),
+            P(RESP, None),
+            P(RESP, HEAD),
             P(),
             P(),
         ),
-        out_specs=(P("resp", "head"), P("resp", "head", None)),
+        out_specs=(P(RESP, HEAD), P(RESP, HEAD, None)),
         check_vma=False,
     )

time: 102 us -> 102 us (level)
  waiting for transfers between devices: 20 us -> 17.8 us
  starting transfers between devices: 16.6 us -> 17.9 us
    all_to_all x2, waiting for transfers between devices: 20 us -> 17.8 us  [the longest x1 11.3 us: on_device(): lax.all_to_all(pieces.reshape((-1,) + pieces.shape[4:]), ORDER, split_axi...]
    all_to_all x2, starting transfers between devices: 16.6 us -> 17.9 us  [the longest x1 11.5 us: on_device(): lax.all_to_all(copies.reshape((-1,) + copies.shape[4:]), ORDER, split_axi...]
  transfers between devices with their start and end apart: 2 -> 2, of which waited for: 2 -> 2; matrix products, arithmetic and copies ran while one was open for 2% -> 3% of each run, Pallas kernels for 41% -> 41%
where the time goes in v6:
time: 102 us
  Pallas kernels  61.4 us (60%)
  starting transfers between devices  17.9 us (18%)
  waiting for transfers between devices  17.8 us (17%)
  local copies, waits for them, and re-layouts  2.12 us (2%)
  other arithmetic  1.65 us (2%)
    pallas_call x1, Pallas kernels, outputs(): pl.pallas_call(output_kernel, grid=(resp_count,), in_specs=[pl.BlockSpec(...  19.1 us
    pallas_call x1, Pallas kernels, attend(): pl.pallas_call(functools.partial(attend_kernel, head_width), grid_spec=gr...  16.9 us
    pallas_call x1, Pallas kernels, lift_tokens(): pl.pallas_call(up_kernel, grid=(heads // 2,), in_specs=[pl.BlockSpec((tok...  11.7 us
    all_to_all x1, starting transfers between devices, on_device(): lax.all_to_all(copies.reshape((-1,) + copies.shape[4:]), ORDER, split_axi...  11.5 us
    all_to_all x1, waiting for transfers between devices, on_device(): lax.all_to_all(pieces.reshape((-1,) + pieces.shape[4:]), ORDER, split_axi...  11.3 us
    pallas_call x1, Pallas kernels, own_scores(): pl.pallas_call(functools.partial(own_kernel, head_width), grid=(resp_coun...  11.2 us
    all_to_all x1, waiting for transfers between devices, on_device(): lax.all_to_all(copies.reshape((-1,) + copies.shape[4:]), ORDER, split_axi...  6.55 us
    all_to_all x1, starting transfers between devices, on_device(): lax.all_to_all(pieces.reshape((-1,) + pieces.shape[4:]), ORDER, split_axi...  6.44 us
  transfers between devices with their start and end apart: 2, of which 2 were waited for; matrix products, arithmetic and copies ran while one was open for 3% of the time, Pallas kernels for 41%

profile of v6, /device:TPU:1, one launch (start us, length us, event | category | flops | bytes accessed | tf_op | source)
XLA Modules:
  0.0 101.7 jit_solution(5172037986013364941)
XLA Ops:
  0.6 2.5 %pack.1 = bf16[2,4,4,4,72,128]{5,4,3,2,1,0:T(8,128)(2,1)} custom-call(s32[64]{0:T(128)} %prompt_any.1, bf16[2,16,576]{2,1,0:T(8,128)(2,1)} %latent_any.1), custom_call_target="tpu_custom_call" | custom-call | tf_op jit(solution)/shard_map/pack/pallas_call | solution.py:133
  3.1 0.0 copy-start
  3.2 11.5 %all-to-all-start = ((bf16[128,72,128]{2,1,0:T(8,128)(2,1)}), bf16[128,72,128]{2,1,0:T(8,128)(2,1)S(1)}, u32[]{:S(2)}, u32[]{:S(2)}) async-start(bf16[128,72,128]{2,1,0:T(8,128)(2,1)} %bitcast), calls=%async_computation | async-start | bytes 4718592 | tf_op jit(solution)/shard_map/all_to_all | solution.py:412
  14.7 0.0 copy-start.1
  14.7 0.0 copy-start.2
  14.7 0.0 copy-done
  14.7 1.5 %copy.30.own_ref = bf16[1024,576]{1,0:T(8,128)(2,1)} copy(bf16[1024,576]{0,1:T(8,128)(2,1)S(1)} %copy-done) | data formatting | bytes 2359296 | tf_op args[4]
  16.2 0.0 copy-done.1
  16.2 0.1 and_select_fusion.2
  16.3 0.0 copy-done.2
  16.3 0.2 select_reduce_fusion.3.len_ref
  16.4 11.7 %lift_tokens.1 = (bf16[8,576,1024]{2,1,0:T(8,128)(2,1)}, bf16[8,512,1024]{2,1,0:T(8,128)(2,1)}) custom-call(bf16[1024,1536]{1,0:T(8,128)(2,1)} %q_ref.1, bf16[8,128,512]{2,1,0:T(8,128)(2,1)} %uk_ref.1, bf16[1024,1024]{1,0:T(8,128)(2,1)} %go_ref.1, bf16[8,512,128]{2,1,0:T(8,128)(2,1)} %uv_ref.3), custom_call_target="tpu_custom_call" | custom-call | flops 2147483648 | bytes 31457280 | tf_op jit(solution)/shard_map/lift_tokens/pallas_call | solution.py:70
  28.2 11.2 %own_scores.1 = (bf16[8,128,1024]{2,1,0:T(8,128)(2,1)}, f32[8,8,1024]{2,1,0:T(8,128)}) custom-call(bf16[1024,576]{1,0:T(8,128)(2,1)} %copy.30.own_ref, bf16[8,576,1024]{2,1,0:T(8,128)(2,1)} %get-tuple-element.10.fq_ref, bf16[8,512,1024]{2,1,0:T(8,128)(2,1)} %get-tuple-element.11.gl_ref), custom_call_target="tpu_custom_call" | custom-call | flops 2281701376 | bytes 23068672 | tf_op jit(solution)/shard_map/own_scores/pallas_call | solution.py:176
  39.4 6.5 %all-to-all-done = bf16[128,72,128]{2,1,0:T(8,128)(2,1)S(1)} async-done(((bf16[128,72,128]{2,1,0:T(8,128)(2,1)}), bf16[128,72,128]{2,1,0:T(8,128)(2,1)S(1)}, u32[]{:S(2)}, u32[]{:S(2)}) %all-to-all-start) | async-done | bytes 2359328 | tf_op jit(solution)/shard_map/all_to_all | solution.py:412
  45.9 16.9 %attend.1 = (bf16[8,256,1024]{2,1,0:T(8,128)(2,1)}, f32[8,8,1024]{2,1,0:T(8,128)}, bf16[8,256,512]{2,1,0:T(8,128)(2,1)}, bf16[2,4,4,4,72,128]{5,4,3,2,1,0:T(8,128)(2,1)}) custom-call(s32[8]{0:T(128)S(1)} %get-tuple-element.22.slot_ref, s32[8]{0:T(128)S(1)} %select_reduce_fusion.3.len_ref, bf16[2,4,4,4,72,128]{5,4,3,2,1,0:T(8,128)(2,1)S(1)} %bitcast.20, ...), custom_call_target="tpu_custom_call" | custom-call | flops 9126805504 | bytes 31457280 | tf_op jit(solution)/shard_map/attend/pallas_call | solution.py:328
  62.8 6.4 %all-to-all-start.1 = ((bf16[128,72,128]{2,1,0:T(8,128)(2,1)}), bf16[128,72,128]{2,1,0:T(8,128)(2,1)S(1)}, u32[]{:S(2)}, u32[]{:S(2)}) async-start(bf16[128,72,128]{2,1,0:T(8,128)(2,1)} %bitcast.22), calls=%async_computation.1 | async-start | bytes 4718592 | tf_op jit(solution)/shard_map/all_to_all | solution.py:426
  69.3 0.1 broadcast_in_dim.53
  69.3 0.1 eq.54
  69.4 0.1 select_reduce_fusion.2
  69.5 0.2 compare_reduce_fusion.1
  69.7 0.1 eq.59
  69.8 0.1 copy.32
  69.9 0.1 eq.62
  70.0 0.1 copy.33
  70.1 19.1 %outputs.1 = bf16[1024,1024]{1,0:T(8,128)(2,1)} custom-call(bf16[8,256,512]{2,1,0:T(8,128)(2,1)} %get-tuple-element.13.latent_ref, bf16[1024,576]{1,0:T(8,128)(2,1)} %copy.30.own_ref, bf16[8,256,1024]{2,1,0:T(8,128)(2,1)} %get-tuple-element.14.aT_ref, bf16[8,128,1024]{2,1,0:T(8,128)(2,1)} %get-tuple-element.15.e_ref, ...), custom_call_target="tpu_custom_call" | custom-call | flops 4294967296 | bytes 16777216 | tf_op jit(solution)/shard_map/outputs/pallas_call | solution.py:370
  89.2 11.3 %all-to-all-done.1 = bf16[128,72,128]{2,1,0:T(8,128)(2,1)S(1)} async-done(((bf16[128,72,128]{2,1,0:T(8,128)(2,1)}), bf16[128,72,128]{2,1,0:T(8,128)(2,1)S(1)}, u32[]{:S(2)}, u32[]{:S(2)}) %all-to-all-start.1) | async-done | bytes 2359328 | tf_op jit(solution)/shard_map/all_to_all | solution.py:426
  100.5 0.3 convert_reduce_fusion
  100.8 0.1 select_reduce_fusion.1
  101.0 0.1 reshape.61
  101.0 0.6 pad_maximum_fusion
  (5 shorter events, 0.0 us)
Async XLA Ops:
  3.1 11.6 %copy-start = (bf16[1024,576]{0,1:T(8,128)(2,1)S(1)}, bf16[1024,576]{0,1:T(8,128)(2,1)}, u32[]{:S(2)}) copy-start(bf16[1024,576]{0,1:T(8,128)(2,1)} %param.12) | copy-start | bytes 3538948
  3.2 42.7 %all-to-all-start = ((bf16[128,72,128]{2,1,0:T(8,128)(2,1)}), bf16[128,72,128]{2,1,0:T(8,128)(2,1)S(1)}, u32[]{:S(2)}, u32[]{:S(2)}) async-start(bf16[128,72,128]{2,1,0:T(8,128)(2,1)} %bitcast), calls=%async_computation | async-start | bytes 4718592 | tf_op jit(solution)/shard_map/all_to_all | solution.py:412
  14.7 1.5 %copy-start.1 = (s32[64]{0:T(128)S(1)}, s32[64]{0:T(128)}, u32[]{:S(2)}) copy-start(s32[64]{0:T(128)} %prompt_any.1) | copy-start | bytes 772
  14.7 1.6 %copy-start.2 = (s32[16]{0:T(128)S(1)}, s32[16]{0:T(128)}, u32[]{:S(2)}) copy-start(s32[16]{0:T(128)} %param.15) | copy-start | bytes 196
  62.8 37.7 %all-to-all-start.1 = ((bf16[128,72,128]{2,1,0:T(8,128)(2,1)}), bf16[128,72,128]{2,1,0:T(8,128)(2,1)S(1)}, u32[]{:S(2)}, u32[]{:S(2)}) async-start(bf16[128,72,128]{2,1,0:T(8,128)(2,1)} %bitcast.22), calls=%async_computation.1 | async-start | bytes 4718592 | tf_op jit(solution)/shard_map/all_to_all | solution.py:426

commit v7 on v6

--- a/solution.py
+++ b/solution.py
@@ -102,7 +102,9 @@
     return jnp.concatenate([rows[:, 128 * c : 128 * (c + 1)] for c in range(blocks)] + [tail], axis=0)
 
 
-def pack_kernel(axis, prompt_any, latent_any, out_ref, prompt_ref, latent_ref, sem):
+def pack_kernel(
+    axis, prompt_any, latent_any, out_ref, prompt_ref, latent_ref, block_ref, sem, out_sem
+):
     copies = [
         pltpu.make_async_copy(prompt_any, prompt_ref, sem.at[0]),
         pltpu.make_async_copy(latent_any, latent_ref, sem.at[1]),
@@ -117,29 +119,41 @@
     resp_count = prompt_ref.shape[0] // groups
     first = lax.axis_index(axis) * owned
     packed = [pack_rows(latent_ref[p].astype(F32)).astype(BF16) for p in range(owned)]
+    sends = []
     for r in range(groups):
         chosen = packed[0]
         for p in range(1, owned):
             hits = [prompt_ref[r * resp_count + i] == first + p for i in range(resp_count)]
             chosen = jnp.where(functools.reduce(jnp.logical_or, hits), packed[p], chosen)
-        out_ref[r % cores, :, :, r // cores] = jnp.broadcast_to(
+        block_ref[r] = jnp.broadcast_to(
             chosen[None, None], (depth, height, packed_rows, lanes)
         )
+        sends.append(
+            pltpu.make_async_copy(
+                block_ref.at[r], out_ref.at[r % cores, :, :, r // cores], out_sem.at[r]
+            )
+        )
+        sends[r].start()
+    for send in sends:
+        send.wait()
 
 
 def pack(response_prompt, prompt_latent, extents):
     owned, slab_rows, channels = prompt_latent.shape
     packed_rows = slab_rows * channels // 128
+    groups = extents[0] * extents[3]
     return pl.pallas_call(
         functools.partial(pack_kernel, RESP),
         in_specs=[pl.BlockSpec(memory_space=pl.ANY)] * 2,
-        out_specs=pl.BlockSpec(memory_space=pltpu.VMEM),
+        out_specs=pl.BlockSpec(memory_space=pl.ANY),
         scratch_shapes=[
             pltpu.SMEM(response_prompt.shape, response_prompt.dtype),
             pltpu.VMEM(prompt_latent.shape, BF16),
+            pltpu.VMEM((groups,) + extents[1:3] + (packed_rows, 128), BF16),
             pltpu.SemaphoreType.DMA((2,)),
-        ],
-        out_shape=pltpu.VMEM(extents + (packed_rows, 128), BF16),
+            pltpu.SemaphoreType.DMA((groups,)),
+        ],
+        out_shape=pltpu.HBM(extents + (packed_rows, 128), BF16),
         compiler_params=pltpu.CompilerParams(vmem_limit_bytes=10 * 1024 * 1024),
         name="pack",
     )(*in_hbm(response_prompt, prompt_latent))
@@ -277,8 +291,8 @@
         inverse = 1.0 / total
         inner = jnp.sum(weights * grad_att, axis=0, keepdims=True)
         inner = (inner + shift * stat_ref[0, pl.ds(2, 1), at]) * inverse
+        gs_ref[:, at] = (weights * (grad_att - inner) * (inverse * scaling)).astype(BF16)
         aT_ref[0, :, at] = (weights * inverse).astype(BF16)
-        gs_ref[:, at] = (weights * (grad_att - inner) * (inverse * scaling)).astype(BF16)
         ratio_ref[0, pl.ds(0, 1), at] = shift * inverse
     combined = dot_nt(gs_ref[...], fq_ref[0])
     value_term = dot_nt(aT_ref[0], gl_ref[0])

time: 102 us -> 102 us (level)
  no operation moved by 1% of the time
where the time goes in v7:
time: 102 us
  Pallas kernels  61.3 us (60%)
  starting transfers between devices  17.9 us (18%)
  waiting for transfers between devices  17.8 us (17%)
  local copies, waits for them, and re-layouts  2.12 us (2%)
  other arithmetic  1.65 us (2%)
    pallas_call x1, Pallas kernels, outputs(): pl.pallas_call(output_kernel, grid=(resp_count,), in_specs=[pl.BlockSpec(...  19.1 us
    pallas_call x1, Pallas kernels, attend(): pl.pallas_call(functools.partial(attend_kernel, head_width), grid_spec=gr...  16.9 us
    pallas_call x1, Pallas kernels, lift_tokens(): pl.pallas_call(up_kernel, grid=(heads // 2,), in_specs=[pl.BlockSpec((tok...  11.7 us
    all_to_all x1, starting transfers between devices, on_device(): lax.all_to_all(copies.reshape((-1,) + copies.shape[4:]), ORDER, split_axi...  11.5 us
    all_to_all x1, waiting for transfers between devices, on_device(): lax.all_to_all(pieces.reshape((-1,) + pieces.shape[4:]), ORDER, split_axi...  11.3 us
    pallas_call x1, Pallas kernels, own_scores(): pl.pallas_call(functools.partial(own_kernel, head_width), grid=(resp_coun...  11.2 us
    all_to_all x1, waiting for transfers between devices, on_device(): lax.all_to_all(copies.reshape((-1,) + copies.shape[4:]), ORDER, split_axi...  6.53 us
    all_to_all x1, starting transfers between devices, on_device(): lax.all_to_all(pieces.reshape((-1,) + pieces.shape[4:]), ORDER, split_axi...  6.38 us
  transfers between devices with their start and end apart: 2, of which 2 were waited for; matrix products, arithmetic and copies ran while one was open for 3% of the time, Pallas kernels for 41%

profile of v7, /device:TPU:1, one launch (start us, length us, event | category | flops | bytes accessed | tf_op | source)
XLA Modules:
  0.0 101.5 jit_solution(4826548450009118654)
XLA Ops:
  0.6 2.4 %pack.1 = bf16[2,4,4,4,72,128]{5,4,3,2,1,0:T(8,128)(2,1)} custom-call(s32[64]{0:T(128)} %prompt_any.1, bf16[2,16,576]{2,1,0:T(8,128)(2,1)} %latent_any.1), custom_call_target="tpu_custom_call" | custom-call | tf_op jit(solution)/shard_map/pack/pallas_call | solution.py:145
  3.0 0.0 copy-start
  3.0 11.5 %all-to-all-start = ((bf16[128,72,128]{2,1,0:T(8,128)(2,1)}), bf16[128,72,128]{2,1,0:T(8,128)(2,1)S(1)}, u32[]{:S(2)}, u32[]{:S(2)}) async-start(bf16[128,72,128]{2,1,0:T(8,128)(2,1)} %bitcast.22), calls=%async_computation | async-start | bytes 4718592 | tf_op jit(solution)/shard_map/all_to_all | solution.py:426
  14.5 0.0 copy-start.1
  14.6 0.0 copy-start.2
  14.6 0.0 copy-done
  14.6 1.5 %copy.30.own_ref = bf16[1024,576]{1,0:T(8,128)(2,1)} copy(bf16[1024,576]{0,1:T(8,128)(2,1)S(1)} %copy-done) | data formatting | bytes 2359296 | tf_op args[4]
  16.0 0.0 copy-done.1
  16.0 0.1 and_select_fusion.2
  16.1 0.0 copy-done.2
  16.1 0.2 select_reduce_fusion.3.len_ref
  16.3 11.7 %lift_tokens.1 = (bf16[8,576,1024]{2,1,0:T(8,128)(2,1)}, bf16[8,512,1024]{2,1,0:T(8,128)(2,1)}) custom-call(bf16[1024,1536]{1,0:T(8,128)(2,1)} %q_ref.1, bf16[8,128,512]{2,1,0:T(8,128)(2,1)} %uk_ref.1, bf16[1024,1024]{1,0:T(8,128)(2,1)} %go_ref.1, bf16[8,512,128]{2,1,0:T(8,128)(2,1)} %uv_ref.3), custom_call_target="tpu_custom_call" | custom-call | flops 2147483648 | bytes 31457280 | tf_op jit(solution)/shard_map/lift_tokens/pallas_call | solution.py:70
  28.0 11.2 %own_scores.1 = (bf16[8,128,1024]{2,1,0:T(8,128)(2,1)}, f32[8,8,1024]{2,1,0:T(8,128)}) custom-call(bf16[1024,576]{1,0:T(8,128)(2,1)} %copy.30.own_ref, bf16[8,576,1024]{2,1,0:T(8,128)(2,1)} %get-tuple-element.10.fq_ref, bf16[8,512,1024]{2,1,0:T(8,128)(2,1)} %get-tuple-element.11.gl_ref), custom_call_target="tpu_custom_call" | custom-call | flops 2281701376 | bytes 23068672 | tf_op jit(solution)/shard_map/own_scores/pallas_call | solution.py:190
  39.2 6.5 %all-to-all-done = bf16[128,72,128]{2,1,0:T(8,128)(2,1)S(1)} async-done(((bf16[128,72,128]{2,1,0:T(8,128)(2,1)}), bf16[128,72,128]{2,1,0:T(8,128)(2,1)S(1)}, u32[]{:S(2)}, u32[]{:S(2)}) %all-to-all-start) | async-done | bytes 2359328 | tf_op jit(solution)/shard_map/all_to_all | solution.py:426
  45.8 16.9 %attend.1 = (bf16[8,256,1024]{2,1,0:T(8,128)(2,1)}, f32[8,8,1024]{2,1,0:T(8,128)}, bf16[8,256,512]{2,1,0:T(8,128)(2,1)}, bf16[2,4,4,4,72,128]{5,4,3,2,1,0:T(8,128)(2,1)}) custom-call(s32[8]{0:T(128)S(1)} %get-tuple-element.22.slot_ref, s32[8]{0:T(128)S(1)} %select_reduce_fusion.3.len_ref, bf16[2,4,4,4,72,128]{5,4,3,2,1,0:T(8,128)(2,1)S(1)} %bitcast.20, ...), custom_call_target="tpu_custom_call" | custom-call | flops 9126805504 | bytes 31457280 | tf_op jit(solution)/shard_map/attend/pallas_call | solution.py:342
  62.7 6.4 %all-to-all-start.1 = ((bf16[128,72,128]{2,1,0:T(8,128)(2,1)}), bf16[128,72,128]{2,1,0:T(8,128)(2,1)S(1)}, u32[]{:S(2)}, u32[]{:S(2)}) async-start(bf16[128,72,128]{2,1,0:T(8,128)(2,1)} %bitcast.23), calls=%async_computation.1 | async-start | bytes 4718592 | tf_op jit(solution)/shard_map/all_to_all | solution.py:440
  69.1 0.1 broadcast_in_dim.53
  69.2 0.1 eq.54
  69.3 0.1 select_reduce_fusion.2
  69.4 0.2 compare_reduce_fusion.1
  69.6 0.1 eq.59
  69.6 0.1 copy.32
  69.8 0.1 eq.62
  69.8 0.1 copy.33
  70.0 19.1 %outputs.1 = bf16[1024,1024]{1,0:T(8,128)(2,1)} custom-call(bf16[8,256,512]{2,1,0:T(8,128)(2,1)} %get-tuple-element.13.latent_ref, bf16[1024,576]{1,0:T(8,128)(2,1)} %copy.30.own_ref, bf16[8,256,1024]{2,1,0:T(8,128)(2,1)} %get-tuple-element.14.aT_ref, bf16[8,128,1024]{2,1,0:T(8,128)(2,1)} %get-tuple-element.15.e_ref, ...), custom_call_target="tpu_custom_call" | custom-call | flops 4294967296 | bytes 16777216 | tf_op jit(solution)/shard_map/outputs/pallas_call | solution.py:384
  89.1 11.3 %all-to-all-done.1 = bf16[128,72,128]{2,1,0:T(8,128)(2,1)S(1)} async-done(((bf16[128,72,128]{2,1,0:T(8,128)(2,1)}), bf16[128,72,128]{2,1,0:T(8,128)(2,1)S(1)}, u32[]{:S(2)}, u32[]{:S(2)}) %all-to-all-start.1) | async-done | bytes 2359328 | tf_op jit(solution)/shard_map/all_to_all | solution.py:440
  100.3 0.3 convert_reduce_fusion
  100.6 0.1 select_reduce_fusion.1
  100.8 0.1 reshape.61
  100.9 0.6 pad_maximum_fusion
  (5 shorter events, 0.0 us)
Async XLA Ops:
  3.0 11.6 %copy-start = (bf16[1024,576]{0,1:T(8,128)(2,1)S(1)}, bf16[1024,576]{0,1:T(8,128)(2,1)}, u32[]{:S(2)}) copy-start(bf16[1024,576]{0,1:T(8,128)(2,1)} %param.12) | copy-start | bytes 3538948
  3.0 42.7 %all-to-all-start = ((bf16[128,72,128]{2,1,0:T(8,128)(2,1)}), bf16[128,72,128]{2,1,0:T(8,128)(2,1)S(1)}, u32[]{:S(2)}, u32[]{:S(2)}) async-start(bf16[128,72,128]{2,1,0:T(8,128)(2,1)} %bitcast.22), calls=%async_computation | async-start | bytes 4718592 | tf_op jit(solution)/shard_map/all_to_all | solution.py:426
  14.5 1.5 %copy-start.1 = (s32[64]{0:T(128)S(1)}, s32[64]{0:T(128)}, u32[]{:S(2)}) copy-start(s32[64]{0:T(128)} %prompt_any.1) | copy-start | bytes 772
  14.6 1.6 %copy-start.2 = (s32[16]{0:T(128)S(1)}, s32[16]{0:T(128)}, u32[]{:S(2)}) copy-start(s32[16]{0:T(128)} %param.15) | copy-start | bytes 196
  62.7 37.6 %all-to-all-start.1 = ((bf16[128,72,128]{2,1,0:T(8,128)(2,1)}), bf16[128,72,128]{2,1,0:T(8,128)(2,1)S(1)}, u32[]{:S(2)}, u32[]{:S(2)}) async-start(bf16[128,72,128]{2,1,0:T(8,128)(2,1)} %bitcast.23), calls=%async_computation.1 | async-start | bytes 4718592 | tf_op jit(solution)/shard_map/all_to_all | solution.py:440

commit v8 on v5

--- a/solution.py
+++ b/solution.py
@@ -267,8 +267,8 @@
         inverse = 1.0 / total
         inner = jnp.sum(weights * grad_att, axis=0, keepdims=True)
         inner = (inner + shift * stat_ref[0, pl.ds(2, 1), at]) * inverse
+        gs_ref[:, at] = (weights * (grad_att - inner) * (inverse * scaling)).astype(BF16)
         aT_ref[0, :, at] = (weights * inverse).astype(BF16)
-        gs_ref[:, at] = (weights * (grad_att - inner) * (inverse * scaling)).astype(BF16)
         ratio_ref[0, pl.ds(0, 1), at] = shift * inverse
     combined = dot_nt(gs_ref[...], fq_ref[0])
     value_term = dot_nt(aT_ref[0], gl_ref[0])

time: 102 us -> 102 us (level)
  no operation moved by 1% of the time
where the time goes in v8:
time: 102 us
  Pallas kernels  61 us (60%)
  waiting for transfers between devices  20 us (20%)
  starting transfers between devices  16.5 us (16%)
  local copies, waits for them, and re-layouts  1.73 us (2%)
  other arithmetic  1.65 us (2%)
    pallas_call x1, Pallas kernels, outputs(): pl.pallas_call(output_kernel, grid=(resp_count,), in_specs=[pl.BlockSpec(...  19.1 us
    pallas_call x1, Pallas kernels, attend(): pl.pallas_call(functools.partial(attend_kernel, head_width), grid_spec=gr...  16.5 us
    all_to_all x1, waiting for transfers between devices, on_device(): lax.all_to_all(pieces.reshape(groups * slab_count, -1, 128), ('resp', 'he...  12.6 us
    pallas_call x1, Pallas kernels, lift_tokens(): pl.pallas_call(up_kernel, grid=(heads // 2,), in_specs=[pl.BlockSpec((tok...  11.7 us
    all_to_all x1, starting transfers between devices, on_device(): lax.all_to_all(copies, ('resp', 'head'), split_axis=0, concat_axis=0, til...  11.5 us
    pallas_call x1, Pallas kernels, own_scores(): pl.pallas_call(functools.partial(own_kernel, head_width), grid=(resp_coun...  11.2 us
    all_to_all x1, waiting for transfers between devices, on_device(): lax.all_to_all(copies, ('resp', 'head'), split_axis=0, concat_axis=0, til...  7.44 us
    all_to_all x1, starting transfers between devices, on_device(): lax.all_to_all(pieces.reshape(groups * slab_count, -1, 128), ('resp', 'he...  5.03 us
  transfers between devices with their start and end apart: 2, of which 2 were waited for; matrix products, arithmetic and copies ran while one was open for 2% of the time, Pallas kernels for 41%

profile of v8, /device:TPU:1, one launch (start us, length us, event | category | flops | bytes accessed | tf_op | source)
XLA Modules:
  0.0 101.7 jit_solution(13270583459089707624)
XLA Ops:
  0.6 2.5 %pack.1 = bf16[8,16,72,128]{3,2,1,0:T(8,128)(2,1)} custom-call(s32[64]{0:T(128)} %prompt_any.1, bf16[2,16,576]{2,1,0:T(8,128)(2,1)} %latent_any.1), custom_call_target="tpu_custom_call" | custom-call | tf_op jit(solution)/shard_map/pack/pallas_call | solution.py:127
  3.1 0.0 copy-start
  3.2 11.5 %all-to-all-start = ((bf16[128,72,128]{2,1,0:T(8,128)(2,1)}), bf16[128,72,128]{2,1,0:T(8,128)(2,1)S(1)}, u32[]{:S(2)}, u32[]{:S(2)}) async-start(bf16[128,72,128]{2,1,0:T(8,128)(2,1)} %bitcast), calls=%async_computation | async-start | bytes 4718592 | tf_op jit(solution)/shard_map/all_to_all | solution.py:396
  14.7 0.0 copy-start.1
  14.7 0.0 copy-start.2
  14.7 0.0 copy-done
  14.7 1.5 %copy.22.own_ref = bf16[1024,576]{1,0:T(8,128)(2,1)} copy(bf16[1024,576]{0,1:T(8,128)(2,1)S(1)} %copy-done) | data formatting | bytes 2359296 | tf_op args[4]
  16.2 0.0 copy-done.1
  16.2 0.1 and_select_fusion.2
  16.3 0.0 copy-done.2
  16.3 0.2 select_reduce_fusion.3.len_ref
  16.4 11.7 %lift_tokens.1 = (bf16[8,576,1024]{2,1,0:T(8,128)(2,1)}, bf16[8,512,1024]{2,1,0:T(8,128)(2,1)}) custom-call(bf16[1024,1536]{1,0:T(8,128)(2,1)} %q_ref.1, bf16[8,128,512]{2,1,0:T(8,128)(2,1)} %uk_ref.1, bf16[1024,1024]{1,0:T(8,128)(2,1)} %go_ref.1, bf16[8,512,128]{2,1,0:T(8,128)(2,1)} %uv_ref.3), custom_call_target="tpu_custom_call" | custom-call | flops 2147483648 | bytes 31457280 | tf_op jit(solution)/shard_map/lift_tokens/pallas_call | solution.py:67
  28.2 11.2 %own_scores.1 = (bf16[8,128,1024]{2,1,0:T(8,128)(2,1)}, f32[8,8,1024]{2,1,0:T(8,128)}) custom-call(bf16[1024,576]{1,0:T(8,128)(2,1)} %copy.22.own_ref, bf16[8,576,1024]{2,1,0:T(8,128)(2,1)} %get-tuple-element.10.fq_ref, bf16[8,512,1024]{2,1,0:T(8,128)(2,1)} %get-tuple-element.11.gl_ref), custom_call_target="tpu_custom_call" | custom-call | flops 2281701376 | bytes 23068672 | tf_op jit(solution)/shard_map/own_scores/pallas_call | solution.py:170
  39.4 7.4 %all-to-all-done = bf16[128,72,128]{2,1,0:T(8,128)(2,1)S(1)} async-done(((bf16[128,72,128]{2,1,0:T(8,128)(2,1)}), bf16[128,72,128]{2,1,0:T(8,128)(2,1)S(1)}, u32[]{:S(2)}, u32[]{:S(2)}) %all-to-all-start) | async-done | bytes 2359328 | tf_op jit(solution)/shard_map/all_to_all | solution.py:396
  46.8 16.5 %attend.1 = (bf16[8,256,1024]{2,1,0:T(8,128)(2,1)}, f32[8,8,1024]{2,1,0:T(8,128)}, bf16[8,256,512]{2,1,0:T(8,128)(2,1)}, bf16[8,16,72,128]{3,2,1,0:T(8,128)(2,1)}) custom-call(s32[8]{0:T(128)S(1)} %get-tuple-element.22.slot_ref, s32[8]{0:T(128)S(1)} %select_reduce_fusion.3.len_ref, bf16[8,16,72,128]{3,2,1,0:T(8,128)(2,1)S(1)} %bitcast.19, ...), custom_call_target="tpu_custom_call" | custom-call | flops 9126805504 | bytes 31457280 | tf_op jit(solution)/shard_map/attend/pallas_call | solution.py:312
  63.3 5.0 %all-to-all-start.1 = ((bf16[128,72,128]{2,1,0:T(8,128)(2,1)}), bf16[128,72,128]{2,1,0:T(8,128)(2,1)S(1)}, u32[]{:S(2)}, u32[]{:S(2)}) async-start(bf16[128,72,128]{2,1,0:T(8,128)(2,1)} %bitcast.20), calls=%async_computation.1 | async-start | bytes 4718592 | tf_op jit(solution)/shard_map/all_to_all | solution.py:408
  68.3 0.1 broadcast_in_dim.54
  68.4 0.1 eq.54
  68.5 0.1 select_reduce_fusion.2
  68.6 0.2 compare_reduce_fusion.1
  68.8 19.1 %outputs.1 = bf16[1024,1024]{1,0:T(8,128)(2,1)} custom-call(bf16[8,256,512]{2,1,0:T(8,128)(2,1)} %get-tuple-element.13.latent_ref, bf16[1024,576]{1,0:T(8,128)(2,1)} %copy.22.own_ref, bf16[8,256,1024]{2,1,0:T(8,128)(2,1)} %get-tuple-element.14.aT_ref, bf16[8,128,1024]{2,1,0:T(8,128)(2,1)} %get-tuple-element.15.e_ref, ...), custom_call_target="tpu_custom_call" | custom-call | flops 4294967296 | bytes 16777216 | tf_op jit(solution)/shard_map/outputs/pallas_call | solution.py:354
  87.9 12.6 %all-to-all-done.1 = bf16[128,72,128]{2,1,0:T(8,128)(2,1)S(1)} async-done(((bf16[128,72,128]{2,1,0:T(8,128)(2,1)}), bf16[128,72,128]{2,1,0:T(8,128)(2,1)S(1)}, u32[]{:S(2)}, u32[]{:S(2)}) %all-to-all-start.1) | async-done | bytes 2359328 | tf_op jit(solution)/shard_map/all_to_all | solution.py:408
  100.4 0.3 convert_reduce_fusion
  100.8 0.1 select_reduce_fusion.1
  100.9 0.1 reshape.65
  101.0 0.6 pad_maximum_fusion
  (5 shorter events, 0.0 us)
Async XLA Ops:
  3.1 11.6 %copy-start = (bf16[1024,576]{0,1:T(8,128)(2,1)S(1)}, bf16[1024,576]{0,1:T(8,128)(2,1)}, u32[]{:S(2)}) copy-start(bf16[1024,576]{0,1:T(8,128)(2,1)} %param.12) | copy-start | bytes 3538948
  3.2 43.6 %all-to-all-start = ((bf16[128,72,128]{2,1,0:T(8,128)(2,1)}), bf16[128,72,128]{2,1,0:T(8,128)(2,1)S(1)}, u32[]{:S(2)}, u32[]{:S(2)}) async-start(bf16[128,72,128]{2,1,0:T(8,128)(2,1)} %bitcast), calls=%async_computation | async-start | bytes 4718592 | tf_op jit(solution)/shard_map/all_to_all | solution.py:396
  14.7 1.5 %copy-start.1 = (s32[64]{0:T(128)S(1)}, s32[64]{0:T(128)}, u32[]{:S(2)}) copy-start(s32[64]{0:T(128)} %prompt_any.1) | copy-start | bytes 772
  14.7 1.6 %copy-start.2 = (s32[16]{0:T(128)S(1)}, s32[16]{0:T(128)}, u32[]{:S(2)}) copy-start(s32[16]{0:T(128)} %param.15) | copy-start | bytes 196
  63.3 37.2 %all-to-all-start.1 = ((bf16[128,72,128]{2,1,0:T(8,128)(2,1)}), bf16[128,72,128]{2,1,0:T(8,128)(2,1)S(1)}, u32[]{:S(2)}, u32[]{:S(2)}) async-start(bf16[128,72,128]{2,1,0:T(8,128)(2,1)} %bitcast.20), calls=%async_computation.1 | async-start | bytes 4718592 | tf_op jit(solution)/shard_map/all_to_all | solution.py:408
